TPU v7x, 32 devices: a whole 2x2x4 slice. The times are simulated.
32 devices in a mesh: groups: 2 (over y), row: 4 (over z), sect: 2 (over x), batch: 2 (over core).
Axes of the slice: x: 2, y: 2, z: 4, core: 2. Of those that a mesh axis runs over, the one named last changes fastest.
Arguments:
- probe: float32 [2, 512, 512], P(None, 'row'), may hold values from -4.2 to 4.2
- object_delta: float32 [4, 2, 512, 2048], P(('groups', 'sect'), None, 'row'), parts along dimension 0, may hold values from -1.8 to 1.8
- measured: float32 [4, 2, 512, 512], P(('groups', 'batch'), None, 'row'), parts along dimension 0, may hold values from 0.05 to 4
- pos_y: int32 [4, 2], P(('groups', 'batch')), parts along dimension 0, may hold values from 0 to 127
- pos_x: int32 [4, 2], P(('groups', 'batch')), parts along dimension 0, may hold values from 0 to 1536
- prop_phase: float32 [512, 512], P('row'), may hold values from -3.140625 to 3.140625
Outputs:
- object_grad: float32 [4, 2, 512, 2048], P(('groups', 'sect'), None, 'row'), parts along dimension 0
There are 2 independent parts, one for each index of `groups`. A program takes and returns all parts, laid end to end along the dimension named above; an argument that names none is the same for every part. Nothing has to cross between parts.
All inputs are finite; a program needn't handle non-finite values.
Results may differ from a plain program's by a relative error of at most 0.00017.
Values sent between devices are 32-bit elements; how exact they have to be, the bound alone decides.
No kernel may reach another device: no remote copies, remote signals or barrier semaphores. Data moves between devices by JAX's collectives and lax.ppermute only.
A program may use at most 64 MiB of HBM per device.

v0:
```python
import math

import jax
import jax.numpy as jnp
from jax import lax
from jax.sharding import PartitionSpec as P

highest = lax.Precision.HIGHEST


def shifted(value, axis, steps):
    count = lax.axis_size(axis)
    initial, last = (max(0, -steps), min(count, count - steps))
    return lax.ppermute(value, axis, [(source, source + steps) for source in range(initial, last)])


def dft_tables(length):
    counter = jnp.arange(length, dtype=jnp.int32)
    phases = counter[:, None] * counter[None, :] % length
    angles = phases.astype(jnp.float32) * (2.0 * math.pi / length)
    weights = 1.0 / math.sqrt(length)
    return jnp.stack([jnp.cos(angles) * weights, jnp.sin(angles) * weights])


def along(complex_field, dft_table, pattern, orientation):
    products = jnp.einsum(
        pattern, complex_field, dft_table, precision=highest, preferred_element_type=jnp.float32
    )
    return jnp.stack(
        [
            products[0, 0] - orientation * products[1, 1],
            orientation * products[0, 1] + products[1, 0],
        ]
    )


def spectrum(complex_field, dft_table):
    partial_form = along(complex_field, dft_table, "cpyx,dkx->cdpky", -1.0)
    turned = lax.all_to_all(partial_form, "row", split_axis=2, concat_axis=3, tiled=True)
    return along(turned, dft_table, "cpky,dvy->cdpkv", -1.0)


def restore(complex_field, dft_table):
    partial_form = along(complex_field, dft_table, "cpkv,dvy->cdpky", 1.0)
    turned = lax.all_to_all(partial_form, "row", split_axis=3, concat_axis=2, tiled=True)
    return along(turned, dft_table, "cpky,dkx->cdpyx", 1.0)


def product(first_factor, second_factor):
    return jnp.stack(
        [
            first_factor[0] * second_factor[0] - first_factor[1] * second_factor[1],
            first_factor[0] * second_factor[1] + first_factor[1] * second_factor[0],
        ]
    )


def conj_product(first_factor, second_factor):
    return jnp.stack(
        [
            first_factor[0] * second_factor[0] + first_factor[1] * second_factor[1],
            first_factor[0] * second_factor[1] - first_factor[1] * second_factor[0],
        ]
    )


def cut_patches(window, offsets_y, offsets_x, height, breadth):

    def cut_single(start_y, start_x):
        return lax.dynamic_slice(window, (jnp.int32(0), start_y, start_x), (2, height, breadth))

    return jax.vmap(cut_single, out_axes=1)(offsets_y, offsets_x)


def deposit(buffer, contrib, offsets_y, offsets_x):

    def deposit_single(current, entry_now):
        piece_now, start_y, start_x = entry_now
        anchor = (jnp.int32(0), start_y, start_x)
        before = lax.dynamic_slice(current, anchor, piece_now.shape)
        return (lax.dynamic_update_slice(current, before + piece_now, anchor), None)

    updated, _ = lax.scan(
        deposit_single, buffer, (jnp.moveaxis(contrib, 1, 0), offsets_y, offsets_x)
    )
    return updated


def advance(entering, patch_block, dft_table, kernel):
    transmit = patch_block.at[0].add(1.0)
    far_field = spectrum(product(entering, transmit), dft_table)
    onward = restore(product(kernel, far_field), dft_table)
    return (far_field, onward)


def retreat(spectral, entering, patch_block, dft_table):
    inner = restore(spectral, dft_table)
    gradient = conj_product(entering, inner)
    transmit = patch_block.at[0].add(1.0)
    leaving = conj_product(transmit, inner)
    return (gradient, leaving)


def keep(store, update_value, slot_index, active):
    previous = lax.dynamic_slice_in_dim(store, slot_index, 1, axis=1)
    chosen = jnp.where(active, update_value, previous)
    return lax.dynamic_update_slice_in_dim(store, chosen, slot_index, axis=1)


def settle(buffer, height):
    own_rows = buffer[:, :, :height]
    spilled = buffer[:, :, height:]
    arrived = shifted(spilled, "row", 1)
    return lax.psum(own_rows + arrived, "batch")


def on_device(probe, object_delta, measured, pos_y, pos_x, prop_phase):
    sections = lax.axis_size("sect")
    section = lax.axis_index("sect")
    height = probe.shape[1]
    breadth = probe.shape[2]
    number = measured.shape[1]
    dft_table = dft_tables(breadth)
    kernel = jnp.stack([jnp.cos(prop_phase), jnp.sin(prop_phase)])[:, None]
    below_rows = shifted(object_delta, "row", -1)
    window = jnp.concatenate([object_delta, below_rows], axis=2)
    offsets_y = pos_y[0]
    offsets_x = pos_x[0]
    observed = measured[0]
    total_turns = sections + number - 1
    is_first = section == 0
    is_last = section == sections - 1
    zero_wave = jnp.zeros((2, 1, height, breadth), jnp.float32)
    empty_store = jnp.zeros((2, number, height, breadth), jnp.float32)

    def forward_turn(turn_index, state_now):
        arriving, entry_store, far_store = state_now
        block_index = turn_index - section
        active = (block_index >= 0) & (block_index < number)
        slot_index = jnp.clip(block_index, 0, number - 1)
        block_y = lax.dynamic_slice_in_dim(offsets_y, slot_index, 1)
        block_x = lax.dynamic_slice_in_dim(offsets_x, slot_index, 1)
        entering = jnp.where(is_first, probe[:, None], arriving)
        patch_block = cut_patches(window[0], block_y, block_x, height, breadth)
        far_field, onward = advance(entering, patch_block, dft_table, kernel)
        entry_store = keep(entry_store, entering, slot_index, active)
        far_store = keep(far_store, far_field, slot_index, active)
        arriving = shifted(onward, "sect", 1)
        return (arriving, entry_store, far_store)

    _, entry_store, far_store = lax.fori_loop(
        0, total_turns, forward_turn, (zero_wave, empty_store, empty_store)
    )

    def adjoint_turn(turn_index, state_now):
        arriving, buffer = state_now
        block_index = turn_index - (sections - 1 - section)
        active = (block_index >= 0) & (block_index < number)
        slot_index = jnp.clip(block_index, 0, number - 1)
        block_y = lax.dynamic_slice_in_dim(offsets_y, slot_index, 1)
        block_x = lax.dynamic_slice_in_dim(offsets_x, slot_index, 1)
        far_field = lax.dynamic_slice_in_dim(far_store, slot_index, 1, axis=1)
        target = lax.dynamic_slice_in_dim(observed, slot_index, 1, axis=0)
        residual = far_field[0] * far_field[0] + far_field[1] * far_field[1] - target
        seeded = residual[None] * far_field
        looked = conj_product(kernel, spectrum(arriving, dft_table))
        spectral = jnp.where(is_last, seeded, looked)
        entering = lax.dynamic_slice_in_dim(entry_store, slot_index, 1, axis=1)
        patch_block = cut_patches(window[0], block_y, block_x, height, breadth)
        gradient, leaving = retreat(spectral, entering, patch_block, dft_table)
        gradient = jnp.where(active, gradient, 0.0)
        buffer = deposit(buffer, gradient, block_y, block_x)
        arriving = shifted(leaving, "sect", -1)
        return (arriving, buffer)

    empty_buffer = jnp.zeros(window.shape[1:], jnp.float32)
    _, buffer = lax.fori_loop(0, total_turns, adjoint_turn, (zero_wave, empty_buffer))
    settled = settle(buffer[None], height)
    return settled


def solution(mesh):
    in_specs = (
        P(None, "row", None),
        P(("groups", "sect"), None, "row", None),
        P(("groups", "batch"), None, "row", None),
        P(("groups", "batch"), None),
        P(("groups", "batch"), None),
        P("row", None),
    )
    out_specs = P(("groups", "sect"), None, "row", None)
    return jax.shard_map(
        on_device, mesh=mesh, in_specs=in_specs, out_specs=out_specs, check_vma=False
    )
```

profile of v0, /device:TPU:0, one launch (start us, length us, event | category | flops | bytes accessed | tf_op | source)
XLA Modules:
  0.0 577.1 jit_solution(2235874818257598021)
XLA Ops:
  10.6 4.2 sine_multiply_fusion
  16.6 40.8 %collective-permute-done.2 = f32[1,2,128,2048]{3,2,1,0:T(8,128)} collective-permute-done((f32[1,2,128,2048]{3,2,1,0:T(8,128)}, f32[1,2,128,2048]{3,2,1,0:T(8,128)}, u32[]{:S(2)}, u32[]{:S(2)}) %collective-permute-start.2) | collective-permute-done | bytes 2097184 | tf_op jit(solution)/shard_map/ppermute | solution.py:14
  62.9 228.0 %while.48 = (s32[]{:T(128)}, f32[2,1,128,512]{3,2,1,0:T(8,128)}, f32[2,2,128,512]{3,2,0,1:T(8,128)}, f32[2,2,128,512]{3,2,0,1:T(8,128)}, f32[2,1,128,512]{3,2,0,...) while((s32[]{:T(128)}, f32[2,1,128,512]{3,2,1,0:T(8,128)}, ...), condition=%wide.region_1.2_spmd, body=%wide.region_0.1_spmd.sunk | while | flops 6445268992 | bytes 42468236 | solution.py:151
  74.9 17.7 %all_to_all.148 = f32[2,1,512,128]{3,1,0,2:T(1,128)S(1)} all-to-all(f32[2,1,512,128]{3,1,0,2:T(1,128)} %copy.98), channel_id=1, replica_groups=mesh['groups'=2,'row'=4,'sect'=2,'batch'=2] {'row'}, dimensions={2} | all-to-all | bytes 1048576 | tf_op jit(solution)/shard_map/while/body/eval_jaxpr/all_to_all | solution.py:39
  101.9 17.0 %all_to_all.149 = f32[2,1,128,512]{2,1,0,3:T(1,128)S(1)} all-to-all(f32[2,1,128,512]{2,1,0,3:T(1,128)} %copy.100), channel_id=1, replica_groups=mesh['groups'=2,'row'=4,'sect'=2,'batch'=2] {'row'}, dimensions={3} | all-to-all | bytes 1048576 | tf_op jit(solution)/shard_map/while/body/eval_jaxpr/all_to_all | solution.py:45
  126.0 4.2 collective-permute-start
  132.1 7.5 %collective-permute-done = f32[2,1,128,512]{3,2,1,0:T(8,128)} collective-permute-done((f32[2,1,128,512]{3,2,1,0:T(8,128)}, f32[2,1,128,512]{3,2,1,0:T(8,128)}, u32[]{:S(2)}, u32[]{:S(2)}) %collective-permute-start) | collective-permute-done | bytes 524320 | tf_op jit(solution)/shard_map/while/body/eval_jaxpr/ppermute | solution.py:14
  151.4 16.2 %all_to_all.148 = f32[2,1,512,128]{3,1,0,2:T(1,128)S(1)} all-to-all(f32[2,1,512,128]{3,1,0,2:T(1,128)} %copy.98), channel_id=1, replica_groups=mesh['groups'=2,'row'=4,'sect'=2,'batch'=2] {'row'}, dimensions={2} | all-to-all | bytes 1048576 | tf_op jit(solution)/shard_map/while/body/eval_jaxpr/all_to_all | solution.py:39
  177.0 16.8 %all_to_all.149 = f32[2,1,128,512]{2,1,0,3:T(1,128)S(1)} all-to-all(f32[2,1,128,512]{2,1,0,3:T(1,128)} %copy.100), channel_id=1, replica_groups=mesh['groups'=2,'row'=4,'sect'=2,'batch'=2] {'row'}, dimensions={3} | all-to-all | bytes 1048576 | tf_op jit(solution)/shard_map/while/body/eval_jaxpr/all_to_all | solution.py:45
  200.8 5.2 collective-permute-start
  207.9 7.4 %collective-permute-done = f32[2,1,128,512]{3,2,1,0:T(8,128)} collective-permute-done((f32[2,1,128,512]{3,2,1,0:T(8,128)}, f32[2,1,128,512]{3,2,1,0:T(8,128)}, u32[]{:S(2)}, u32[]{:S(2)}) %collective-permute-start) | collective-permute-done | bytes 524320 | tf_op jit(solution)/shard_map/while/body/eval_jaxpr/ppermute | solution.py:14
  227.1 16.0 %all_to_all.148 = f32[2,1,512,128]{3,1,0,2:T(1,128)S(1)} all-to-all(f32[2,1,512,128]{3,1,0,2:T(1,128)} %copy.98), channel_id=1, replica_groups=mesh['groups'=2,'row'=4,'sect'=2,'batch'=2] {'row'}, dimensions={2} | all-to-all | bytes 1048576 | tf_op jit(solution)/shard_map/while/body/eval_jaxpr/all_to_all | solution.py:39
  252.5 16.8 %all_to_all.149 = f32[2,1,128,512]{2,1,0,3:T(1,128)S(1)} all-to-all(f32[2,1,128,512]{2,1,0,3:T(1,128)} %copy.100), channel_id=1, replica_groups=mesh['groups'=2,'row'=4,'sect'=2,'batch'=2] {'row'}, dimensions={3} | all-to-all | bytes 1048576 | tf_op jit(solution)/shard_map/while/body/eval_jaxpr/all_to_all | solution.py:45
  276.3 5.2 collective-permute-start
  283.4 7.4 %collective-permute-done = f32[2,1,128,512]{3,2,1,0:T(8,128)} collective-permute-done((f32[2,1,128,512]{3,2,1,0:T(8,128)}, f32[2,1,128,512]{3,2,1,0:T(8,128)}, u32[]{:S(2)}, u32[]{:S(2)}) %collective-permute-start) | collective-permute-done | bytes 524320 | tf_op jit(solution)/shard_map/while/body/eval_jaxpr/ppermute | solution.py:14
  294.3 202.5 %while.49 = (s32[]{:T(128)}, f32[2,1,128,512]{3,2,1,0:T(8,128)}, f32[2,256,2048]{2,1,0:T(8,128)}, f32[1,2,256,2048]{3,2,1,0:T(8,128)}, s32[]{:T(128)}, /*index=5...) while((s32[]{:T(128)}, f32[2,1,128,512]{3,2,1,0:T(8,128)}, ...), condition=%wide.region_3.4_spmd, body=%wide.region_2.3_spmd.sunk | while | flops 6445924352 | bytes 47972932 | solution.py:177
  298.7 4.1 all-to-all-start.2
  305.1 10.3 %all-to-all-done.2 = f32[2,1,512,128]{3,1,0,2:T(1,128)} async-done(((f32[2,1,512,128]{3,1,0,2:T(1,128)}), f32[2,1,512,128]{3,1,0,2:T(1,128)}, u32[]{:S(2)}, u32[]{:S(2)}) %all-to-all-start.2) | async-done | bytes 524320 | tf_op jit(solution)/shard_map/while/body/eval_jaxpr/all_to_all | solution.py:39
  326.0 3.5 all-to-all-start.3
  334.3 7.5 %all-to-all-done.3 = f32[2,1,128,512]{2,1,0,3:T(1,128)S(1)} async-done(((f32[2,1,128,512]{2,1,0,3:T(1,128)}), f32[2,1,128,512]{2,1,0,3:T(1,128)S(1)}, u32[]{:S(2)}, u32[]{:S(2)}) %all-to-all-start.3) | async-done | bytes 524320 | tf_op jit(solution)/shard_map/while/body/eval_jaxpr/all_to_all | solution.py:45
  354.6 6.3 %dynamic_update_slice.38 = f32[2,256,2048]{2,1,0:T(8,128)} dynamic-update-slice(f32[2,256,2048]{2,1,0:T(8,128)} %get-tuple-element.1086, f32[2,128,512]{2,1,0:T(8,128)S(1)} %fusion.153, s32[]{:T(128)} %constant.349.clone.1..sunk.1, s32[]{:T(128)S(6)} %select_n.250, s32[]{:T(128)S(6)} %select_n.251) | dynamic-update-slice | bytes 1048580 | tf_op jit(solution)/shard_map/while/body/eval_jaxpr/while/body/eval_jaxpr/dynamic_update_slice | solution.py:81
  365.3 4.8 all-to-all-start.2
  372.3 10.0 %all-to-all-done.2 = f32[2,1,512,128]{3,1,0,2:T(1,128)} async-done(((f32[2,1,512,128]{3,1,0,2:T(1,128)}), f32[2,1,512,128]{3,1,0,2:T(1,128)}, u32[]{:S(2)}, u32[]{:S(2)}) %all-to-all-start.2) | async-done | bytes 524320 | tf_op jit(solution)/shard_map/while/body/eval_jaxpr/all_to_all | solution.py:39
  401.2 7.5 %all-to-all-done.3 = f32[2,1,128,512]{2,1,0,3:T(1,128)S(1)} async-done(((f32[2,1,128,512]{2,1,0,3:T(1,128)}), f32[2,1,128,512]{2,1,0,3:T(1,128)S(1)}, u32[]{:S(2)}, u32[]{:S(2)}) %all-to-all-start.3) | async-done | bytes 524320 | tf_op jit(solution)/shard_map/while/body/eval_jaxpr/all_to_all | solution.py:45
  421.6 6.3 %dynamic_update_slice.38 = f32[2,256,2048]{2,1,0:T(8,128)} dynamic-update-slice(f32[2,256,2048]{2,1,0:T(8,128)} %get-tuple-element.1086, f32[2,128,512]{2,1,0:T(8,128)S(1)} %fusion.153, s32[]{:T(128)} %constant.349.clone.1..sunk.1, s32[]{:T(128)S(6)} %select_n.250, s32[]{:T(128)S(6)} %select_n.251) | dynamic-update-slice | bytes 1048580 | tf_op jit(solution)/shard_map/while/body/eval_jaxpr/while/body/eval_jaxpr/dynamic_update_slice | solution.py:81
  432.2 4.6 all-to-all-start.2
  439.2 9.9 %all-to-all-done.2 = f32[2,1,512,128]{3,1,0,2:T(1,128)} async-done(((f32[2,1,512,128]{3,1,0,2:T(1,128)}), f32[2,1,512,128]{3,1,0,2:T(1,128)}, u32[]{:S(2)}, u32[]{:S(2)}) %all-to-all-start.2) | async-done | bytes 524320 | tf_op jit(solution)/shard_map/while/body/eval_jaxpr/all_to_all | solution.py:39
  467.9 7.5 %all-to-all-done.3 = f32[2,1,128,512]{2,1,0,3:T(1,128)S(1)} async-done(((f32[2,1,128,512]{2,1,0,3:T(1,128)}), f32[2,1,128,512]{2,1,0,3:T(1,128)S(1)}, u32[]{:S(2)}, u32[]{:S(2)}) %all-to-all-start.3) | async-done | bytes 524320 | tf_op jit(solution)/shard_map/while/body/eval_jaxpr/all_to_all | solution.py:45
  488.2 4.4 dynamic_update_slice.38
  492.7 4.2 collective-permute-done.1
  500.2 42.9 %collective-permute-done.3 = f32[1,2,128,2048]{3,2,1,0:T(8,128)S(1)} collective-permute-done((f32[1,2,128,2048]{3,2,1,0:T(8,128)S(1)}, f32[1,2,128,2048]{3,2,1,0:T(8,128)S(1)}, u32[]{:S(2)}, u32[]{:S(2)}) %collective-permute-start.3) | collective-permute-done | bytes 2097184 | tf_op jit(solution)/shard_map/ppermute | solution.py:14
  544.7 22.4 %all-reduce.2.cloned.1.call-done = f32[1,2,128,2048]{3,2,1,0:T(8,128)} async-done(((f32[1,2,128,2048]{3,2,1,0:T(8,128)}), f32[1,2,128,2048]{3,2,1,0:T(8,128)}) %all-reduce.2.cloned.1.call-update) | async-done | bytes 2097168 | tf_op jit(solution)/shard_map/psum | solution.py:114
  (193 shorter events, 191.4 us)
Async XLA Ops:
  6.5 560.6 %all-reduce.2.cloned.1.call-start = ((), (), s32[]{:S(2)}) async-start(), calls=%async_computation.4 | async-start | bytes 4194304 | tf_op jit(solution)/shard_map/psum | solution.py:114
  6.5 50.9 %collective-permute-start.2 = (f32[1,2,128,2048]{3,2,1,0:T(8,128)}, f32[1,2,128,2048]{3,2,1,0:T(8,128)}, u32[]{:S(2)}, u32[]{:S(2)}) collective-permute-start(f32[1,2,128,2048]{3,2,1,0:T(8,128)} %param.15), channel_id=1, source_target_pairs={{4,0},{8,4},{12,8},{5,1},{9,5},{13,9},{6,2},{10,6},{14,10},{7,3},{... | collective-permute-start | bytes 6291464 | tf_op jit(solution)/shard_map/ppermute | solution.py:14
  14.8 1.6 copy-start.3
  59.1 3.7 copy-start.2
  59.1 3.7 copy-start.4
  59.2 3.7 copy-start.5
  126.0 13.7 %collective-permute-start = (f32[2,1,128,512]{3,2,1,0:T(8,128)}, f32[2,1,128,512]{3,2,1,0:T(8,128)}, u32[]{:S(2)}, u32[]{:S(2)}) collective-permute-start(f32[2,1,128,512]{3,2,1,0:T(8,128)} %pad_maximum_fusion.16), channel_id=1, source_target_pairs={{0,2},{1,3},{4,6},{5,7},{8,10},{9,11},{12,14},{13,15},{16,18},{17,... | collective-permute-start | bytes 1572872 | tf_op jit(solution)/shard_map/while/body/eval_jaxpr/ppermute | solution.py:14
  200.8 14.6 %collective-permute-start = (f32[2,1,128,512]{3,2,1,0:T(8,128)}, f32[2,1,128,512]{3,2,1,0:T(8,128)}, u32[]{:S(2)}, u32[]{:S(2)}) collective-permute-start(f32[2,1,128,512]{3,2,1,0:T(8,128)} %pad_maximum_fusion.16), channel_id=1, source_target_pairs={{0,2},{1,3},{4,6},{5,7},{8,10},{9,11},{12,14},{13,15},{16,18},{17,... | collective-permute-start | bytes 1572872 | tf_op jit(solution)/shard_map/while/body/eval_jaxpr/ppermute | solution.py:14
  276.3 14.5 %collective-permute-start = (f32[2,1,128,512]{3,2,1,0:T(8,128)}, f32[2,1,128,512]{3,2,1,0:T(8,128)}, u32[]{:S(2)}, u32[]{:S(2)}) collective-permute-start(f32[2,1,128,512]{3,2,1,0:T(8,128)} %pad_maximum_fusion.16), channel_id=1, source_target_pairs={{0,2},{1,3},{4,6},{5,7},{8,10},{9,11},{12,14},{13,15},{16,18},{17,... | collective-permute-start | bytes 1572872 | tf_op jit(solution)/shard_map/while/body/eval_jaxpr/ppermute | solution.py:14
  298.7 16.7 %all-to-all-start.2 = ((f32[2,1,512,128]{3,1,0,2:T(1,128)}), f32[2,1,512,128]{3,1,0,2:T(1,128)}, u32[]{:S(2)}, u32[]{:S(2)}) async-start(f32[2,1,512,128]{3,1,0,2:T(1,128)} %copy.102), calls=%async_computation.2 | async-start | bytes 1048576 | tf_op jit(solution)/shard_map/while/body/eval_jaxpr/all_to_all | solution.py:39
  319.7 3.0 copy-start.1
  326.0 15.7 %all-to-all-start.3 = ((f32[2,1,128,512]{2,1,0,3:T(1,128)}), f32[2,1,128,512]{2,1,0,3:T(1,128)S(1)}, u32[]{:S(2)}, u32[]{:S(2)}) async-start(f32[2,1,128,512]{2,1,0,3:T(1,128)} %copy.104), calls=%async_computation.3 | async-start | bytes 1048576 | tf_op jit(solution)/shard_map/while/body/eval_jaxpr/all_to_all | solution.py:45
  348.4 12.5 %collective-permute-start.1 = (f32[2,1,128,512]{3,2,1,0:T(8,128)}, f32[2,1,128,512]{3,2,1,0:T(8,128)}, u32[]{:S(2)}, u32[]{:S(2)}) collective-permute-start(f32[2,1,128,512]{3,2,1,0:T(8,128)} %pad_maximum_fusion.19), channel_id=1, source_target_pairs={{2,0},{3,1},{6,4},{7,5},{10,8},{11,9},{14,12},{15,13},{18,16},{19,... | collective-permute-start | bytes 1572872 | tf_op jit(solution)/shard_map/while/body/eval_jaxpr/ppermute | solution.py:14
  365.3 17.1 %all-to-all-start.2 = ((f32[2,1,512,128]{3,1,0,2:T(1,128)}), f32[2,1,512,128]{3,1,0,2:T(1,128)}, u32[]{:S(2)}, u32[]{:S(2)}) async-start(f32[2,1,512,128]{3,1,0,2:T(1,128)} %copy.102), calls=%async_computation.2 | async-start | bytes 1048576 | tf_op jit(solution)/shard_map/while/body/eval_jaxpr/all_to_all | solution.py:39
  386.6 3.0 copy-start.1
  393.0 15.7 %all-to-all-start.3 = ((f32[2,1,128,512]{2,1,0,3:T(1,128)}), f32[2,1,128,512]{2,1,0,3:T(1,128)S(1)}, u32[]{:S(2)}, u32[]{:S(2)}) async-start(f32[2,1,128,512]{2,1,0,3:T(1,128)} %copy.104), calls=%async_computation.3 | async-start | bytes 1048576 | tf_op jit(solution)/shard_map/while/body/eval_jaxpr/all_to_all | solution.py:45
  415.4 12.5 %collective-permute-start.1 = (f32[2,1,128,512]{3,2,1,0:T(8,128)}, f32[2,1,128,512]{3,2,1,0:T(8,128)}, u32[]{:S(2)}, u32[]{:S(2)}) collective-permute-start(f32[2,1,128,512]{3,2,1,0:T(8,128)} %pad_maximum_fusion.19), channel_id=1, source_target_pairs={{2,0},{3,1},{6,4},{7,5},{10,8},{11,9},{14,12},{15,13},{18,16},{19,... | collective-permute-start | bytes 1572872 | tf_op jit(solution)/shard_map/while/body/eval_jaxpr/ppermute | solution.py:14
  432.2 16.8 %all-to-all-start.2 = ((f32[2,1,512,128]{3,1,0,2:T(1,128)}), f32[2,1,512,128]{3,1,0,2:T(1,128)}, u32[]{:S(2)}, u32[]{:S(2)}) async-start(f32[2,1,512,128]{3,1,0,2:T(1,128)} %copy.102), calls=%async_computation.2 | async-start | bytes 1048576 | tf_op jit(solution)/shard_map/while/body/eval_jaxpr/all_to_all | solution.py:39
  453.4 3.0 copy-start.1
  459.7 15.7 %all-to-all-start.3 = ((f32[2,1,128,512]{2,1,0,3:T(1,128)}), f32[2,1,128,512]{2,1,0,3:T(1,128)S(1)}, u32[]{:S(2)}, u32[]{:S(2)}) async-start(f32[2,1,128,512]{2,1,0,3:T(1,128)} %copy.104), calls=%async_computation.3 | async-start | bytes 1048576 | tf_op jit(solution)/shard_map/while/body/eval_jaxpr/all_to_all | solution.py:45
  482.1 14.7 %collective-permute-start.1 = (f32[2,1,128,512]{3,2,1,0:T(8,128)}, f32[2,1,128,512]{3,2,1,0:T(8,128)}, u32[]{:S(2)}, u32[]{:S(2)}) collective-permute-start(f32[2,1,128,512]{3,2,1,0:T(8,128)} %pad_maximum_fusion.19), channel_id=1, source_target_pairs={{2,0},{3,1},{6,4},{7,5},{10,8},{11,9},{14,12},{15,13},{18,16},{19,... | collective-permute-start | bytes 1572872 | tf_op jit(solution)/shard_map/while/body/eval_jaxpr/ppermute | solution.py:14
  496.8 46.3 %copy-start = (f32[2,256,2048]{2,1,0:T(8,128)S(1)}, f32[2,256,2048]{2,1,0:T(8,128)}, u32[]{:S(2)}) copy-start(f32[2,256,2048]{2,1,0:T(8,128)} %get-tuple-element.673) | copy-start | bytes 12582916
  498.7 44.4 %collective-permute-start.3 = (f32[1,2,128,2048]{3,2,1,0:T(8,128)S(1)}, f32[1,2,128,2048]{3,2,1,0:T(8,128)S(1)}, u32[]{:S(2)}, u32[]{:S(2)}) collective-permute-start(f32[1,2,128,2048]{3,2,1,0:T(8,128)S(1)} %slice.647), channel_id=1, source_target_pairs={{0,4},{4,8},{8,12},{1,5},{5,9},{9,13},{2,6},{6,10},{10,14},{3,7},{... | collective-permute-start | bytes 6291464 | tf_op jit(solution)/shard_map/ppermute | solution.py:14
Sparse Core Ops, SparseCore 0:
  544.8 22.1 all-reduce.1
where the time goes:
time: 581 us; the launch traced here: 577 us
  waiting for transfers between devices  185 us (32%)
  blocking collectives  100 us (17%)
  local copies, waits for them, and re-layouts  98.7 us (17%)
  matrix products  55.2 us (10%)
  other arithmetic  45.2 us (8%)
  starting transfers between devices  45 us (8%)
  loops' own time  33.8 us (6%)
  between operations  13.5 us (2%)
    ppermute x8, waiting for transfers between devices, shifted(): lax.ppermute(value, axis, [(source, source + steps) for source in range(i...  110 us
    dot_general x24, matrix products, along(): jnp.einsum(pattern, complex_field, dft_table, precision=highest, preferre...  55.2 us
    all_to_all x3, blocking collectives, restore(): lax.all_to_all(partial_form, 'row', split_axis=3, concat_axis=2, tiled=True)  50.5 us
    all_to_all x3, blocking collectives, spectrum(): lax.all_to_all(partial_form, 'row', split_axis=2, concat_axis=3, tiled=True)  49.8 us
    all_to_all x3, waiting for transfers between devices, spectrum(): lax.all_to_all(partial_form, 'row', split_axis=2, concat_axis=3, tiled=True)  30.2 us
    all_to_all x3, waiting for transfers between devices, restore(): lax.all_to_all(partial_form, 'row', split_axis=3, concat_axis=2, tiled=True)  22.5 us
    psum x1, waiting for transfers between devices, settle(): return lax.psum(own_rows + arrived, 'batch')  22.4 us
    another operation x1, loops' own time, on_device(): lax.fori_loop(0, total_turns, adjoint_turn, (zero_wave, empty_buffer))  21.8 us
  transfers between devices with their start and end apart: 15, of which 13 were waited for; matrix products, arithmetic and copies ran while one was open for 8% of the time, Pallas kernels for 0%

commit v1 on v0

v1 whole, which is shorter than its diff:
```python
import functools
import math

import jax
import jax.numpy as jnp
import ml_dtypes
import numpy as np
from jax import lax
from jax.experimental import pallas as pl
from jax.experimental.pallas import tpu as pltpu
from jax.sharding import PartitionSpec as P

highest = lax.Precision.HIGHEST
line_axes = ("row", "sect", "batch")
vmem_bytes = 40 * 1024 * 1024
smem = pltpu.MemorySpace.SMEM


def halves(table):
    table = table.astype(np.float64)
    upper = table.astype(ml_dtypes.bfloat16)
    lower = (table - upper.astype(np.float64)).astype(ml_dtypes.bfloat16)
    return np.stack([upper, lower])


def circle(length):
    quarter = length // 4
    index = np.arange(quarter)
    angles = (index[:, None] * index[None, :] % quarter) * (2.0 * math.pi / quarter)
    scale = 1.0 / math.sqrt(length)
    return np.cos(angles) * scale, np.sin(angles) * scale


def column_tables(length):
    cosine, sine = circle(length)
    forward = np.block([[cosine, sine], [-sine, cosine]])
    inverse = np.block([[cosine, -sine], [sine, cosine]])
    return halves(forward), halves(inverse)


def row_tables(length, shift):
    cosine, sine = circle(length)
    order = (np.arange(length // 4) + shift) % (length // 4)
    cosine, sine = cosine[:, order], sine[:, order]
    forward = np.block([[cosine, -sine], [sine, cosine]])
    inverse = np.block([[cosine.T, sine.T], [-sine.T, cosine.T]])
    return halves(forward), halves(inverse)


def twiddles(length):
    quarter = length // 4
    angles = np.arange(4)[:, None] * np.arange(quarter)[None, :] * (2.0 * math.pi / length)
    pairs = np.stack([np.cos(angles), np.sin(angles)], axis=1).astype(np.float32)
    along_lanes = pairs.reshape(8, quarter)
    along_rows = np.broadcast_to(pairs[..., None], (4, 2, quarter, 128)).copy()
    return along_lanes, along_rows


def split(value):
    upper = value.astype(jnp.bfloat16)
    lower = (value - upper.astype(jnp.float32)).astype(jnp.bfloat16)
    return upper, lower


def dot(first, second):
    return jnp.dot(first, second, preferred_element_type=jnp.float32)


def right_dot(value, table):
    upper, lower = split(value)
    return dot(upper, table[0]) + dot(lower, table[0]) + dot(upper, table[1])


def left_dot(table, value):
    upper, lower = split(value)
    return dot(table[0], upper) + dot(table[0], lower) + dot(table[1], upper)


def times(first, second):
    return (
        first[0] * second[0] - first[1] * second[1],
        first[0] * second[1] + first[1] * second[0],
    )


def conj_times(first, second):
    return (
        first[0] * second[0] + first[1] * second[1],
        first[0] * second[1] - first[1] * second[0],
    )


def plus(first, second):
    return (first[0] + second[0], first[1] + second[1])


def minus(first, second):
    return (first[0] - second[0], first[1] - second[1])


def turned(value):
    return (-value[1], value[0])


def scatter4(parts):
    sum02, dif02 = plus(parts[0], parts[2]), minus(parts[0], parts[2])
    sum13, dif13 = plus(parts[1], parts[3]), turned(minus(parts[1], parts[3]))
    return [plus(sum02, sum13), minus(dif02, dif13), minus(sum02, sum13), plus(dif02, dif13)]


def gather4(parts):
    sum02, dif02 = plus(parts[0], parts[2]), minus(parts[0], parts[2])
    sum13, dif13 = plus(parts[1], parts[3]), turned(minus(parts[1], parts[3]))
    return [plus(sum02, sum13), plus(dif02, dif13), minus(sum02, sum13), minus(dif02, dif13)]


def lane_twiddle(reference, index):
    return (reference[2 * index : 2 * index + 1, :], reference[2 * index + 1 : 2 * index + 2, :])


def forward_lanes(quarters, table, twiddle):
    rows = quarters[0][0].shape[0]
    classes = scatter4(quarters)
    packed = []
    for index, value in enumerate(classes):
        if index > 0:
            value = conj_times(lane_twiddle(twiddle, index), value)
        packed.append(jnp.concatenate(value, axis=1))
    result = right_dot(jnp.concatenate(packed, axis=0), table)
    half = result.shape[1] // 2
    return [
        (result[rows * index : rows * (index + 1), :half], result[rows * index : rows * (index + 1), half:])
        for index in range(4)
    ]


def inverse_lanes(classes, table, twiddle):
    rows = classes[0][0].shape[0]
    packed = jnp.concatenate([jnp.concatenate(value, axis=1) for value in classes], axis=0)
    result = right_dot(packed, table)
    half = result.shape[1] // 2
    parts = []
    for index in range(4):
        value = (result[rows * index : rows * (index + 1), :half], result[rows * index : rows * (index + 1), half:])
        if index > 0:
            value = times(lane_twiddle(twiddle, index), value)
        parts.append(value)
    return gather4(parts)


def forward_rows(quarters, table, twiddle):
    lanes = quarters[0][0].shape[1]
    packed = []
    for index, value in enumerate(scatter4(quarters)):
        if index > 0:
            value = conj_times((twiddle[index, 0], twiddle[index, 1]), value)
        packed.append(jnp.concatenate(value, axis=0))
    result = left_dot(table, jnp.concatenate(packed, axis=1))
    half = result.shape[0] // 2
    return [
        (result[:half, lanes * index : lanes * (index + 1)], result[half:, lanes * index : lanes * (index + 1)])
        for index in range(4)
    ]


def inverse_rows(classes, table, twiddle):
    lanes = classes[0][0].shape[1]
    packed = jnp.concatenate([jnp.concatenate(value, axis=0) for value in classes], axis=1)
    result = left_dot(table, packed)
    half = result.shape[0] // 2
    parts = []
    for index in range(4):
        value = (result[:half, lanes * index : lanes * (index + 1)], result[half:, lanes * index : lanes * (index + 1)])
        if index > 0:
            value = times((twiddle[index, 0], twiddle[index, 1]), value)
        parts.append(value)
    return gather4(parts)


def joined(parts, axis):
    return parts[0] if len(parts) == 1 else jnp.concatenate(parts, axis=axis)


def window_delta(info, near, far, height, breadth):
    lane = lax.broadcasted_iota(jnp.int32, (height, breadth), 1)
    line = lax.broadcasted_iota(jnp.int32, (height, breadth), 0)
    vacuum = (line < info[5]) & (info[1] == 1)
    use_near = lane >= info[4]
    return [
        jnp.where(vacuum, 0.0, jnp.where(use_near, near[0, part], far[0, part])) for part in range(2)
    ]


def patch_kernel(info, near, far, patch, scratch):
    height, breadth = near.shape[2], near.shape[3]
    real, imag = window_delta(info, near, far, height, breadth)
    scratch[0] = real + 1.0
    scratch[1] = imag
    first = pl.multiple_of(info[0] * (height // 2), height // 2)
    patch[...] = scratch[:, pl.ds(first, height // 2), :]


def launch_kernel(info, near, far, window, table, twiddle, message, rolled):
    height, breadth = near.shape[2], near.shape[3]
    quarter = breadth // 4
    real, imag = window_delta(info, near, far, height, breadth)
    transmit = (real + 1.0, imag)
    entering = []
    for part in range(2):
        lines = pltpu.roll(window[part], info[5], 0)[height:]
        entering.append(pltpu.roll(lines, info[4], 1))
        rolled[part] = entering[part]
    value = times(entering, transmit)
    quarters = [tuple(item[:, quarter * m : quarter * (m + 1)] for item in value) for m in range(4)]
    lower = info[0] == 0
    classes = scatter4(quarters)
    packed = []
    for index in range(2):
        chosen = tuple(jnp.where(lower, classes[index][i], classes[index + 2][i]) for i in range(2))
        low, high = lane_twiddle(twiddle, index), lane_twiddle(twiddle, index + 2)
        factor = tuple(jnp.where(lower, low[i], high[i]) for i in range(2))
        packed.append(jnp.concatenate(conj_times(factor, chosen), axis=1))
    result = right_dot(jnp.concatenate(packed, axis=0), table[0])
    for index in range(2):
        block = result[height * index : height * (index + 1)]
        message[0, :, quarter * index : quarter * (index + 1)] = block[:, :quarter]
        message[1, :, quarter * index : quarter * (index + 1)] = block[:, quarter:]


def settle_kernel(number, info, tables, twiddle, *refs):
    own_spectra, other_spectra = refs[:number], refs[number : 2 * number]
    own_terms, other_terms = refs[2 * number : 3 * number], refs[3 * number : 4 * number]
    rolled = refs[4 * number : 5 * number]
    out, scratch = refs[5 * number :]
    height, breadth = scratch.shape[1], scratch.shape[2]
    quarter = breadth // 4
    lower = info[0, 0] == 0
    lane = lax.broadcasted_iota(jnp.int32, (height, breadth), 1)
    line = lax.broadcasted_iota(jnp.int32, (height, breadth), 0)
    out[...] = jnp.zeros_like(out)
    for j in range(number):

        @pl.when(info[j, 7] == 0)
        def _():
            classes = []
            for index in range(4):
                first = quarter * (index % 2)
                pair = []
                for part in range(2):
                    own = own_spectra[j][part, :, first : first + quarter]
                    other = other_spectra[j][part, :, first : first + quarter]
                    pair.append(jnp.where(lower, own, other) if index < 2 else jnp.where(lower, other, own))
                classes.append(tuple(pair))
            table = tables[info[j, 6]]
            inner = inverse_lanes(classes, table, twiddle)
            for m in range(4):
                columns = slice(quarter * m, quarter * (m + 1))
                entering = (rolled[j][0, :, columns], rolled[j][1, :, columns])
                term = conj_times(entering, inner[m])
                scratch[0, :, columns] = term[0]
                scratch[1, :, columns] = term[1]

        @pl.when(info[j, 7] != 0)
        def _():
            own, other = own_terms[j][...], other_terms[j][...]
            scratch[:, : height // 2, :] = jnp.where(lower, own, other)
            scratch[:, height // 2 :, :] = jnp.where(lower, other, own)

        present = (line >= info[j, 5]) | (info[j, 1] != 1)
        near = pl.ds(pl.multiple_of(info[j, 2] * breadth, breadth), breadth)
        far = pl.ds(pl.multiple_of(info[j, 3] * breadth, breadth), breadth)
        use_near = lane >= info[j, 4]
        for part in range(2):
            term = jnp.where(present, scratch[part], 0.0)
            out[0, part, :, near] += jnp.where(use_near, term, 0.0)
            out[0, part, :, far] += jnp.where(use_near, 0.0, term)


def split_lines(value, lower, count):
    height = value.shape[0] // count
    firsts, seconds = [], []
    for index in range(count):
        first = value[height * index : height * index + height // 2]
        second = value[height * index + height // 2 : height * (index + 1)]
        firsts.append(jnp.where(lower, first, second))
        seconds.append(jnp.where(lower, second, first))
    return joined(firsts, 0), joined(seconds, 0)


def merge_lines(own, other, lower, count):
    height = own.shape[0] // count
    parts = []
    for index in range(count):
        first = own[height * index : height * (index + 1)]
        second = other[height * index : height * (index + 1)]
        parts.append(jnp.where(lower, first, second))
        parts.append(jnp.where(lower, second, first))
    return jnp.concatenate(parts, axis=0)


def merged_quarters(own, other, lower, count):
    lines = own.shape[1] // 4
    quarters = []
    for m in range(4):
        rows = slice(lines * m, lines * (m + 1))
        quarters.append(tuple(merge_lines(own[part, rows], other[part, rows], lower, count) for part in range(2)))
    return quarters


def hand_over(quarters, lower, count, keep, send):
    lines = keep.shape[1] // 4
    for m in range(4):
        rows = slice(lines * m, lines * (m + 1))
        for part in range(2):
            keep[part, rows], send[part, rows] = split_lines(quarters[m][part], lower, count)


def filtered(classes, phase, conjugate):
    quarter = classes[0][0].shape[0]
    result = []
    for index in range(4):
        rows = slice(quarter * index, quarter * (index + 1))
        factor = (phase[0, rows], phase[1, rows])
        result.append((conj_times if conjugate else times)(factor, classes[index]))
    return result


def enter_kernel(number, info, forward, inverse, twiddle, phase, *refs):
    blocks, (keep, send) = refs[:number], refs[number:]
    lower = info[0] == 0
    count = number // 4
    quarters = [
        tuple(joined([blocks[count * m + i][part] for i in range(count)], 0) for part in range(2)) for m in range(4)
    ]
    far = forward_rows(quarters, forward, twiddle)
    hand_over(inverse_rows(filtered(far, phase, False), inverse, twiddle), lower, count, keep, send)


def through_kernel(number, info, forward, inverse, twiddle, phase, own, other, keep, send):
    lower = info[0] == 0
    count = number // 4
    far = forward_rows(merged_quarters(own, other, lower, count), forward, twiddle)
    hand_over(inverse_rows(filtered(far, phase, False), inverse, twiddle), lower, count, keep, send)


def back_kernel(number, info, forward, inverse, twiddle, phase, own, other, keep, send):
    lower = info[0] == 0
    count = number // 4
    far = forward_rows(merged_quarters(own, other, lower, count), forward, twiddle)
    hand_over(inverse_rows(filtered(far, phase, True), inverse, twiddle), lower, count, keep, send)


def residual_kernel(number, info, forward, inverse, twiddle, observed, own, other, keep, send):
    lower = info[0] == 0
    count = number // 4
    far = forward_rows(merged_quarters(own, other, lower, count), forward, twiddle)
    quarter = far[0][0].shape[0]
    seeded = []
    for index in range(4):
        target = observed[0, :, quarter * index : quarter * (index + 1)].T
        residual = far[index][0] * far[index][0] + far[index][1] * far[index][1] - target
        seeded.append((residual * far[index][0], residual * far[index][1]))
    hand_over(inverse_rows(seeded, inverse, twiddle), lower, count, keep, send)


def leave_kernel(number, info, forward, inverse, twiddle, phase, own, other, *blocks):
    lower = info[0] == 0
    count = number // 4
    far = forward_rows(merged_quarters(own, other, lower, count), forward, twiddle)
    quarters = inverse_rows(filtered(far, phase, True), inverse, twiddle)
    height = blocks[0].shape[1]
    for m in range(4):
        for i in range(count):
            for part in range(2):
                blocks[count * m + i][part] = quarters[m][part][height * i : height * (i + 1)]


def lane_classes(own, other, lower, rows):
    quarter = own.shape[2] // 2
    classes = []
    for index in range(4):
        columns = slice(quarter * (index % 2), quarter * (index % 2) + quarter)
        pair = []
        for part in range(2):
            first, second = own[part, rows, columns], other[part, rows, columns]
            pair.append(jnp.where(lower, first, second) if index < 2 else jnp.where(lower, second, first))
        classes.append(tuple(pair))
    return classes


def lanes_out(classes, lower, rows, keep, send):
    quarter = keep.shape[2] // 2
    for index in range(2):
        columns = slice(quarter * index, quarter * (index + 1))
        for part in range(2):
            low, high = classes[index][part], classes[index + 2][part]
            keep[part, rows, columns] = jnp.where(lower, low, high)
            send[part, rows, columns] = jnp.where(lower, high, low)


def lane_quarter(refs, part, columns):
    return joined([ref[part, :, columns] for ref in refs], 0)


def meet_kernel(number, info, forward, inverse, twiddle, own, other, *refs):
    patches, (entering, keep, send) = refs[:number], refs[number:]
    lower = info[0] == 0
    count = number // 4
    lines = own.shape[1] // 4
    table_back, table_on = inverse[0], forward[0]
    quarter = own.shape[2] // 2
    for m in range(4):
        rows = slice(lines * m, lines * (m + 1))
        wave = inverse_lanes(lane_classes(own, other, lower, rows), table_back, twiddle)
        quarters = []
        for piece in range(4):
            columns = slice(quarter * piece, quarter * (piece + 1))
            group = patches[count * m : count * (m + 1)]
            transmit = tuple(lane_quarter(group, part, columns) for part in range(2))
            entering[0, rows, columns] = wave[piece][0]
            entering[1, rows, columns] = wave[piece][1]
            quarters.append(times(wave[piece], transmit))
        lanes_out(forward_lanes(quarters, table_on, twiddle), lower, rows, keep, send)


def grade_kernel(number, info, forward, inverse, twiddle, own, other, entering, *refs):
    patches, terms, (keep, send) = refs[:number], refs[number : 2 * number], refs[2 * number :]
    lower = info[0] == 0
    count = number // 4
    lines = own.shape[1] // 4
    height = lines // count
    table_back, table_on = inverse[0], forward[0]
    quarter = own.shape[2] // 2
    for m in range(4):
        rows = slice(lines * m, lines * (m + 1))
        inner = inverse_lanes(lane_classes(own, other, lower, rows), table_back, twiddle)
        quarters = []
        for piece in range(4):
            columns = slice(quarter * piece, quarter * (piece + 1))
            group = patches[count * m : count * (m + 1)]
            transmit = tuple(lane_quarter(group, part, columns) for part in range(2))
            wave = (entering[0, rows, columns], entering[1, rows, columns])
            term = conj_times(wave, inner[piece])
            for i in range(count):
                for part in range(2):
                    terms[count * m + i][part, :, columns] = term[part][height * i : height * (i + 1)]
            quarters.append(conj_times(transmit, inner[piece]))
        lanes_out(forward_lanes(quarters, table_on, twiddle), lower, rows, keep, send)


def run(kernel, outs, info, *operands):
    return pl.pallas_call(
        kernel,
        out_shape=[jax.ShapeDtypeStruct(shape, jnp.float32) for shape in outs],
        in_specs=[pl.BlockSpec(memory_space=smem)] + [pl.BlockSpec(memory_space=pltpu.VMEM)] * len(operands),
        out_specs=[pl.BlockSpec(memory_space=pltpu.VMEM)] * len(outs),
        compiler_params=pltpu.CompilerParams(vmem_limit_bytes=vmem_bytes),
    )(info, *operands)


def on_device(probe, object_delta, measured, pos_y, pos_x, prop_phase):
    number = lax.axis_size("row")
    sections = lax.axis_size("sect")
    cores = lax.axis_size("batch")
    place, section, core = (lax.axis_index(axis) for axis in line_axes)
    height, breadth = probe.shape[1], probe.shape[2]
    own_probes = measured.shape[1]
    total = cores * own_probes
    spans = object_delta.shape[3] // breadth
    half = height // 2
    wide = breadth // 2
    quarter = breadth // 4

    depth = -(-total // sections)
    top = (number - depth) // 2
    home_x = [q % sections for q in range(total)]
    home_z = [top + q // sections for q in range(total)]
    base = [(home_z[q] + (number // sections) * home_x[q]) % number for q in range(total)]
    assert len(set(base)) == total
    of_base = np.zeros(number, np.int32)
    for q in range(total):
        of_base[base[q]] = q

    def spot(z, x, c):
        return (z * sections + x) * cores + c

    every = [(q, c) for q in range(total) for c in range(cores)]

    def inward(j, layer):
        return [
            (spot((base[q] + j) % number, layer, c), spot(home_z[q], home_x[q], c)) for q, c in every
        ]

    def outward(j, layer):
        return [(target, source) for source, target in inward(j, layer)]

    def inward_line(j):
        return [
            (spot((base[q] + j) % number, home_x[q], c), spot(home_z[q], home_x[q], c)) for q, c in every
        ]

    def move(value, pairs):
        return lax.ppermute(value, line_axes, pairs)

    def swap(value):
        return lax.ppermute(value, "batch", [(i, (i + 1) % cores) for i in range(cores)])

    def ordered(own, other):
        return jnp.where(core == 0, jnp.concatenate([own, other]), jnp.concatenate([other, own]))

    column_forward, column_inverse = (jnp.asarray(table) for table in column_tables(breadth))
    row_pairs = [row_tables(breadth, (height // 4) * base[q]) for q in range(total)]
    row_forward = jnp.asarray(np.stack([pair[0] for pair in row_pairs]))
    row_inverse = jnp.asarray(np.stack([pair[1] for pair in row_pairs]))
    lane_factors, line_factors = (jnp.asarray(table) for table in twiddles(breadth))
    mine = jnp.clip((place - top) * sections + section, 0, total - 1)
    my_forward = lax.dynamic_slice_in_dim(row_forward, mine, 1, 0)
    my_inverse = lax.dynamic_slice_in_dim(row_inverse, mine, 1, 0)

    part = lax.dynamic_slice_in_dim(probe, core * half, half, 1)
    above = lax.ppermute(part, "row", [(i, (i + 1) % number) for i in range(number)])
    above_other = swap(above)
    above = jnp.where(
        core == 0,
        jnp.concatenate([above, above_other], axis=1),
        jnp.concatenate([above_other, above], axis=1),
    )
    window = jnp.concatenate([above, probe], axis=1)

    positions = jnp.stack([pos_y[0], pos_x[0]], axis=1)
    positions = ordered(positions, swap(positions))
    which = [jnp.asarray(of_base)[(place - j) % number] for j in range(number)]
    infos = []
    for j in range(number):
        offset_y, offset_x = positions[which[j], 0], positions[which[j], 1]
        block = offset_x // breadth
        infos.append(
            jnp.stack(
                [
                    core,
                    (place == 0).astype(jnp.int32),
                    block,
                    jnp.minimum(block + 1, spans - 1),
                    offset_x % breadth,
                    offset_y,
                    which[j],
                    section,
                ]
            ).astype(jnp.int32)
        )

    lane_index = jnp.arange(breadth)
    to_classes = (lane_index[:, None] == (4 * (lane_index % quarter) + lane_index // quarter)[None, :]).astype(jnp.float32)
    line_index = jnp.arange(half)

    def class_rows(which_core):
        wanted = 4 * (line_index % (half // 2)) + 2 * which_core + line_index // (half // 2)
        return (wanted[:, None] == jnp.arange(height)[None, :]).astype(jnp.float32)

    def classed(planes, which_core):
        picked = jnp.einsum("au,quv->qav", class_rows(which_core), planes, precision=highest)
        return jnp.einsum("qav,vw->qaw", picked, to_classes, precision=highest)

    def assemble(pieces):
        stacked = jnp.stack([piece.reshape(2, half // 2, breadth) for piece in pieces], axis=1)
        return stacked.reshape(2, quarter, breadth)

    phase_piece = classed(prop_phase[None], core)[0]
    phase = assemble([move(phase_piece, inward_line(j)) for j in range(number)])
    phase = jnp.transpose(phase, (2, 0, 1)).reshape(breadth, wide)
    filter_field = jnp.stack([jnp.cos(phase), jnp.sin(phase)])

    def near_spec(slot):
        return pl.BlockSpec((1, 2, height, breadth), lambda i, info: (0, 0, 0, info[slot]))

    def whole_spec(value):
        return pl.BlockSpec(value.shape, lambda i, info: (0,) * value.ndim)

    def patch_of(info):
        return pl.pallas_call(
            patch_kernel,
            out_shape=jax.ShapeDtypeStruct((2, half, breadth), jnp.float32),
            grid_spec=pltpu.PrefetchScalarGridSpec(
                num_scalar_prefetch=1,
                grid=(1,),
                in_specs=[near_spec(2), near_spec(3)],
                out_specs=pl.BlockSpec((2, half, breadth), lambda i, info: (0, 0, 0)),
                scratch_shapes=[pltpu.VMEM((2, height, breadth), jnp.float32)],
            ),
            compiler_params=pltpu.CompilerParams(vmem_limit_bytes=vmem_bytes),
        )(info, object_delta, object_delta)

    def launch_of(info):
        return pl.pallas_call(
            launch_kernel,
            out_shape=[
                jax.ShapeDtypeStruct((2, height, wide), jnp.float32),
                jax.ShapeDtypeStruct((2, height, breadth), jnp.float32),
            ],
            grid_spec=pltpu.PrefetchScalarGridSpec(
                num_scalar_prefetch=1,
                grid=(1,),
                in_specs=[
                    near_spec(2),
                    near_spec(3),
                    whole_spec(window),
                    pl.BlockSpec((1,) + row_forward.shape[1:], lambda i, info: (info[6], 0, 0, 0)),
                    whole_spec(lane_factors),
                ],
                out_specs=[
                    pl.BlockSpec((2, height, wide), lambda i, info: (0, 0, 0)),
                    pl.BlockSpec((2, height, breadth), lambda i, info: (0, 0, 0)),
                ],
            ),
            compiler_params=pltpu.CompilerParams(vmem_limit_bytes=vmem_bytes),
        )(info, object_delta, object_delta, window, row_forward, lane_factors)

    own_patches = [patch_of(infos[j]) for j in range(number)]
    patches = {
        layer: [move(own_patches[j], inward(j, layer)) for j in range(number)] for layer in range(1, sections)
    }
    launched = [launch_of(infos[j]) for j in range(number)]
    rolled = [item[1] for item in launched]
    blocks = [move(launched[j][0], inward(j, 0)) for j in range(number)]

    own_measured = classed(measured[0], core)
    other_measured = classed(measured[0], 1 - core)
    all_measured = ordered(own_measured, swap(other_measured))
    observed = assemble(
        [
            move(lax.dynamic_index_in_dim(all_measured, which[j], 0, keepdims=False), inward_line(j))
            for j in range(number)
        ]
    )

    about = jnp.stack([core]).astype(jnp.int32)
    traded = (2, breadth // 2, wide)
    column_set = (column_forward, column_inverse, line_factors)
    row_set = (my_forward, my_inverse, lane_factors)

    def rows_run(kernel, outs, field, *operands):
        lanes = 128
        steps = wide // lanes

        def lane_spec(shape):
            return pl.BlockSpec(tuple(shape[:-1]) + (lanes,), lambda i: (0,) * (len(shape) - 1) + (i,))

        if kernel is residual_kernel:
            field_spec = pl.BlockSpec((1,) + field.shape[1:], lambda i: (i, 0, 0))
        else:
            field_spec = lane_spec(field.shape)
        return pl.pallas_call(
            functools.partial(kernel, number),
            grid=(steps,),
            out_shape=[jax.ShapeDtypeStruct(shape, jnp.float32) for shape in outs],
            in_specs=[pl.BlockSpec(memory_space=smem)]
            + [pl.BlockSpec(value.shape, lambda i, nd=value.ndim: (0,) * nd) for value in column_set]
            + [field_spec]
            + [lane_spec(value.shape) for value in operands],
            out_specs=[lane_spec(shape) for shape in outs],
            compiler_params=pltpu.CompilerParams(vmem_limit_bytes=vmem_bytes),
        )(about, *column_set, field, *operands)

    entries = {}
    keep, send = rows_run(enter_kernel, [traded, traded], filter_field, *blocks)
    for layer in range(1, sections):
        other = swap(send)
        entries[layer], keep, send = run(
            functools.partial(meet_kernel, number),
            [(2, breadth // 2, breadth), traded, traded],
            about,
            *row_set,
            keep,
            other,
            *patches[layer],
        )
        other = swap(send)
        if layer < sections - 1:
            keep, send = rows_run(through_kernel, [traded, traded], filter_field, keep, other)
    keep, send = rows_run(residual_kernel, [traded, traded], observed, keep, other)

    terms = None
    for layer in range(sections - 1, 0, -1):
        other = swap(send)
        found = run(
            functools.partial(grade_kernel, number),
            [(2, half, breadth)] * number + [traded, traded],
            about,
            *row_set,
            keep,
            other,
            entries[layer],
            *patches[layer],
        )
        came = [move(found[j], outward(j, layer)) for j in range(number)]
        terms = came if terms is None else [first + second for first, second in zip(terms, came)]
        keep, send = found[number:]
        other = swap(send)
        if layer > 1:
            keep, send = rows_run(back_kernel, [traded, traded], filter_field, keep, other)
    leaving = rows_run(leave_kernel, [(2, height, wide)] * number, filter_field, keep, other)
    spectra = [move(leaving[j], outward(j, 0)) for j in range(number)]

    other_terms = [swap(value) for value in terms]
    other_spectra = [swap(value) for value in spectra]
    info_all = jnp.stack(infos)
    operands = [row_inverse, lane_factors, *spectra, *other_spectra, *terms, *other_terms, *rolled]
    return pl.pallas_call(
        functools.partial(settle_kernel, number),
        out_shape=jax.ShapeDtypeStruct(object_delta.shape, jnp.float32),
        in_specs=[pl.BlockSpec(memory_space=smem)] + [pl.BlockSpec(memory_space=pltpu.VMEM)] * len(operands),
        out_specs=pl.BlockSpec(memory_space=pltpu.VMEM),
        scratch_shapes=[pltpu.VMEM((2, height, breadth), jnp.float32)],
        compiler_params=pltpu.CompilerParams(vmem_limit_bytes=vmem_bytes),
    )(info_all, *operands)


def solution(mesh):
    in_specs = (
        P(None, "row", None),
        P(("groups", "sect"), None, "row", None),
        P(("groups", "batch"), None, "row", None),
        P(("groups", "batch"), None),
        P(("groups", "batch"), None),
        P("row", None),
    )
    out_specs = P(("groups", "sect"), None, "row", None)
    return jax.shard_map(
        on_device, mesh=mesh, in_specs=in_specs, out_specs=out_specs, check_vma=False
    )
```

time: 581 us -> 185 us (0.32)
  waiting for transfers between devices: 185 us -> 37.7 us
  blocking collectives: 100 us -> 0 us
  local copies, waits for them, and re-layouts: 98.7 us -> 15.1 us
  matrix products: 55.2 us -> 5.43 us
  other arithmetic: 45.2 us -> 6.94 us
  loops' own time: 33.8 us -> 0 us
  Pallas kernels: 0 us -> 29.5 us
  starting transfers between devices: 45 us -> 69.9 us
    all_to_all x6 -> x0, blocking collectives: 100 us -> none  [the longest x3 50.5 us: restore(): lax.all_to_all(partial_form, 'row', split_axis=3, concat_axis=2, tiled=True)]
    ppermute x8 -> x40, waiting for transfers between devices: 110 us -> 37.7 us  [the longest x24 34.4 us: move(): return lax.ppermute(value, line_axes, pairs)]
    all_to_all x6 -> x0, waiting for transfers between devices: 52.7 us -> none  [the longest x3 30.2 us: spectrum(): lax.all_to_all(partial_form, 'row', split_axis=2, concat_axis=3, tiled=True)]
    dot_general x24 -> x6, matrix products: 55.2 us -> 5.43 us  [the longest x3 3.32 us: classed(): jnp.einsum('au,quv->qav', class_rows(which_core), planes, precision=highest)]
    ppermute x8 -> x40, starting transfers between devices: 21.1 us -> 69.9 us  [the longest x24 63.6 us: move(): return lax.ppermute(value, line_axes, pairs)]
    another operation x2 -> x0, loops' own time: 33.8 us -> none  [the longest x1 21.8 us: on_device(): lax.fori_loop(0, total_turns, adjoint_turn, (zero_wave, empty_buffer))]
    another operation x25 -> x4, local copies, waits for them, and re-layouts: 37.9 us -> 5.55 us  [on_device(): jnp.stack([core, (place == 0).astype(jnp.int32), block, jnp.minimum(block...]
    pallas_call x0 -> x14, Pallas kernels: none -> 29.5 us  [the longest x3 8.57 us: rows_run(): pl.pallas_call(functools.partial(kernel, number), grid=(steps,), out_shap...]
  transfers between devices with their start and end apart: 15 -> 40, of which waited for: 13 -> 8; matrix products, arithmetic and copies ran while one was open for 8% -> 13% of each run, Pallas kernels for 0% -> 11%
where the time goes in v1:
time: 185 us; the launch traced here: 183 us
  starting transfers between devices  69.9 us (38%)
  waiting for transfers between devices  37.7 us (20%)
  Pallas kernels  29.5 us (16%)
  between operations  18.6 us (10%)
  local copies, waits for them, and re-layouts  15.1 us (8%)
  other arithmetic  6.94 us (4%)
  matrix products  5.43 us (3%)
    ppermute x24, starting transfers between devices, move(): return lax.ppermute(value, line_axes, pairs)  63.6 us
    ppermute x24, waiting for transfers between devices, move(): return lax.ppermute(value, line_axes, pairs)  34.4 us
    pallas_call x3, Pallas kernels, rows_run(): pl.pallas_call(functools.partial(kernel, number), grid=(steps,), out_shap...  8.57 us
    pallas_call x4, Pallas kernels, launch_of(): pl.pallas_call(launch_kernel, out_shape=[jax.ShapeDtypeStruct((2, height,...  8.11 us
    another operation x4, local copies, waits for them, and re-layouts, on_device(): jnp.stack([core, (place == 0).astype(jnp.int32), block, jnp.minimum(block...  5.55 us
    pallas_call x2, Pallas kernels, run(): pl.pallas_call(kernel, out_shape=[jax.ShapeDtypeStruct(shape, jnp.float32...  4.9 us
    pallas_call x1, Pallas kernels, on_device(): pl.pallas_call(functools.partial(settle_kernel, number), out_shape=jax.Sh...  4.44 us
  transfers between devices with their start and end apart: 40, of which 8 were waited for; matrix products, arithmetic and copies ran while one was open for 13% of the time, Pallas kernels for 11%

profile of v1, /device:TPU:0, one launch (start us, length us, event | category | flops | bytes accessed | tf_op | source)
XLA Modules:
  0.0 183.3 jit_solution(10626395282362055524)
XLA Ops:
  1.2 3.1 %collective-permute-start.10 = (f32[2,64,512]{2,1,0:T(8,128)S(1)}, f32[2,64,512]{2,1,0:T(8,128)S(1)}, u32[]{:S(2)}, u32[]{:S(2)}) collective-permute-start(f32[2,64,512]{2,1,0:T(8,128)S(1)} %constant_dynamic-slice_fusion), channel_id=1, source_target_pairs={{0,4},{4,8},{8,12},{12,0},{1,5},{5,9},{9,13},{13,1},{2,6},{6,10},{... | collective-permute-start | bytes 786440 | tf_op jit(solution)/shard_map/ppermute | solution.py:521
  6.6 4.1 %collective-permute-start.4 = (f32[64,512]{1,0:T(8,128)}, f32[64,512]{1,0:T(8,128)}, u32[]{:S(2)}, u32[]{:S(2)}) collective-permute-start(f32[64,512]{1,0:T(8,128)} %fusion.1), channel_id=1, source_target_pairs={{0,4},{1,5},{10,6},{11,7},{4,8},{5,9},{14,10},{15,11},{16,20},{17,... | collective-permute-start | bytes 393224 | tf_op jit(solution)/shard_map/ppermute | solution.py:503
  10.7 2.3 %collective-permute-start.3 = (f32[64,512]{1,0:T(8,128)}, f32[64,512]{1,0:T(8,128)}, u32[]{:S(2)}, u32[]{:S(2)}) collective-permute-start(f32[64,512]{1,0:T(8,128)} %fusion.1), channel_id=1, source_target_pairs={{12,4},{13,5},{6,6},{7,7},{0,8},{1,9},{10,10},{11,11},{28,20},{29,... | collective-permute-start | bytes 393224 | tf_op jit(solution)/shard_map/ppermute | solution.py:503
  38.8 1.4 shard_map.132
  41.5 1.4 stack.117.info
  42.9 1.4 stack.112.info
  44.3 1.5 collective-permute-start.17
  47.1 2.0 %shard_map.127 = (f32[2,128,256]{2,1,0:T(8,128)}, f32[2,128,512]{2,1,0:T(8,128)S(1)}) custom-call(s32[8]{0:T(128)S(1)} %stack.107.info, f32[1,2,128,2048]{3,2,1,0:T(8,128)S(1)} %copy-done.1, f32[1,2,128,2048]{3,2,1,0:T(8,128)S(1)} %copy-done.1, f32[2,256,512]{2,1,0:T(8,128)S(1)} %pad_maximum_fusion.1.window, bf16[4,2,256,256]{3,2,1,0:T(8,128)(2,1)S(1)} %copy-done.2, ...), custom_call_target="tpu_custom_call" | custom-call | tf_op jit(solution)/shard_map/pallas_call | solution.py:594
  49.1 2.0 %shard_map.130 = (f32[2,128,256]{2,1,0:T(8,128)}, f32[2,128,512]{2,1,0:T(8,128)S(1)}) custom-call(s32[8]{0:T(128)S(1)} %stack.122.info, f32[1,2,128,2048]{3,2,1,0:T(8,128)S(1)} %copy-done.1, f32[1,2,128,2048]{3,2,1,0:T(8,128)S(1)} %copy-done.1, f32[2,256,512]{2,1,0:T(8,128)S(1)} %pad_maximum_fusion.1.window, bf16[4,2,256,256]{3,2,1,0:T(8,128)(2,1)S(1)} %copy-done.2, ...), custom_call_target="tpu_custom_call" | custom-call | tf_op jit(solution)/shard_map/pallas_call | solution.py:594
  51.2 2.0 %shard_map.129 = (f32[2,128,256]{2,1,0:T(8,128)}, f32[2,128,512]{2,1,0:T(8,128)S(1)}) custom-call(s32[8]{0:T(128)S(1)} %stack.117.info, f32[1,2,128,2048]{3,2,1,0:T(8,128)S(1)} %copy-done.1, f32[1,2,128,2048]{3,2,1,0:T(8,128)S(1)} %copy-done.1, f32[2,256,512]{2,1,0:T(8,128)S(1)} %pad_maximum_fusion.1.window, bf16[4,2,256,256]{3,2,1,0:T(8,128)(2,1)S(1)} %copy-done.2, ...), custom_call_target="tpu_custom_call" | custom-call | tf_op jit(solution)/shard_map/pallas_call | solution.py:594
  53.2 2.0 %shard_map.128 = (f32[2,128,256]{2,1,0:T(8,128)}, f32[2,128,512]{2,1,0:T(8,128)S(1)}) custom-call(s32[8]{0:T(128)S(1)} %stack.112.info, f32[1,2,128,2048]{3,2,1,0:T(8,128)S(1)} %copy-done.1, f32[1,2,128,2048]{3,2,1,0:T(8,128)S(1)} %copy-done.1, f32[2,256,512]{2,1,0:T(8,128)S(1)} %pad_maximum_fusion.1.window, bf16[4,2,256,256]{3,2,1,0:T(8,128)(2,1)S(1)} %copy-done.2, ...), custom_call_target="tpu_custom_call" | custom-call | tf_op jit(solution)/shard_map/pallas_call | solution.py:594
  55.3 3.3 %collective-permute-start.15 = (f32[2,128,256]{2,1,0:T(8,128)}, f32[2,128,256]{2,1,0:T(8,128)}, u32[]{:S(2)}, u32[]{:S(2)}) collective-permute-start(f32[2,128,256]{2,1,0:T(8,128)} %get-tuple-element.33), channel_id=1, source_target_pairs={{0,4},{1,5},{8,6},{9,7},{4,8},{5,9},{12,10},{13,11},{16,20},{17,21... | collective-permute-start | bytes 786440 | tf_op jit(solution)/shard_map/ppermute | solution.py:503
  58.6 6.0 %collective-permute-start.14 = (f32[2,128,256]{2,1,0:T(8,128)}, f32[2,128,256]{2,1,0:T(8,128)}, u32[]{:S(2)}, u32[]{:S(2)}) collective-permute-start(f32[2,128,256]{2,1,0:T(8,128)} %get-tuple-element.32), channel_id=1, source_target_pairs={{12,4},{13,5},{4,6},{5,7},{0,8},{1,9},{8,10},{9,11},{28,20},{29,21... | collective-permute-start | bytes 786440 | tf_op jit(solution)/shard_map/ppermute | solution.py:503
  64.6 2.0 %collective-permute-start.13 = (f32[2,128,256]{2,1,0:T(8,128)}, f32[2,128,256]{2,1,0:T(8,128)}, u32[]{:S(2)}, u32[]{:S(2)}) collective-permute-start(f32[2,128,256]{2,1,0:T(8,128)} %get-tuple-element.31), channel_id=1, source_target_pairs={{8,4},{9,5},{0,6},{1,7},{12,8},{13,9},{4,10},{5,11},{24,20},{25,21... | collective-permute-start | bytes 786440 | tf_op jit(solution)/shard_map/ppermute | solution.py:503
  66.6 2.0 %collective-permute-start.12 = (f32[2,128,256]{2,1,0:T(8,128)}, f32[2,128,256]{2,1,0:T(8,128)}, u32[]{:S(2)}, u32[]{:S(2)}) collective-permute-start(f32[2,128,256]{2,1,0:T(8,128)} %get-tuple-element.30), channel_id=1, source_target_pairs={{4,4},{5,5},{12,6},{13,7},{8,8},{9,9},{0,10},{1,11},{20,20},{21,21... | collective-permute-start | bytes 786440 | tf_op jit(solution)/shard_map/ppermute | solution.py:503
  68.6 3.6 %fusion.12 = (f32[2,4,32,512]{3,2,1,0:T(8,128)}, f32[2,4,32,512]{3,2,1,0:T(8,128)}) fusion(f32[2,1,32,512]{3,2,1,0:T(8,128)} %bitcast.40, f32[2,1,32,512]{3,2,1,0:T(8,128)} %bitcast.38, f32[2,1,32,512]{3,2,1,0:T(8,128)} %bitcast.36, f32[2,1,32,512]{3,2,1,0:T(8,128)} %bitcast.34), kind=kLoop, calls=%fused_computation.19 | loop fusion | flops 393216 | bytes 1572864 | tf_op jit(solution)/shard_map/cos | solution.py:571
  72.2 2.1 %copy.22 = f32[1,512,256]{2,1,0:T(8,128)} copy(f32[1,512,256]{1,2,0:T(8,128)} %bitcast.97) | data formatting | bytes 1048576 | tf_op jit(solution)/shard_map/cos | solution.py:571
  74.3 2.0 %copy.23 = f32[1,512,256]{2,1,0:T(8,128)} copy(f32[1,512,256]{1,2,0:T(8,128)} %bitcast.96) | data formatting | bytes 1048576 | tf_op jit(solution)/shard_map/sin | solution.py:571
  77.7 3.3 %collective-permute-done.12.refs_0_ = f32[2,128,256]{2,1,0:T(8,128)} collective-permute-done((f32[2,128,256]{2,1,0:T(8,128)}, f32[2,128,256]{2,1,0:T(8,128)}, u32[]{:S(2)}, u32[]{:S(2)}) %collective-permute-start.12) | collective-permute-done | bytes 262176 | tf_op jit(solution)/shard_map/ppermute | solution.py:503
  81.0 4.0 %shard_map.131 = (f32[2,256,256]{2,1,0:T(8,128)S(1)}, f32[2,256,256]{2,1,0:T(8,128)}) custom-call(s32[1]{0:T(128)} %bitcast.info, bf16[2,256,256]{2,1,0:T(8,128)(2,1)S(1)} %copy-done.7, bf16[2,256,256]{2,1,0:T(8,128)(2,1)S(1)} %copy-done.6, f32[4,2,128,128]{3,2,1,0:T(8,128)S(1)} %copy-done.5, f32[2,512,256]{2,1,0:T(8,128)S(1)} %pad_maximum_fusion.phase, ...), custom_call_target="tpu_custom_call" | custom-call | tf_op jit(solution)/shard_map/pallas_call | solution.py:652
  94.3 2.5 %shard_map.136 = (f32[2,256,512]{2,1,0:T(8,128)S(1)}, f32[2,256,256]{2,1,0:T(8,128)S(1)}, f32[2,256,256]{2,1,0:T(8,128)S(1)}) custom-call(s32[1]{0:T(128)} %bitcast.info, bf16[1,2,256,256]{3,2,1,0:T(8,128)(2,1)S(1)} %get-tuple-element.74.forward, bf16[1,2,256,256]{3,2,1,0:T(8,128)(2,1)S(1)} %get-tuple-element.73.inverse, f32[8,128]{1,0:T(8,128)S(1)} %copy-done.20, ...), custom_call_target="tpu_custom_call" | custom-call | tf_op jit(solution)/shard_map/pallas_call | solution.py:452
  98.4 26.7 %collective-permute-start.9 = (f32[64,512]{1,0:T(8,128)S(1)}, f32[64,512]{1,0:T(8,128)S(1)}, u32[]{:S(2)}, u32[]{:S(2)}) collective-permute-start(f32[64,512]{1,0:T(8,128)S(1)} %get-tuple-element.56), channel_id=1, source_target_pairs={{0,4},{1,5},{10,6},{11,7},{4,8},{5,9},{14,10},{15,11},{16,20},{17,... | collective-permute-start | bytes 393224 | tf_op jit(solution)/shard_map/ppermute | solution.py:503
  127.1 1.8 collective-permute-done.9
  128.9 2.4 %collective-permute-done.8 = f32[64,512]{1,0:T(8,128)S(1)} collective-permute-done((f32[64,512]{1,0:T(8,128)S(1)}, f32[64,512]{1,0:T(8,128)S(1)}, u32[]{:S(2)}, u32[]{:S(2)}) %collective-permute-start.8) | collective-permute-done | bytes 131104 | tf_op jit(solution)/shard_map/ppermute | solution.py:503
  131.4 2.3 %shard_map.137 = (f32[2,256,256]{2,1,0:T(8,128)S(1)}, f32[2,256,256]{2,1,0:T(8,128)S(1)}) custom-call(s32[1]{0:T(128)} %bitcast.info, bf16[2,256,256]{2,1,0:T(8,128)(2,1)S(1)} %copy-done.8, bf16[2,256,256]{2,1,0:T(8,128)(2,1)S(1)} %copy-done.6, f32[4,2,128,128]{3,2,1,0:T(8,128)S(1)} %copy-done.5, f32[2,128,512]{2,1,0:T(8,128)S(1)} %bitcast.91, ...), custom_call_target="tpu_custom_call" | custom-call | tf_op jit(solution)/shard_map/pallas_call | solution.py:652
  133.8 1.9 %collective-permute-done.22.other = f32[2,256,256]{2,1,0:T(8,128)S(1)} collective-permute-done((f32[2,256,256]{2,1,0:T(8,128)S(1)}, f32[2,256,256]{2,1,0:T(8,128)S(1)}, u32[]{:S(2)}, u32[]{:S(2)}) %collective-permute-start.22) | collective-permute-done | bytes 524320 | tf_op jit(solution)/shard_map/ppermute | solution.py:506
  135.7 2.4 %shard_map.138 = (f32[2,64,512]{2,1,0:T(8,128)S(1)}, f32[2,64,512]{2,1,0:T(8,128)S(1)}, f32[2,64,512]{2,1,0:T(8,128)S(1)}, f32[2,64,512]{2,1,0:T(8,128)S(1)}, f3...) custom-call(s32[1]{0:T(128)} %bitcast.info, bf16[1,2,256,256]{3,2,1,0:T(8,128)(2,1)S(1)} %get-tuple-element.74.forward, ...), custom_call_target="tpu_custom_call" | custom-call | tf_op jit(solution)/shard_map/pallas_call | solution.py:452
  142.1 2.3 %shard_map.139 = (f32[2,128,256]{2,1,0:T(8,128)S(1)}, f32[2,128,256]{2,1,0:T(8,128)S(1)}, f32[2,128,256]{2,1,0:T(8,128)S(1)}, f32[2,128,256]{2,1,0:T(8,128)S(1)}) custom-call(s32[1]{0:T(128)} %bitcast.info, bf16[2,256,256]{2,1,0:T(8,128)(2,1)S(1)} %copy-done.8, bf16[2,256,256]{2,1,0:T(8,128)(2,1)S(1)} %copy-done.6, f32[4,2,128,128]{3,2,1,0:T(8,128)S(1)} %copy-done.5, ...), custom_call_target="tpu_custom_call" | custom-call | tf_op jit(solution)/shard_map/pallas_call | solution.py:652
  149.9 20.7 %collective-permute-done.24.refs_0_ = f32[2,128,256]{2,1,0:T(8,128)S(1)} collective-permute-done((f32[2,128,256]{2,1,0:T(8,128)S(1)}, f32[2,128,256]{2,1,0:T(8,128)S(1)}, u32[]{:S(2)}, u32[]{:S(2)}) %collective-permute-start.24) | collective-permute-done | bytes 262176 | tf_op jit(solution)/shard_map/ppermute | solution.py:503
  170.6 4.4 %collective-permute-done.25.refs_1_ = f32[2,128,256]{2,1,0:T(8,128)S(1)} collective-permute-done((f32[2,128,256]{2,1,0:T(8,128)S(1)}, f32[2,128,256]{2,1,0:T(8,128)S(1)}, u32[]{:S(2)}, u32[]{:S(2)}) %collective-permute-start.25) | collective-permute-done | bytes 262176 | tf_op jit(solution)/shard_map/ppermute | solution.py:503
  175.5 1.7 collective-permute-done.27.refs_3_
  178.8 4.4 %shard_map.140 = f32[1,2,128,2048]{3,2,1,0:T(8,128)} custom-call(s32[4,8]{1,0:T(4,128)S(1)} %pad_add_fusion.info, bf16[4,2,256,256]{3,2,1,0:T(8,128)(2,1)S(1)} %copy-done.9, f32[8,128]{1,0:T(8,128)S(1)} %copy-done.20, f32[2,128,256]{2,1,0:T(8,128)S(1)} %collective-permute-done.24.refs_0_, f32[2,128,256]{2,1,0:T(8,128)S(1)} %collective-permute-done.25.refs_1_, ...), custom_call_target="tpu_custom_call" | custom-call | tf_op jit(solution)/shard_map/pallas_call | solution.py:708
  (145 shorter events, 39.3 us)
Async XLA Ops:
  1.2 13.9 %collective-permute-start.10 = (f32[2,64,512]{2,1,0:T(8,128)S(1)}, f32[2,64,512]{2,1,0:T(8,128)S(1)}, u32[]{:S(2)}, u32[]{:S(2)}) collective-permute-start(f32[2,64,512]{2,1,0:T(8,128)S(1)} %constant_dynamic-slice_fusion), channel_id=1, source_target_pairs={{0,4},{4,8},{8,12},{12,0},{1,5},{5,9},{9,13},{13,1},{2,6},{6,10},{... | collective-permute-start | bytes 786440 | tf_op jit(solution)/shard_map/ppermute | solution.py:521
  6.6 48.6 %collective-permute-start.4 = (f32[64,512]{1,0:T(8,128)}, f32[64,512]{1,0:T(8,128)}, u32[]{:S(2)}, u32[]{:S(2)}) collective-permute-start(f32[64,512]{1,0:T(8,128)} %fusion.1), channel_id=1, source_target_pairs={{0,4},{1,5},{10,6},{11,7},{4,8},{5,9},{14,10},{15,11},{16,20},{17,... | collective-permute-start | bytes 393224 | tf_op jit(solution)/shard_map/ppermute | solution.py:503
  10.7 47.8 %collective-permute-start.3 = (f32[64,512]{1,0:T(8,128)}, f32[64,512]{1,0:T(8,128)}, u32[]{:S(2)}, u32[]{:S(2)}) collective-permute-start(f32[64,512]{1,0:T(8,128)} %fusion.1), channel_id=1, source_target_pairs={{12,4},{13,5},{6,6},{7,7},{0,8},{1,9},{10,10},{11,11},{28,20},{29,... | collective-permute-start | bytes 393224 | tf_op jit(solution)/shard_map/ppermute | solution.py:503
  13.1 51.5 %collective-permute-start.2 = (f32[64,512]{1,0:T(8,128)}, f32[64,512]{1,0:T(8,128)}, u32[]{:S(2)}, u32[]{:S(2)}) collective-permute-start(f32[64,512]{1,0:T(8,128)} %fusion.1), channel_id=1, source_target_pairs={{8,4},{9,5},{2,6},{3,7},{12,8},{13,9},{6,10},{7,11},{24,20},{25,21... | collective-permute-start | bytes 393224 | tf_op jit(solution)/shard_map/ppermute | solution.py:503
  15.1 10.1 %collective-permute-start = (s32[2,2]{0,1:T(2,128)S(1)}, s32[2,2]{0,1:T(2,128)S(1)}, u32[]{:S(2)}, u32[]{:S(2)}) collective-permute-start(s32[2,2]{0,1:T(2,128)S(1)} %pad_add_fusion.1), channel_id=1, source_target_pairs={{0,1},{1,0},{2,3},{3,2},{4,5},{5,4},{6,7},{7,6},{8,9},{9,8},{10,11... | collective-permute-start | bytes 56 | tf_op jit(solution)/shard_map/ppermute | solution.py:506
  15.1 29.3 %collective-permute-start.11 = (f32[2,64,512]{2,1,0:T(8,128)S(1)}, f32[2,64,512]{2,1,0:T(8,128)}, u32[]{:S(2)}, u32[]{:S(2)}) collective-permute-start(f32[2,64,512]{2,1,0:T(8,128)S(1)} %collective-permute-done.10), channel_id=1, source_target_pairs={{0,1},{1,0},{2,3},{3,2},{4,5},{5,4},{6,7},{7,6},{8,9},{9,8},{10,11... | collective-permute-start | bytes 786440 | tf_op jit(solution)/shard_map/ppermute | solution.py:506
  25.2 41.4 %collective-permute-start.1 = (f32[64,512]{1,0:T(8,128)}, f32[64,512]{1,0:T(8,128)}, u32[]{:S(2)}, u32[]{:S(2)}) collective-permute-start(f32[64,512]{1,0:T(8,128)} %fusion.1), channel_id=1, source_target_pairs={{4,4},{5,5},{14,6},{15,7},{8,8},{9,9},{2,10},{3,11},{20,20},{21,21... | collective-permute-start | bytes 393224 | tf_op jit(solution)/shard_map/ppermute | solution.py:503
  44.3 48.3 %collective-permute-start.17 = (f32[2,64,512]{2,1,0:T(8,128)}, f32[2,64,512]{2,1,0:T(8,128)}, u32[]{:S(2)}, u32[]{:S(2)}) collective-permute-start(f32[2,64,512]{2,1,0:T(8,128)} %shard_map.132), channel_id=1, source_target_pairs={{6,4},{7,5},{14,6},{15,7},{10,8},{11,9},{2,10},{3,11},{22,20},{23,... | collective-permute-start | bytes 786440 | tf_op jit(solution)/shard_map/ppermute | solution.py:503
  55.3 22.4 %collective-permute-start.15 = (f32[2,128,256]{2,1,0:T(8,128)}, f32[2,128,256]{2,1,0:T(8,128)}, u32[]{:S(2)}, u32[]{:S(2)}) collective-permute-start(f32[2,128,256]{2,1,0:T(8,128)} %get-tuple-element.33), channel_id=1, source_target_pairs={{0,4},{1,5},{8,6},{9,7},{4,8},{5,9},{12,10},{13,11},{16,20},{17,21... | collective-permute-start | bytes 786440 | tf_op jit(solution)/shard_map/ppermute | solution.py:503
  58.6 19.1 %collective-permute-start.14 = (f32[2,128,256]{2,1,0:T(8,128)}, f32[2,128,256]{2,1,0:T(8,128)}, u32[]{:S(2)}, u32[]{:S(2)}) collective-permute-start(f32[2,128,256]{2,1,0:T(8,128)} %get-tuple-element.32), channel_id=1, source_target_pairs={{12,4},{13,5},{4,6},{5,7},{0,8},{1,9},{8,10},{9,11},{28,20},{29,21... | collective-permute-start | bytes 786440 | tf_op jit(solution)/shard_map/ppermute | solution.py:503
  64.6 13.1 %collective-permute-start.13 = (f32[2,128,256]{2,1,0:T(8,128)}, f32[2,128,256]{2,1,0:T(8,128)}, u32[]{:S(2)}, u32[]{:S(2)}) collective-permute-start(f32[2,128,256]{2,1,0:T(8,128)} %get-tuple-element.31), channel_id=1, source_target_pairs={{8,4},{9,5},{0,6},{1,7},{12,8},{13,9},{4,10},{5,11},{24,20},{25,21... | collective-permute-start | bytes 786440 | tf_op jit(solution)/shard_map/ppermute | solution.py:503
  66.6 14.4 %collective-permute-start.12 = (f32[2,128,256]{2,1,0:T(8,128)}, f32[2,128,256]{2,1,0:T(8,128)}, u32[]{:S(2)}, u32[]{:S(2)}) collective-permute-start(f32[2,128,256]{2,1,0:T(8,128)} %get-tuple-element.30), channel_id=1, source_target_pairs={{4,4},{5,5},{12,6},{13,7},{8,8},{9,9},{0,10},{1,11},{20,20},{21,21... | collective-permute-start | bytes 786440 | tf_op jit(solution)/shard_map/ppermute | solution.py:503
  86.8 7.5 %collective-permute-start.16 = (f32[2,256,256]{2,1,0:T(8,128)}, f32[2,256,256]{2,1,0:T(8,128)}, u32[]{:S(2)}, u32[]{:S(2)}) collective-permute-start(f32[2,256,256]{2,1,0:T(8,128)} %get-tuple-element.35), channel_id=1, source_target_pairs={{0,1},{1,0},{2,3},{3,2},{4,5},{5,4},{6,7},{7,6},{8,9},{9,8},{10,11... | collective-permute-start | bytes 1572872 | tf_op jit(solution)/shard_map/ppermute | solution.py:506
  90.0 4.3 %collective-permute-start.20 = (f32[2,64,512]{2,1,0:T(8,128)S(1)}, f32[2,64,512]{2,1,0:T(8,128)S(1)}, u32[]{:S(2)}, u32[]{:S(2)}) collective-permute-start(f32[2,64,512]{2,1,0:T(8,128)S(1)} %shard_map.135), channel_id=1, source_target_pairs={{2,4},{3,5},{10,6},{11,7},{6,8},{7,9},{14,10},{15,11},{18,20},{19,... | collective-permute-start | bytes 786440 | tf_op jit(solution)/shard_map/ppermute | solution.py:503
  90.8 3.5 %collective-permute-start.19 = (f32[2,64,512]{2,1,0:T(8,128)S(1)}, f32[2,64,512]{2,1,0:T(8,128)S(1)}, u32[]{:S(2)}, u32[]{:S(2)}) collective-permute-start(f32[2,64,512]{2,1,0:T(8,128)S(1)} %shard_map.134), channel_id=1, source_target_pairs={{14,4},{15,5},{6,6},{7,7},{2,8},{3,9},{10,10},{11,11},{30,20},{31,... | collective-permute-start | bytes 786440 | tf_op jit(solution)/shard_map/ppermute | solution.py:503
  92.7 4.7 %collective-permute-start.5 = (f32[2,64,512]{2,1,0:T(8,128)S(1)}, f32[2,64,512]{2,1,0:T(8,128)S(1)}, u32[]{:S(2)}, u32[]{:S(2)}) collective-permute-start(f32[2,64,512]{2,1,0:T(8,128)S(1)} %fusion.2), channel_id=1, source_target_pairs={{0,1},{1,0},{2,3},{3,2},{4,5},{5,4},{6,7},{7,6},{8,9},{9,8},{10,11... | collective-permute-start | bytes 786440 | tf_op jit(solution)/shard_map/ppermute | solution.py:506
  96.8 34.5 %collective-permute-start.21 = (f32[2,256,256]{2,1,0:T(8,128)S(1)}, f32[2,256,256]{2,1,0:T(8,128)S(1)}, u32[]{:S(2)}, u32[]{:S(2)}) collective-permute-start(f32[2,256,256]{2,1,0:T(8,128)S(1)} %get-tuple-element.37), channel_id=1, source_target_pairs={{0,1},{1,0},{2,3},{3,2},{4,5},{5,4},{6,7},{7,6},{8,9},{9,8},{10,11... | collective-permute-start | bytes 1572872 | tf_op jit(solution)/shard_map/ppermute | solution.py:506
  97.5 29.6 %collective-permute-start.6 = (f32[64,512]{1,0:T(8,128)S(1)}, f32[64,512]{1,0:T(8,128)S(1)}, u32[]{:S(2)}, u32[]{:S(2)}) collective-permute-start(f32[64,512]{1,0:T(8,128)S(1)} %get-tuple-element.55), channel_id=1, source_target_pairs={{4,4},{5,5},{14,6},{15,7},{8,8},{9,9},{2,10},{3,11},{20,20},{21,21... | collective-permute-start | bytes 393224 | tf_op jit(solution)/shard_map/ppermute | solution.py:503
  98.4 30.5 %collective-permute-start.9 = (f32[64,512]{1,0:T(8,128)S(1)}, f32[64,512]{1,0:T(8,128)S(1)}, u32[]{:S(2)}, u32[]{:S(2)}) collective-permute-start(f32[64,512]{1,0:T(8,128)S(1)} %get-tuple-element.56), channel_id=1, source_target_pairs={{0,4},{1,5},{10,6},{11,7},{4,8},{5,9},{14,10},{15,11},{16,20},{17,... | collective-permute-start | bytes 393224 | tf_op jit(solution)/shard_map/ppermute | solution.py:503
  125.1 6.2 %collective-permute-start.8 = (f32[64,512]{1,0:T(8,128)S(1)}, f32[64,512]{1,0:T(8,128)S(1)}, u32[]{:S(2)}, u32[]{:S(2)}) collective-permute-start(f32[64,512]{1,0:T(8,128)S(1)} %get-tuple-element.57), channel_id=1, source_target_pairs={{12,4},{13,5},{6,6},{7,7},{0,8},{1,9},{10,10},{11,11},{28,20},{29,... | collective-permute-start | bytes 393224 | tf_op jit(solution)/shard_map/ppermute | solution.py:503
  126.4 4.9 %collective-permute-start.7 = (f32[64,512]{1,0:T(8,128)S(1)}, f32[64,512]{1,0:T(8,128)S(1)}, u32[]{:S(2)}, u32[]{:S(2)}) collective-permute-start(f32[64,512]{1,0:T(8,128)S(1)} %get-tuple-element.58), channel_id=1, source_target_pairs={{8,4},{9,5},{2,6},{3,7},{12,8},{13,9},{6,10},{7,11},{24,20},{25,21... | collective-permute-start | bytes 393224 | tf_op jit(solution)/shard_map/ppermute | solution.py:503
  138.1 4.0 %collective-permute-start.23 = (f32[2,256,256]{2,1,0:T(8,128)S(1)}, f32[2,256,256]{2,1,0:T(8,128)S(1)}, u32[]{:S(2)}, u32[]{:S(2)}) collective-permute-start(f32[2,256,256]{2,1,0:T(8,128)S(1)} %get-tuple-element.42), channel_id=1, source_target_pairs={{0,1},{1,0},{2,3},{3,2},{4,5},{5,4},{6,7},{7,6},{8,9},{9,8},{10,11... | collective-permute-start | bytes 1572872 | tf_op jit(solution)/shard_map/ppermute | solution.py:506
  140.5 5.3 %collective-permute-start.35 = (f32[2,64,512]{2,1,0:T(8,128)S(1)}, f32[2,64,512]{2,1,0:T(8,128)S(1)}, u32[]{:S(2)}, u32[]{:S(2)}) collective-permute-start(f32[2,64,512]{2,1,0:T(8,128)S(1)} %get-tuple-element.50), channel_id=1, source_target_pairs={{4,2},{5,3},{6,10},{7,11},{8,6},{9,7},{10,14},{11,15},{20,18},{21,... | collective-permute-start | bytes 786440 | tf_op jit(solution)/shard_map/ppermute | solution.py:503
  141.2 5.9 %collective-permute-start.36 = (f32[2,64,512]{2,1,0:T(8,128)S(1)}, f32[2,64,512]{2,1,0:T(8,128)S(1)}, u32[]{:S(2)}, u32[]{:S(2)}) collective-permute-start(f32[2,64,512]{2,1,0:T(8,128)S(1)} %collective-permute-done.32.refs_8_), channel_id=1, source_target_pairs={{0,1},{1,0},{2,3},{3,2},{4,5},{5,4},{6,7},{7,6},{8,9},{9,8},{10,11... | collective-permute-start | bytes 786440 | tf_op jit(solution)/shard_map/ppermute | solution.py:506
  141.6 6.8 %collective-permute-start.37 = (f32[2,64,512]{2,1,0:T(8,128)S(1)}, f32[2,64,512]{2,1,0:T(8,128)S(1)}, u32[]{:S(2)}, u32[]{:S(2)}) collective-permute-start(f32[2,64,512]{2,1,0:T(8,128)S(1)} %collective-permute-done.33.refs_9_), channel_id=1, source_target_pairs={{0,1},{1,0},{2,3},{3,2},{4,5},{5,4},{6,7},{7,6},{8,9},{9,8},{10,11... | collective-permute-start | bytes 786440 | tf_op jit(solution)/shard_map/ppermute | solution.py:506
  141.8 7.9 %collective-permute-start.38 = (f32[2,64,512]{2,1,0:T(8,128)S(1)}, f32[2,64,512]{2,1,0:T(8,128)S(1)}, u32[]{:S(2)}, u32[]{:S(2)}) collective-permute-start(f32[2,64,512]{2,1,0:T(8,128)S(1)} %collective-permute-done.34.refs_10_), channel_id=1, source_target_pairs={{0,1},{1,0},{2,3},{3,2},{4,5},{5,4},{6,7},{7,6},{8,9},{9,8},{10,11... | collective-permute-start | bytes 786440 | tf_op jit(solution)/shard_map/ppermute | solution.py:506
  144.5 26.1 %collective-permute-start.24 = (f32[2,128,256]{2,1,0:T(8,128)S(1)}, f32[2,128,256]{2,1,0:T(8,128)S(1)}, u32[]{:S(2)}, u32[]{:S(2)}) collective-permute-start(f32[2,128,256]{2,1,0:T(8,128)S(1)} %get-tuple-element.43), channel_id=1, source_target_pairs={{4,4},{5,5},{6,12},{7,13},{8,8},{9,9},{10,0},{11,1},{20,20},{21,21... | collective-permute-start | bytes 786440 | tf_op jit(solution)/shard_map/ppermute | solution.py:503
  145.8 29.2 %collective-permute-start.25 = (f32[2,128,256]{2,1,0:T(8,128)S(1)}, f32[2,128,256]{2,1,0:T(8,128)S(1)}, u32[]{:S(2)}, u32[]{:S(2)}) collective-permute-start(f32[2,128,256]{2,1,0:T(8,128)S(1)} %get-tuple-element.44), channel_id=1, source_target_pairs={{4,8},{5,9},{6,0},{7,1},{8,12},{9,13},{10,4},{11,5},{20,24},{21,25... | collective-permute-start | bytes 786440 | tf_op jit(solution)/shard_map/ppermute | solution.py:503
  147.1 27.9 %collective-permute-start.26 = (f32[2,128,256]{2,1,0:T(8,128)S(1)}, f32[2,128,256]{2,1,0:T(8,128)S(1)}, u32[]{:S(2)}, u32[]{:S(2)}) collective-permute-start(f32[2,128,256]{2,1,0:T(8,128)S(1)} %get-tuple-element.45), channel_id=1, source_target_pairs={{4,12},{5,13},{6,4},{7,5},{8,0},{9,1},{10,8},{11,9},{20,28},{21,29... | collective-permute-start | bytes 786440 | tf_op jit(solution)/shard_map/ppermute | solution.py:503
  148.4 28.9 %collective-permute-start.27 = (f32[2,128,256]{2,1,0:T(8,128)S(1)}, f32[2,128,256]{2,1,0:T(8,128)S(1)}, u32[]{:S(2)}, u32[]{:S(2)}) collective-permute-start(f32[2,128,256]{2,1,0:T(8,128)S(1)} %get-tuple-element.46), channel_id=1, source_target_pairs={{4,0},{5,1},{6,8},{7,9},{8,4},{9,5},{10,12},{11,13},{20,16},{21,17... | collective-permute-start | bytes 786440 | tf_op jit(solution)/shard_map/ppermute | solution.py:503
  149.7 27.7 %collective-permute-start.39 = (f32[2,64,512]{2,1,0:T(8,128)S(1)}, f32[2,64,512]{2,1,0:T(8,128)S(1)}, u32[]{:S(2)}, u32[]{:S(2)}) collective-permute-start(f32[2,64,512]{2,1,0:T(8,128)S(1)} %collective-permute-done.35.refs_11_), channel_id=1, source_target_pairs={{0,1},{1,0},{2,3},{3,2},{4,5},{5,4},{6,7},{7,6},{8,9},{9,8},{10,11... | collective-permute-start | bytes 786440 | tf_op jit(solution)/shard_map/ppermute | solution.py:506
  170.6 6.8 %collective-permute-start.28 = (f32[2,128,256]{2,1,0:T(8,128)S(1)}, f32[2,128,256]{2,1,0:T(8,128)S(1)}, u32[]{:S(2)}, u32[]{:S(2)}) collective-permute-start(f32[2,128,256]{2,1,0:T(8,128)S(1)} %collective-permute-done.24.refs_0_), channel_id=1, source_target_pairs={{0,1},{1,0},{2,3},{3,2},{4,5},{5,4},{6,7},{7,6},{8,9},{9,8},{10,11... | collective-permute-start | bytes 786440 | tf_op jit(solution)/shard_map/ppermute | solution.py:506
  (35 other events, 432.3 us)

commit v2 on v1

v2 whole, which is shorter than its diff:
```python
import functools
import math

import jax
import jax.numpy as jnp
import ml_dtypes
import numpy as np
from jax import lax
from jax.experimental import pallas as pl
from jax.experimental.pallas import tpu as pltpu
from jax.sharding import PartitionSpec as P

highest = lax.Precision.HIGHEST
line_axes = ("row", "sect", "batch")
vmem_bytes = 20 * 1024 * 1024
light = pl.CostEstimate(flops=0, transcendentals=0, bytes_accessed=0)
smem = pltpu.MemorySpace.SMEM


def halves(table):
    table = table.astype(np.float64)
    upper = table.astype(ml_dtypes.bfloat16)
    lower = (table - upper.astype(np.float64)).astype(ml_dtypes.bfloat16)
    return np.stack([upper, lower])


def circle(length):
    quarter = length // 4
    index = np.arange(quarter)
    angles = (index[:, None] * index[None, :] % quarter) * (2.0 * math.pi / quarter)
    scale = 1.0 / math.sqrt(length)
    return np.cos(angles) * scale, np.sin(angles) * scale


def column_tables(length):
    cosine, sine = circle(length)
    forward = np.block([[cosine, sine], [-sine, cosine]])
    inverse = np.block([[cosine, -sine], [sine, cosine]])
    return halves(forward), halves(inverse)


def row_tables(length):
    cosine, sine = circle(length)
    forward = np.block([[cosine, -sine], [sine, cosine]])
    inverse = np.block([[cosine.T, sine.T], [-sine.T, cosine.T]])
    return halves(forward), halves(inverse)


def twiddles(length):
    quarter = length // 4
    angles = np.arange(4)[:, None] * np.arange(quarter)[None, :] * (2.0 * math.pi / length)
    pairs = np.stack([np.cos(angles), np.sin(angles)], axis=1).astype(np.float32)
    along_lanes = pairs.reshape(8, quarter)
    along_rows = np.broadcast_to(pairs[..., None], (4, 2, quarter, 128)).copy()
    return along_lanes, along_rows


def circle_polynomials(reach):
    grid = np.cos((np.arange(64) + 0.5) * math.pi / 64.0)
    square = (grid + 1.0) * 0.5 * reach * reach
    root = np.sqrt(square)
    found = []
    for values in (np.cos(root), np.sinc(root / math.pi)):
        fitted = np.polynomial.Polynomial.fit(square, values, 9, domain=[0.0, reach * reach])
        found.append([float(item) for item in fitted.convert().coef])
    return found


def split(value):
    upper = value.astype(jnp.bfloat16)
    lower = (value - upper.astype(jnp.float32)).astype(jnp.bfloat16)
    return upper, lower


def dot(first, second):
    return jnp.dot(first, second, preferred_element_type=jnp.float32)


def right_dot(value, table):
    upper, lower = split(value)
    return dot(upper, table[0]) + dot(lower, table[0]) + dot(upper, table[1])


def left_dot(table, value):
    upper, lower = split(value)
    return dot(table[0], upper) + dot(table[0], lower) + dot(table[1], upper)


def times(first, second):
    return (
        first[0] * second[0] - first[1] * second[1],
        first[0] * second[1] + first[1] * second[0],
    )


def conj_times(first, second):
    return (
        first[0] * second[0] + first[1] * second[1],
        first[0] * second[1] - first[1] * second[0],
    )


def plus(first, second):
    return (first[0] + second[0], first[1] + second[1])


def minus(first, second):
    return (first[0] - second[0], first[1] - second[1])


def turned(value):
    return (-value[1], value[0])


def scatter4(parts):
    sum02, dif02 = plus(parts[0], parts[2]), minus(parts[0], parts[2])
    sum13, dif13 = plus(parts[1], parts[3]), turned(minus(parts[1], parts[3]))
    return [plus(sum02, sum13), minus(dif02, dif13), minus(sum02, sum13), plus(dif02, dif13)]


def gather4(parts):
    sum02, dif02 = plus(parts[0], parts[2]), minus(parts[0], parts[2])
    sum13, dif13 = plus(parts[1], parts[3]), turned(minus(parts[1], parts[3]))
    return [plus(sum02, sum13), plus(dif02, dif13), minus(sum02, sum13), minus(dif02, dif13)]


def lane_twiddle(reference, index):
    return (reference[2 * index : 2 * index + 1, :], reference[2 * index + 1 : 2 * index + 2, :])


def forward_lanes(quarters, table, twiddle):
    rows = quarters[0][0].shape[0]
    classes = scatter4(quarters)
    packed = []
    for index, value in enumerate(classes):
        if index > 0:
            value = conj_times(lane_twiddle(twiddle, index), value)
        packed.append(jnp.concatenate(value, axis=1))
    result = right_dot(jnp.concatenate(packed, axis=0), table)
    half = result.shape[1] // 2
    return [
        (result[rows * index : rows * (index + 1), :half], result[rows * index : rows * (index + 1), half:])
        for index in range(4)
    ]


def inverse_lanes(classes, table, twiddle):
    rows = classes[0][0].shape[0]
    packed = jnp.concatenate([jnp.concatenate(value, axis=1) for value in classes], axis=0)
    result = right_dot(packed, table)
    half = result.shape[1] // 2
    parts = []
    for index in range(4):
        value = (result[rows * index : rows * (index + 1), :half], result[rows * index : rows * (index + 1), half:])
        if index > 0:
            value = times(lane_twiddle(twiddle, index), value)
        parts.append(value)
    return gather4(parts)


def forward_rows(quarters, table, twiddle):
    lanes = quarters[0][0].shape[1]
    packed = []
    for index, value in enumerate(scatter4(quarters)):
        if index > 0:
            value = conj_times((twiddle[index, 0], twiddle[index, 1]), value)
        packed.append(jnp.concatenate(value, axis=0))
    result = left_dot(table, jnp.concatenate(packed, axis=1))
    half = result.shape[0] // 2
    return [
        (result[:half, lanes * index : lanes * (index + 1)], result[half:, lanes * index : lanes * (index + 1)])
        for index in range(4)
    ]


def inverse_rows(classes, table, twiddle):
    lanes = classes[0][0].shape[1]
    packed = jnp.concatenate([jnp.concatenate(value, axis=0) for value in classes], axis=1)
    result = left_dot(table, packed)
    half = result.shape[0] // 2
    parts = []
    for index in range(4):
        value = (result[:half, lanes * index : lanes * (index + 1)], result[half:, lanes * index : lanes * (index + 1)])
        if index > 0:
            value = times((twiddle[index, 0], twiddle[index, 1]), value)
        parts.append(value)
    return gather4(parts)


def joined(parts, axis):
    return parts[0] if len(parts) == 1 else jnp.concatenate(parts, axis=axis)


class Plan:
    def __init__(self, number, sections, cores, own_probes, spans, breadth):
        assert own_probes == sections and spans > 1
        self.number, self.sections, self.cores = number, sections, cores
        self.own_probes, self.spans, self.breadth = own_probes, spans, breadth
        self.stride = number // sections
        assert self.stride >= cores
        self.top = (number - cores) // 2
        self.total = cores * own_probes

    def home(self, q):
        return self.top + q // self.sections, q % self.sections

    def base(self, q):
        z, x = self.home(q)
        return (z + self.stride * x) % self.number

    def own_base(self, info):
        return lax.rem(info[1] + self.stride * info[2], self.number)

    def served(self, info, j):
        step = lax.rem(info[1] - j - self.top + 2 * self.number, self.number)
        return jnp.minimum(lax.rem(step, self.stride), self.cores - 1), lax.div(step, self.stride)

    def offsets(self, info, j):
        batch, probe = self.served(info, j)
        spot = 3 + probe + jnp.where(batch == info[0], 0, 2 * self.own_probes)
        return info[spot], info[spot + self.own_probes]

    def blocks(self, info, j):
        column = self.offsets(info, j)[1]
        near = lax.div(column, self.breadth)
        far = jnp.where(near + 1 < self.spans, near + 1, near - 1)
        return near, far, lax.rem(column, self.breadth)


def prepare_kernel(info, phase, measured, phase_piece, own_pieces, other_pieces, scratch):
    rows = phase.shape[0] // 4
    width = scratch.shape[2]
    tasks = [(phase, (phase_piece,))]
    for probe in range(measured.shape[1]):
        tasks.append((measured.at[0, probe], (own_pieces.at[probe], other_pieces.at[probe])))
    for source, targets in tasks:
        for tile in range(phase.shape[1] // width):
            columns = slice(width * tile, width * (tile + 1))
            scratch[tile] = source[:, columns]
            for index in range(2):
                part = slice(rows * index, rows * (index + 1))
                for flip, target in enumerate(targets):
                    low = scratch[tile, pl.ds(2 * flip + index, rows, stride=4), :]
                    high = scratch[tile, pl.ds(2 - 2 * flip + index, rows, stride=4), :]
                    target[part, columns] = jnp.where(info[0] == 0, low, high)


def exact_turn(value):
    length = value.shape[1]
    quarter = length // 4
    row = lax.broadcasted_iota(jnp.int32, (length, length), 0)
    column = lax.broadcasted_iota(jnp.int32, (length, length), 1)
    wanted = 4 * lax.rem(row, quarter) + lax.div(row, quarter)
    order = (wanted == column).astype(jnp.float32).astype(jnp.bfloat16)
    first = value.astype(jnp.bfloat16)
    rest = value - first.astype(jnp.float32)
    second = rest.astype(jnp.bfloat16)
    third = (rest - second.astype(jnp.float32)).astype(jnp.bfloat16)
    dims = (((1,), (1,)), ((), ()))
    parts = [
        lax.dot_general(order, item, dims, preferred_element_type=jnp.float32) for item in (first, second, third)
    ]
    return (parts[0] + parts[1]) + parts[2]


def class_rows(pieces, index):
    rows = pieces[0].shape[0] // 2
    return joined([piece[rows * index : rows * (index + 1), :] for piece in pieces], 0)


def polynomial(coefficients, value):
    result = jnp.full_like(value, coefficients[-1])
    for item in coefficients[-2::-1]:
        result = result * value + item
    return result


def filter_kernel(plan, info, *refs):
    pieces, field = refs[:-1], refs[-1]
    cosine, sine = circle_polynomials(3.1416)
    quarter = field.shape[2] // 2
    shift = plan.own_base(info) * (pieces[0].shape[1] // 2)
    for index in range(2):
        columns = slice(quarter * index, quarter * (index + 1))
        phase = pltpu.roll(exact_turn(class_rows([piece.at[2] for piece in pieces], index)), shift, 1)
        square = phase * phase
        field[0, :, columns] = polynomial(cosine, square)
        field[1, :, columns] = polynomial(sine, square) * phase


def target_kernel(plan, info, *refs):
    pieces, target = refs[:-1], refs[-1]
    quarter = target.shape[1] // 2
    rows = pieces[0].shape[1] // 4
    shift = plan.own_base(info) * rows
    for index in range(2):
        columns = slice(quarter * index, quarter * (index + 1))
        first, second = slice(rows * index, rows * (index + 1)), slice(rows * (index + 2), rows * (index + 3))
        lines = [jnp.concatenate([piece[2, first], piece[2, second]], axis=1) for piece in pieces]
        target[:, columns] = pltpu.roll(exact_turn(joined(lines, 0)), shift, 1)


def window_delta(info, plan, j, near, far):
    height, breadth = near.shape[2], near.shape[3]
    offset_y = plan.offsets(info, j)[0]
    column = plan.blocks(info, j)[2]
    lane = lax.broadcasted_iota(jnp.int32, (height, breadth), 1)
    line = lax.broadcasted_iota(jnp.int32, (height, breadth), 0)
    vacuum = (line < offset_y) & (info[1] == 0)
    use_near = lane >= column
    return [
        jnp.where(vacuum, 0.0, jnp.where(use_near, near[0, part], far[0, part])) for part in range(2)
    ]


def patch_kernel(plan, j, info, near, far, phase_piece, patch, scratch):
    height = near.shape[2]
    real, imag = window_delta(info, plan, j, near, far)
    scratch[0] = real + 1.0
    scratch[1] = imag
    first = pl.multiple_of(info[0] * (height // 2), height // 2)
    patch[:2] = scratch[:, pl.ds(first, height // 2), :]
    patch[2] = phase_piece[...]


def launch_kernel(
    plan, j, info, near, far, above, above_other, probe, own_piece, other_piece, table, twiddle, message, rolled
):
    height, breadth = near.shape[2], near.shape[3]
    quarter = breadth // 4
    real, imag = window_delta(info, plan, j, near, far)
    transmit = (real + 1.0, imag)
    offset_y = plan.offsets(info, j)[0]
    column = plan.blocks(info, j)[2]
    lower = info[0] == 0
    entering = []
    for part in range(2):
        first, second = above[part], above_other[part]
        pieces = [jnp.where(lower, first, second), jnp.where(lower, second, first), probe[part]]
        lines = pltpu.roll(jnp.concatenate(pieces, axis=0), offset_y, 0)[height:]
        entering.append(pltpu.roll(lines, column, 1))
        rolled[part] = entering[part]
    value = times(entering, transmit)
    quarters = [tuple(item[:, quarter * m : quarter * (m + 1)] for item in value) for m in range(4)]
    classes = scatter4(quarters)
    packed = []
    for index in range(2):
        chosen = tuple(jnp.where(lower, classes[index][i], classes[index + 2][i]) for i in range(2))
        low, high = lane_twiddle(twiddle, index), lane_twiddle(twiddle, index + 2)
        factor = tuple(jnp.where(lower, low[i], high[i]) for i in range(2))
        packed.append(jnp.concatenate(conj_times(factor, chosen), axis=1))
    result = right_dot(jnp.concatenate(packed, axis=0), table)
    for index in range(2):
        block = result[height * index : height * (index + 1)]
        message[0, :, quarter * index : quarter * (index + 1)] = block[:, :quarter]
        message[1, :, quarter * index : quarter * (index + 1)] = block[:, quarter:]
    piece = jnp.where(plan.served(info, j)[0] == info[0], own_piece[0], other_piece[0])
    message[2, : height // 2] = piece[:, : breadth // 2]
    message[2, height // 2 :] = piece[:, breadth // 2 :]


def settle_kernel(plan, info, table, twiddle, *refs):
    number = plan.number
    own_spectra, other_spectra = refs[:number], refs[number : 2 * number]
    own_terms, other_terms = refs[2 * number : 3 * number], refs[3 * number : 4 * number]
    rolled = refs[4 * number : 5 * number]
    out, scratch = refs[5 * number :]
    height, breadth = scratch.shape[1], scratch.shape[2]
    quarter = breadth // 4
    lower = info[0] == 0
    lane = lax.broadcasted_iota(jnp.int32, (height, breadth), 1)
    line = lax.broadcasted_iota(jnp.int32, (height, breadth), 0)
    out[...] = jnp.zeros_like(out)
    for j in range(number):

        @pl.when(info[2] == 0)
        def _():
            classes = []
            for index in range(4):
                first = quarter * (index % 2)
                pair = []
                for part in range(2):
                    own = own_spectra[j][part, :, first : first + quarter]
                    other = other_spectra[j][part, :, first : first + quarter]
                    pair.append(jnp.where(lower, own, other) if index < 2 else jnp.where(lower, other, own))
                classes.append(tuple(pair))
            inner = inverse_lanes(classes, table, twiddle)
            for m in range(4):
                columns = slice(quarter * m, quarter * (m + 1))
                entering = (rolled[j][0, :, columns], rolled[j][1, :, columns])
                term = conj_times(entering, inner[m])
                scratch[0, :, columns] = term[0]
                scratch[1, :, columns] = term[1]

        @pl.when(info[2] != 0)
        def _():
            own, other = own_terms[j][...], other_terms[j][...]
            scratch[:, : height // 2, :] = jnp.where(lower, own, other)
            scratch[:, height // 2 :, :] = jnp.where(lower, other, own)

        near_block, far_block, column = plan.blocks(info, j)
        present = (line >= plan.offsets(info, j)[0]) | (info[1] != 0)
        near = pl.ds(pl.multiple_of(near_block * breadth, breadth), breadth)
        far = pl.ds(pl.multiple_of(far_block * breadth, breadth), breadth)
        use_near = lane >= column
        for part in range(2):
            term = jnp.where(present, scratch[part], 0.0)
            out[0, part, :, near] += jnp.where(use_near, term, 0.0)
            out[0, part, :, far] += jnp.where(use_near, 0.0, term)


def split_lines(value, lower, count):
    height = value.shape[0] // count
    firsts, seconds = [], []
    for index in range(count):
        first = value[height * index : height * index + height // 2]
        second = value[height * index + height // 2 : height * (index + 1)]
        firsts.append(jnp.where(lower, first, second))
        seconds.append(jnp.where(lower, second, first))
    return joined(firsts, 0), joined(seconds, 0)


def merge_lines(own, other, lower, count):
    height = own.shape[0] // count
    parts = []
    for index in range(count):
        first = own[height * index : height * (index + 1)]
        second = other[height * index : height * (index + 1)]
        parts.append(jnp.where(lower, first, second))
        parts.append(jnp.where(lower, second, first))
    return jnp.concatenate(parts, axis=0)


def tiles(width):
    quarter = width // 2
    return [slice(quarter * index, quarter * (index + 1)) for index in range(2)]


def merged_quarters(own, other, lower, count, columns):
    lines = own.shape[1] // 4
    quarters = []
    for m in range(4):
        rows = slice(lines * m, lines * (m + 1))
        quarters.append(
            tuple(merge_lines(own[part, rows, columns], other[part, rows, columns], lower, count) for part in range(2))
        )
    return quarters


def hand_over(quarters, lower, count, columns, keep, send):
    lines = keep.shape[1] // 4
    for m in range(4):
        rows = slice(lines * m, lines * (m + 1))
        for part in range(2):
            keep[part, rows, columns], send[part, rows, columns] = split_lines(quarters[m][part], lower, count)


def filtered(classes, field, conjugate, columns):
    quarter = classes[0][0].shape[0]
    result = []
    for index in range(4):
        rows = slice(quarter * index, quarter * (index + 1))
        factor = (field[0, rows, columns], field[1, rows, columns])
        result.append((conj_times if conjugate else times)(factor, classes[index]))
    return result


def enter_kernel(number, info, forward, inverse, twiddle, field, *refs):
    blocks, (keep, send) = refs[:number], refs[number:]
    lower = info[0] == 0
    count = number // 4
    for columns in tiles(keep.shape[2]):
        quarters = [
            tuple(
                joined([blocks[count * m + i][part, :, columns] for i in range(count)], 0) for part in range(2)
            )
            for m in range(4)
        ]
        far = filtered(forward_rows(quarters, forward, twiddle), field, False, columns)
        hand_over(inverse_rows(far, inverse, twiddle), lower, count, columns, keep, send)


def through_kernel(number, conjugate, info, forward, inverse, twiddle, field, own, other, keep, send):
    lower = info[0] == 0
    count = number // 4
    for columns in tiles(keep.shape[2]):
        far = forward_rows(merged_quarters(own, other, lower, count, columns), forward, twiddle)
        far = filtered(far, field, conjugate, columns)
        hand_over(inverse_rows(far, inverse, twiddle), lower, count, columns, keep, send)


def residual_kernel(number, info, forward, inverse, twiddle, target, own, other, keep, send):
    lower = info[0] == 0
    count = number // 4
    for columns in tiles(keep.shape[2]):
        far = forward_rows(merged_quarters(own, other, lower, count, columns), forward, twiddle)
        quarter = far[0][0].shape[0]
        seeded = []
        for index in range(4):
            real, imag = far[index]
            residual = real * real + imag * imag - target[quarter * index : quarter * (index + 1), columns]
            seeded.append((residual * real, residual * imag))
        hand_over(inverse_rows(seeded, inverse, twiddle), lower, count, columns, keep, send)


def leave_kernel(number, info, forward, inverse, twiddle, field, own, other, *blocks):
    lower = info[0] == 0
    count = number // 4
    height = blocks[0].shape[1]
    for columns in tiles(own.shape[2]):
        far = forward_rows(merged_quarters(own, other, lower, count, columns), forward, twiddle)
        quarters = inverse_rows(filtered(far, field, True, columns), inverse, twiddle)
        for m in range(4):
            for i in range(count):
                for part in range(2):
                    blocks[count * m + i][part, :, columns] = quarters[m][part][height * i : height * (i + 1)]


def lane_classes(own, other, lower, rows):
    quarter = own.shape[2] // 2
    classes = []
    for index in range(4):
        columns = slice(quarter * (index % 2), quarter * (index % 2) + quarter)
        pair = []
        for part in range(2):
            first, second = own[part, rows, columns], other[part, rows, columns]
            pair.append(jnp.where(lower, first, second) if index < 2 else jnp.where(lower, second, first))
        classes.append(tuple(pair))
    return classes


def lanes_out(classes, lower, rows, keep, send):
    quarter = keep.shape[2] // 2
    for index in range(2):
        columns = slice(quarter * index, quarter * (index + 1))
        for part in range(2):
            low, high = classes[index][part], classes[index + 2][part]
            keep[part, rows, columns] = jnp.where(lower, low, high)
            send[part, rows, columns] = jnp.where(lower, high, low)


def meet_kernel(plan, info, forward, inverse, twiddle, own, other, *refs):
    number = plan.number
    patches, (entering, keep, send) = refs[:number], refs[number:]
    lower = info[0] == 0
    count = number // 4
    lines = own.shape[1] // 4
    quarter = own.shape[2] // 2
    for m in range(4):
        rows = slice(lines * m, lines * (m + 1))
        group = patches[count * m : count * (m + 1)]
        wave = inverse_lanes(lane_classes(own, other, lower, rows), inverse, twiddle)
        quarters = []
        for piece in range(4):
            columns = slice(quarter * piece, quarter * (piece + 1))
            transmit = tuple(joined([patch[part, :, columns] for patch in group], 0) for part in range(2))
            entering[0, rows, columns] = wave[piece][0]
            entering[1, rows, columns] = wave[piece][1]
            quarters.append(times(wave[piece], transmit))
        lanes_out(forward_lanes(quarters, forward, twiddle), lower, rows, keep, send)


def grade_kernel(plan, info, forward, inverse, twiddle, own, other, entering, *refs):
    number = plan.number
    patches, terms, (keep, send) = refs[:number], refs[number : 2 * number], refs[2 * number :]
    lower = info[0] == 0
    count = number // 4
    lines = own.shape[1] // 4
    height = lines // count
    quarter = own.shape[2] // 2
    for m in range(4):
        rows = slice(lines * m, lines * (m + 1))
        group = patches[count * m : count * (m + 1)]
        inner = inverse_lanes(lane_classes(own, other, lower, rows), inverse, twiddle)
        quarters = []
        for piece in range(4):
            columns = slice(quarter * piece, quarter * (piece + 1))
            transmit = tuple(joined([patch[part, :, columns] for patch in group], 0) for part in range(2))
            wave = (entering[0, rows, columns], entering[1, rows, columns])
            term = conj_times(wave, inner[piece])
            for i in range(count):
                for part in range(2):
                    terms[count * m + i][part, :, columns] = term[part][height * i : height * (i + 1)]
            quarters.append(conj_times(transmit, inner[piece]))
        lanes_out(forward_lanes(quarters, forward, twiddle), lower, rows, keep, send)


def after(value, *others):
    return lax.optimization_barrier((value, *others))[0]


def on_device(probe, object_delta, measured, pos_y, pos_x, prop_phase):
    number = lax.axis_size("row")
    sections = lax.axis_size("sect")
    cores = lax.axis_size("batch")
    place, section, core = (lax.axis_index(axis) for axis in line_axes)
    height, breadth = probe.shape[1], probe.shape[2]
    spans = object_delta.shape[3] // breadth
    half, wide = height // 2, breadth // 2
    plan = Plan(number, sections, cores, measured.shape[1], spans, breadth)
    total = plan.total
    home_z = [plan.home(q)[0] for q in range(total)]
    home_x = [plan.home(q)[1] for q in range(total)]
    base = [plan.base(q) for q in range(total)]
    assert len(set(base)) == total

    def spot(z, x, c):
        return (z * sections + x) * cores + c

    every = [(q, c) for q in range(total) for c in range(cores)]

    def inward(j, layer):
        return [
            (spot((base[q] + j) % number, layer, c), spot(home_z[q], home_x[q], c)) for q, c in every
        ]

    def outward(j, layer):
        return [(target, source) for source, target in inward(j, layer)]

    def move(value, pairs):
        return lax.ppermute(value, line_axes, pairs)

    def swap(value):
        return lax.ppermute(value, "batch", [(i, (i + 1) % cores) for i in range(cores)])

    column_forward, column_inverse = (jnp.asarray(table) for table in column_tables(breadth))
    row_forward, row_inverse = (jnp.asarray(table) for table in row_tables(breadth))
    lane_factors, line_factors = (jnp.asarray(table) for table in twiddles(breadth))

    params = pltpu.CompilerParams(vmem_limit_bytes=vmem_bytes)
    part = jnp.where(core == 0, probe[:, :half], probe[:, half:])
    above = lax.ppermute(part, "row", [(i, (i + 1) % number) for i in range(number)])
    def beside(*vectors):
        sizes = [value.shape[0] for value in vectors]
        return sum(
            jnp.pad(value, (sum(sizes[:i]), sum(sizes[i + 1 :]))) for i, value in enumerate(vectors)
        ).astype(jnp.int32)

    own_positions = beside(pos_y[0], pos_x[0])
    about = jnp.stack([core, place, section]).astype(jnp.int32)
    info = beside(about, own_positions, swap(own_positions))

    def whole(shape):
        return pl.BlockSpec(tuple(shape), lambda i, *_: (0,) * len(shape))

    def floats(*shape):
        return jax.ShapeDtypeStruct(shape, jnp.float32)

    pieces_shape = (plan.own_probes, half, breadth)
    phase_piece, own_pieces, other_pieces = pl.pallas_call(
        prepare_kernel,
        out_shape=[floats(half, breadth), floats(*pieces_shape), floats(*pieces_shape)],
        grid_spec=pltpu.PrefetchScalarGridSpec(
            num_scalar_prefetch=1,
            grid=(1,),
            in_specs=[
                whole(prop_phase.shape),
                whole(measured.shape),
            ],
            out_specs=[whole((half, breadth)), whole(pieces_shape), whole(pieces_shape)],
            scratch_shapes=[pltpu.VMEM((breadth // 128, height, 128), jnp.float32)],
        ),
        cost_estimate=light,
            compiler_params=params,
    )(after(about, part), prop_phase, measured)
    other_pieces = swap(other_pieces)

    def near_spec(j, far):
        return pl.BlockSpec(
            (1, 2, height, breadth), lambda i, info: (0, 0, 0, plan.blocks(info, j)[1 if far else 0])
        )

    def patch_of(j, info):
        return pl.pallas_call(
            functools.partial(patch_kernel, plan, j),
            out_shape=floats(3, half, breadth),
            grid_spec=pltpu.PrefetchScalarGridSpec(
                num_scalar_prefetch=1,
                grid=(1,),
                in_specs=[near_spec(j, False), near_spec(j, True), whole(phase_piece.shape)],
                out_specs=whole((3, half, breadth)),
                scratch_shapes=[pltpu.VMEM((2, height, breadth), jnp.float32)],
            ),
            cost_estimate=light,
            compiler_params=params,
        )(info, object_delta, object_delta, phase_piece)

    def launch_of(j, info):
        piece_spec = pl.BlockSpec((1, half, breadth), lambda i, info: (plan.served(info, j)[1], 0, 0))
        return pl.pallas_call(
            functools.partial(launch_kernel, plan, j),
            out_shape=[floats(3, height, wide), floats(2, height, breadth)],
            grid_spec=pltpu.PrefetchScalarGridSpec(
                num_scalar_prefetch=1,
                grid=(1,),
                in_specs=[
                    near_spec(j, False),
                    near_spec(j, True),
                    whole(above.shape),
                    whole(above.shape),
                    whole(probe.shape),
                    piece_spec,
                    piece_spec,
                    whole(row_forward.shape),
                    whole(lane_factors.shape),
                ],
                out_specs=[whole((3, height, wide)), whole((2, height, breadth))],
            ),
            cost_estimate=light,
            compiler_params=params,
        )(
            info,
            object_delta,
            object_delta,
            above,
            above_other,
            probe,
            own_pieces,
            other_pieces,
            row_forward,
            lane_factors,
        )

    later = range(1, sections)
    own_patches = [patch_of(j, info) for j in range(number)]
    patches = {layer: [] for layer in later}
    above_other = swap(after(above, *own_patches))
    launched, blocks = [], []
    for j in range(number):
        value = own_patches[j]
        if j >= 2:
            value = after(value, *(patches[layer][j - 2] for layer in later))
        for layer in later:
            patches[layer].append(move(value, inward(j, layer)))
        launched.append(launch_of(j, info if j == 0 else after(info, launched[j - 1][0])))
        message = launched[j][0]
        if j >= 2:
            message = after(message, blocks[j - 2])
        blocks.append(move(message, inward(j, 0)))
    rolled = [item[1] for item in launched]
    blocks = lax.optimization_barrier((*blocks, *(patches[layer][j] for layer in later for j in range(number))))[:number]

    traded = (2, wide, wide)
    column_set = (column_forward, column_inverse, line_factors)
    row_set = (row_forward, row_inverse, lane_factors)

    def at_home(kernel, outs, *operands):
        return pl.pallas_call(
            kernel,
            out_shape=[floats(*shape) for shape in outs],
            in_specs=[pl.BlockSpec(memory_space=smem)] + [pl.BlockSpec(memory_space=pltpu.VMEM)] * len(operands),
            out_specs=[pl.BlockSpec(memory_space=pltpu.VMEM)] * len(outs),
            cost_estimate=light,
            compiler_params=params,
        )(about, *operands)

    def through(conjugate, own, other):
        kernel = functools.partial(through_kernel, number, conjugate)
        return at_home(kernel, [traded, traded], *column_set, field, own, other)

    entries = {}
    field = at_home(
        functools.partial(filter_kernel, plan), [(2, breadth, wide)], after(patches[1][0], launched[-1][0]), *patches[1][1:]
    )[0]
    keep, send = at_home(
        functools.partial(enter_kernel, number), [traded, traded], *column_set, field, *blocks
    )
    target = at_home(functools.partial(target_kernel, plan), [(breadth, wide)], *blocks)[0]
    for layer in later:
        other = swap(send)
        entries[layer], keep, send = at_home(
            functools.partial(meet_kernel, plan),
            [(2, wide, breadth), traded, traded],
            *row_set,
            keep,
            after(other, target) if layer == 1 else other,
            *patches[layer],
        )
        other = swap(send)
        if layer < sections - 1:
            keep, send = through(False, keep, other)
    keep, send = at_home(
        functools.partial(residual_kernel, number), [traded, traded], *column_set, target, keep, other
    )

    terms = None
    for layer in reversed(later):
        other = swap(send)
        found = at_home(
            functools.partial(grade_kernel, plan),
            [(2, half, breadth)] * number + [traded, traded],
            *row_set,
            keep,
            other,
            entries[layer],
            *patches[layer],
        )
        keep, send = found[number:]
        other = swap(send)
        if layer > 1:
            came = [move(after(found[j], other), outward(j, layer)) for j in range(number)]
            terms = came if terms is None else [first + second for first, second in zip(terms, came)]
            keep, send = through(True, keep, other)
    leaving = at_home(
        functools.partial(leave_kernel, number), [(2, height, wide)] * number, *column_set, field, keep, other
    )
    came = [move(after(found[j], other if j < 2 else leaving[0]), outward(j, 1)) for j in range(number)]
    spectra = [move(leaving[j], outward(j, 0)) for j in range(number)]
    terms = came if terms is None else [first + second for first, second in zip(terms, came)]

    operands = [
        row_inverse,
        lane_factors,
        *spectra,
        *(swap(value) for value in spectra),
        *terms,
        *(swap(value) for value in terms),
        *rolled,
    ]
    return pl.pallas_call(
        functools.partial(settle_kernel, plan),
        out_shape=jax.ShapeDtypeStruct(object_delta.shape, jnp.float32),
        in_specs=[pl.BlockSpec(memory_space=smem)] + [pl.BlockSpec(memory_space=pltpu.VMEM)] * len(operands),
        out_specs=pl.BlockSpec(memory_space=pltpu.VMEM),
        scratch_shapes=[pltpu.VMEM((2, height, breadth), jnp.float32)],
        cost_estimate=light,
        compiler_params=params,
    )(info, *operands)


def solution(mesh):
    in_specs = (
        P(None, "row", None),
        P(("groups", "sect"), None, "row", None),
        P(("groups", "batch"), None, "row", None),
        P(("groups", "batch"), None),
        P(("groups", "batch"), None),
        P("row", None),
    )
    out_specs = P(("groups", "sect"), None, "row", None)
    return jax.shard_map(
        on_device, mesh=mesh, in_specs=in_specs, out_specs=out_specs, check_vma=False
    )
```

time: 185 us -> 123 us (0.66)
  starting transfers between devices: 69.9 us -> 36 us
  between operations: 18.6 us -> 0.43 us
  waiting for transfers between devices: 37.7 us -> 52.5 us
  local copies, waits for them, and re-layouts: 15.1 us -> 3.63 us
  matrix products: 5.43 us -> 0 us
  other arithmetic: 6.94 us -> 1.96 us
    ppermute x24 -> x16, starting transfers between devices: 63.6 us -> 29.9 us  [move(): return lax.ppermute(value, line_axes, pairs)]
    ppermute x24 -> x16, waiting for transfers between devices: 34.4 us -> 45.2 us  [move(): return lax.ppermute(value, line_axes, pairs)]
    another operation x4 -> x0, local copies, waits for them, and re-layouts: 5.55 us -> none  [on_device(): jnp.stack([core, (place == 0).astype(jnp.int32), block, jnp.minimum(block...]
    dot_general x6 -> x0, matrix products: 5.43 us -> none  [the longest x3 3.32 us: classed(): jnp.einsum('au,quv->qav', class_rows(which_core), planes, precision=highest)]
    ppermute x15, waiting for transfers between devices: 3.31 us -> 7.27 us  [swap(): lax.ppermute(value, 'batch', [(i, (i + 1) % cores) for i in range(cores)])]
    cos x1 -> x0, other arithmetic: 3.56 us -> none  [on_device(): filter_field = jnp.stack([jnp.cos(phase), jnp.sin(phase)])]
    dynamic_slice x4 -> x0, local copies, waits for them, and re-layouts: 3.46 us -> none  [the longest x1 1.13 us: on_device(): part = lax.dynamic_slice_in_dim(probe, core * half, half, 1)]
    cos x1 -> x0, local copies, waits for them, and re-layouts: 2.13 us -> none  [on_device(): filter_field = jnp.stack([jnp.cos(phase), jnp.sin(phase)])]
  transfers between devices with their start and end apart: 40 -> 32, of which waited for: 8 -> 16; matrix products, arithmetic and copies ran while one was open for 13% -> 1% of each run, Pallas kernels for 11% -> 12%
where the time goes in v2:
time: 123 us
  waiting for transfers between devices  52.5 us (43%)
  starting transfers between devices  36 us (29%)
  Pallas kernels  28.2 us (23%)
  local copies, waits for them, and re-layouts  3.63 us (3%)
  other arithmetic  1.96 us (2%)
    ppermute x16, waiting for transfers between devices, move(): return lax.ppermute(value, line_axes, pairs)  45.2 us
    ppermute x16, starting transfers between devices, move(): return lax.ppermute(value, line_axes, pairs)  29.9 us
    pallas_call x7, Pallas kernels, at_home(): pl.pallas_call(kernel, out_shape=[floats(*shape) for shape in outs], in_s...  14.9 us
    ppermute x15, waiting for transfers between devices, swap(): lax.ppermute(value, 'batch', [(i, (i + 1) % cores) for i in range(cores)])  7.27 us
    pallas_call x4, Pallas kernels, launch_of(): pl.pallas_call(functools.partial(launch_kernel, plan, j), out_shape=[floa...  5.34 us
    pallas_call x1, Pallas kernels, on_device(): pl.pallas_call(functools.partial(settle_kernel, plan), out_shape=jax.Shap...  4.46 us
    unnamed x18, local copies, waits for them, and re-layouts  3.63 us
    ppermute x1, starting transfers between devices, on_device(): lax.ppermute(part, 'row', [(i, (i + 1) % number) for i in range(number)])  3.08 us
  transfers between devices with their start and end apart: 32, of which 16 were waited for; matrix products, arithmetic and copies ran while one was open for 1% of the time, Pallas kernels for 12%

profile of v2, /device:TPU:0, one launch (start us, length us, event | category | flops | bytes accessed | tf_op | source)
XLA Modules:
  0.0 122.7 jit_solution(1559182944237496231)
XLA Ops:
  0.0 1.1 slice_select_fusion
  1.1 3.1 %collective-permute-start.2 = (f32[2,64,512]{2,1,0:T(8,128)S(1)}, f32[2,64,512]{2,1,0:T(8,128)S(1)}, u32[]{:S(2)}, u32[]{:S(2)}) collective-permute-start(f32[2,64,512]{2,1,0:T(8,128)S(1)} %slice_select_fusion), channel_id=1, source_target_pairs={{0,4},{4,8},{8,12},{12,0},{1,5},{5,9},{9,13},{13,1},{2,6},{6,10},{... | collective-permute-start | bytes 786440 | tf_op jit(solution)/shard_map/ppermute | solution.py:632
  8.3 1.6 %copy-done = f32[1,2,128,2048]{3,2,1,0:T(8,128)S(1)} copy-done((f32[1,2,128,2048]{3,2,1,0:T(8,128)S(1)}, f32[1,2,128,2048]{3,2,1,0:T(8,128)}, u32[]{:S(2)}) %copy-start) | copy-done | bytes 2097176
  14.5 1.3 %shard_map.123 = (f32[3,128,256]{2,1,0:T(8,128)S(1)}, f32[2,128,512]{2,1,0:T(8,128)S(1)}) custom-call(s32[11]{0:T(128)S(1)} %pad_add_fusion.1.info, f32[1,2,128,2048]{3,2,1,0:T(8,128)S(1)} %copy-done.1, f32[1,2,128,2048]{3,2,1,0:T(8,128)S(1)} %copy-done.1, f32[2,64,512]{2,1,0:T(8,128)S(1)} %collective-permute-done.2.above, ...), custom_call_target="tpu_custom_call" | custom-call | tf_op jit(solution)/shard_map/pallas_call | solution.py:690
  15.8 8.4 %collective-permute-start.8 = (f32[3,128,256]{2,1,0:T(8,128)S(1)}, f32[3,128,256]{2,1,0:T(8,128)S(1)}, u32[]{:S(2)}, u32[]{:S(2)}) collective-permute-start(f32[3,128,256]{2,1,0:T(8,128)S(1)} %get-tuple-element.57), channel_id=1, source_target_pairs={{4,4},{5,5},{12,6},{13,7},{8,8},{9,9},{0,10},{1,11},{20,20},{21,21... | collective-permute-start | bytes 1179656 | tf_op jit(solution)/shard_map/ppermute | solution.py:621
  24.2 1.3 %shard_map.124 = (f32[3,128,256]{2,1,0:T(8,128)S(1)}, f32[2,128,512]{2,1,0:T(8,128)S(1)}) custom-call(s32[11]{0:T(128)S(1)} %pad_add_fusion.1.info, f32[1,2,128,2048]{3,2,1,0:T(8,128)S(1)} %copy-done.1, f32[1,2,128,2048]{3,2,1,0:T(8,128)S(1)} %copy-done.1, f32[2,64,512]{2,1,0:T(8,128)S(1)} %collective-permute-done.2.above, ...), custom_call_target="tpu_custom_call" | custom-call | tf_op jit(solution)/shard_map/pallas_call | solution.py:690
  25.6 1.8 %collective-permute-start.9 = (f32[3,128,256]{2,1,0:T(8,128)S(1)}, f32[3,128,256]{2,1,0:T(8,128)S(1)}, u32[]{:S(2)}, u32[]{:S(2)}) collective-permute-start(f32[3,128,256]{2,1,0:T(8,128)S(1)} %get-tuple-element.59), channel_id=1, source_target_pairs={{8,4},{9,5},{0,6},{1,7},{12,8},{13,9},{4,10},{5,11},{24,20},{25,21... | collective-permute-start | bytes 1179656 | tf_op jit(solution)/shard_map/ppermute | solution.py:621
  28.8 1.3 %shard_map.125 = (f32[3,128,256]{2,1,0:T(8,128)S(1)}, f32[2,128,512]{2,1,0:T(8,128)S(1)}) custom-call(s32[11]{0:T(128)S(1)} %pad_add_fusion.1.info, f32[1,2,128,2048]{3,2,1,0:T(8,128)S(1)} %copy-done.1, f32[1,2,128,2048]{3,2,1,0:T(8,128)S(1)} %copy-done.1, f32[2,64,512]{2,1,0:T(8,128)S(1)} %collective-permute-done.2.above, ...), custom_call_target="tpu_custom_call" | custom-call | tf_op jit(solution)/shard_map/pallas_call | solution.py:690
  30.2 1.3 %shard_map.126 = (f32[3,128,256]{2,1,0:T(8,128)S(1)}, f32[2,128,512]{2,1,0:T(8,128)S(1)}) custom-call(s32[11]{0:T(128)S(1)} %pad_add_fusion.1.info, f32[1,2,128,2048]{3,2,1,0:T(8,128)S(1)} %copy-done.1, f32[1,2,128,2048]{3,2,1,0:T(8,128)S(1)} %copy-done.1, f32[2,64,512]{2,1,0:T(8,128)S(1)} %collective-permute-done.2.above, ...), custom_call_target="tpu_custom_call" | custom-call | tf_op jit(solution)/shard_map/pallas_call | solution.py:690
  31.6 2.2 %collective-permute-done.8.refs_0_ = f32[3,128,256]{2,1,0:T(8,128)S(1)} collective-permute-done((f32[3,128,256]{2,1,0:T(8,128)S(1)}, f32[3,128,256]{2,1,0:T(8,128)S(1)}, u32[]{:S(2)}, u32[]{:S(2)}) %collective-permute-start.8) | collective-permute-done | bytes 393248 | tf_op jit(solution)/shard_map/ppermute | solution.py:621
  33.7 8.7 %collective-permute-done.9.refs_1_ = f32[3,128,256]{2,1,0:T(8,128)S(1)} collective-permute-done((f32[3,128,256]{2,1,0:T(8,128)S(1)}, f32[3,128,256]{2,1,0:T(8,128)S(1)}, u32[]{:S(2)}, u32[]{:S(2)}) %collective-permute-start.9) | collective-permute-done | bytes 393248 | tf_op jit(solution)/shard_map/ppermute | solution.py:621
  42.5 2.3 %collective-permute-start.11 = (f32[3,128,256]{2,1,0:T(8,128)S(1)}, f32[3,128,256]{2,1,0:T(8,128)S(1)}, u32[]{:S(2)}, u32[]{:S(2)}) collective-permute-start(f32[3,128,256]{2,1,0:T(8,128)S(1)} %get-tuple-element.68), channel_id=1, source_target_pairs={{0,4},{1,5},{8,6},{9,7},{4,8},{5,9},{12,10},{13,11},{16,20},{17,21... | collective-permute-start | bytes 1179656 | tf_op jit(solution)/shard_map/ppermute | solution.py:621
  44.8 6.6 %collective-permute-start.10 = (f32[3,128,256]{2,1,0:T(8,128)S(1)}, f32[3,128,256]{2,1,0:T(8,128)S(1)}, u32[]{:S(2)}, u32[]{:S(2)}) collective-permute-start(f32[3,128,256]{2,1,0:T(8,128)S(1)} %get-tuple-element.67), channel_id=1, source_target_pairs={{12,4},{13,5},{4,6},{5,7},{0,8},{1,9},{8,10},{9,11},{28,20},{29,21... | collective-permute-start | bytes 1179656 | tf_op jit(solution)/shard_map/ppermute | solution.py:621
  51.4 2.1 %shard_map.127.field = f32[2,512,256]{2,1,0:T(8,128)S(1)} custom-call(s32[3]{0:T(128)S(1)} %pad_add_fusion.info, f32[3,64,512]{2,1,0:T(8,128)S(1)} %collective-permute-done.1.refs_0_, f32[3,64,512]{2,1,0:T(8,128)S(1)} %collective-permute-done.5.refs_1_, f32[3,64,512]{2,1,0:T(8,128)S(1)} %collective-permute-done.6.refs_2_, ...), custom_call_target="tpu_custom_call" | custom-call | tf_op jit(solution)/shard_map/pallas_call | solution.py:748
  54.2 7.5 %collective-permute-done.10.refs_2_ = f32[3,128,256]{2,1,0:T(8,128)S(1)} collective-permute-done((f32[3,128,256]{2,1,0:T(8,128)S(1)}, f32[3,128,256]{2,1,0:T(8,128)S(1)}, u32[]{:S(2)}, u32[]{:S(2)}) %collective-permute-start.10) | collective-permute-done | bytes 393248 | tf_op jit(solution)/shard_map/ppermute | solution.py:621
  61.8 2.3 %shard_map.129 = (f32[2,256,256]{2,1,0:T(8,128)S(1)}, f32[2,256,256]{2,1,0:T(8,128)S(1)}) custom-call(s32[3]{0:T(128)S(1)} %pad_add_fusion.info, bf16[2,256,256]{2,1,0:T(8,128)(2,1)S(1)} %copy-done.4, bf16[2,256,256]{2,1,0:T(8,128)(2,1)S(1)} %copy-done.2, f32[4,2,128,128]{3,2,1,0:T(8,128)S(1)} %copy-done.5, f32[2,512,256]{2,1,0:T(8,128)S(1)} %shard_map.127.field, ...), custom_call_target="tpu_custom_call" | custom-call | tf_op jit(solution)/shard_map/pallas_call | solution.py:748
  64.2 1.6 %shard_map.128.target = f32[512,256]{1,0:T(8,128)S(1)} custom-call(s32[3]{0:T(128)S(1)} %pad_add_fusion.info, f32[3,128,256]{2,1,0:T(8,128)S(1)} %collective-permute-done.8.refs_0_, f32[3,128,256]{2,1,0:T(8,128)S(1)} %collective-permute-done.9.refs_1_, f32[3,128,256]{2,1,0:T(8,128)S(1)} %collective-permute-done.10.refs_2_, ...), custom_call_target="tpu_custom_call" | custom-call | tf_op jit(solution)/shard_map/pallas_call | solution.py:748
  66.0 2.0 %shard_map.130 = (f32[2,256,512]{2,1,0:T(8,128)S(1)}, f32[2,256,256]{2,1,0:T(8,128)S(1)}, f32[2,256,256]{2,1,0:T(8,128)S(1)}) custom-call(s32[3]{0:T(128)S(1)} %pad_add_fusion.info, bf16[2,256,256]{2,1,0:T(8,128)(2,1)S(1)} %copy-done.2, bf16[2,256,256]{2,1,0:T(8,128)(2,1)S(1)} %copy-done.4, f32[8,128]{1,0:T(8,128)S(1)} %copy-done.8, ...), custom_call_target="tpu_custom_call" | custom-call | tf_op jit(solution)/shard_map/pallas_call | solution.py:748
  68.4 1.7 %collective-permute-done.13.other = f32[2,256,256]{2,1,0:T(8,128)S(1)} collective-permute-done((f32[2,256,256]{2,1,0:T(8,128)S(1)}, f32[2,256,256]{2,1,0:T(8,128)S(1)}, u32[]{:S(2)}, u32[]{:S(2)}) %collective-permute-start.13) | collective-permute-done | bytes 524320 | tf_op jit(solution)/shard_map/ppermute | solution.py:624
  70.1 2.4 %shard_map.131 = (f32[2,256,256]{2,1,0:T(8,128)S(1)}, f32[2,256,256]{2,1,0:T(8,128)S(1)}) custom-call(s32[3]{0:T(128)S(1)} %pad_add_fusion.info, bf16[2,256,256]{2,1,0:T(8,128)(2,1)S(1)} %copy-done.4, bf16[2,256,256]{2,1,0:T(8,128)(2,1)S(1)} %copy-done.2, f32[4,2,128,128]{3,2,1,0:T(8,128)S(1)} %copy-done.5, f32[512,256]{1,0:T(8,128)S(1)} %shard_map.128.target, ...), custom_call_target="tpu_custom_call" | custom-call | tf_op jit(solution)/shard_map/pallas_call | solution.py:748
  72.8 1.7 %collective-permute-done.14.other = f32[2,256,256]{2,1,0:T(8,128)S(1)} collective-permute-done((f32[2,256,256]{2,1,0:T(8,128)S(1)}, f32[2,256,256]{2,1,0:T(8,128)S(1)}, u32[]{:S(2)}, u32[]{:S(2)}) %collective-permute-start.14) | collective-permute-done | bytes 524320 | tf_op jit(solution)/shard_map/ppermute | solution.py:624
  74.5 2.1 %shard_map.132 = (f32[2,64,512]{2,1,0:T(8,128)S(1)}, f32[2,64,512]{2,1,0:T(8,128)S(1)}, f32[2,64,512]{2,1,0:T(8,128)S(1)}, f32[2,64,512]{2,1,0:T(8,128)S(1)}, f3...) custom-call(s32[3]{0:T(128)S(1)} %pad_add_fusion.info, bf16[2,256,256]{2,1,0:T(8,128)(2,1)S(1)} %copy-done.2, ...), custom_call_target="tpu_custom_call" | custom-call | tf_op jit(solution)/shard_map/pallas_call | solution.py:748
  76.9 1.7 %collective-permute-done.15.other = f32[2,256,256]{2,1,0:T(8,128)S(1)} collective-permute-done((f32[2,256,256]{2,1,0:T(8,128)S(1)}, f32[2,256,256]{2,1,0:T(8,128)S(1)}, u32[]{:S(2)}, u32[]{:S(2)}) %collective-permute-start.15) | collective-permute-done | bytes 524320 | tf_op jit(solution)/shard_map/ppermute | solution.py:624
  79.2 2.3 %shard_map.133 = (f32[2,128,256]{2,1,0:T(8,128)S(1)}, f32[2,128,256]{2,1,0:T(8,128)S(1)}, f32[2,128,256]{2,1,0:T(8,128)S(1)}, f32[2,128,256]{2,1,0:T(8,128)S(1)}) custom-call(s32[3]{0:T(128)S(1)} %pad_add_fusion.info, bf16[2,256,256]{2,1,0:T(8,128)(2,1)S(1)} %copy-done.4, bf16[2,256,256]{2,1,0:T(8,128)(2,1)S(1)} %copy-done.2, ...), custom_call_target="tpu_custom_call" | custom-call | tf_op jit(solution)/shard_map/pallas_call | solution.py:748
  83.6 1.3 %collective-permute-start.17 = (f32[2,128,256]{2,1,0:T(8,128)S(1)}, f32[2,128,256]{2,1,0:T(8,128)S(1)}, u32[]{:S(2)}, u32[]{:S(2)}) collective-permute-start(f32[2,128,256]{2,1,0:T(8,128)S(1)} %get-tuple-element.84), channel_id=1, source_target_pairs={{4,8},{5,9},{6,0},{7,1},{8,12},{9,13},{10,4},{11,5},{20,24},{21,25... | collective-permute-start | bytes 786440 | tf_op jit(solution)/shard_map/ppermute | solution.py:621
  84.9 1.3 %collective-permute-start.18 = (f32[2,128,256]{2,1,0:T(8,128)S(1)}, f32[2,128,256]{2,1,0:T(8,128)S(1)}, u32[]{:S(2)}, u32[]{:S(2)}) collective-permute-start(f32[2,128,256]{2,1,0:T(8,128)S(1)} %get-tuple-element.85), channel_id=1, source_target_pairs={{4,12},{5,13},{6,4},{7,5},{8,0},{9,1},{10,8},{11,9},{20,28},{21,29... | collective-permute-start | bytes 786440 | tf_op jit(solution)/shard_map/ppermute | solution.py:621
  86.2 1.3 %collective-permute-start.19 = (f32[2,128,256]{2,1,0:T(8,128)S(1)}, f32[2,128,256]{2,1,0:T(8,128)S(1)}, u32[]{:S(2)}, u32[]{:S(2)}) collective-permute-start(f32[2,128,256]{2,1,0:T(8,128)S(1)} %get-tuple-element.86), channel_id=1, source_target_pairs={{4,0},{5,1},{6,8},{7,9},{8,4},{9,5},{10,12},{11,13},{20,16},{21,17... | collective-permute-start | bytes 786440 | tf_op jit(solution)/shard_map/ppermute | solution.py:621
  87.6 1.3 %collective-permute-start.16 = (f32[2,128,256]{2,1,0:T(8,128)S(1)}, f32[2,128,256]{2,1,0:T(8,128)S(1)}, u32[]{:S(2)}, u32[]{:S(2)}) collective-permute-start(f32[2,128,256]{2,1,0:T(8,128)S(1)} %get-tuple-element.83), channel_id=1, source_target_pairs={{4,4},{5,5},{6,12},{7,13},{8,8},{9,9},{10,0},{11,1},{20,20},{21,21... | collective-permute-start | bytes 786440 | tf_op jit(solution)/shard_map/ppermute | solution.py:621
  89.2 16.1 %collective-permute-done.17.refs_1_ = f32[2,128,256]{2,1,0:T(8,128)S(1)} collective-permute-done((f32[2,128,256]{2,1,0:T(8,128)S(1)}, f32[2,128,256]{2,1,0:T(8,128)S(1)}, u32[]{:S(2)}, u32[]{:S(2)}) %collective-permute-start.17) | collective-permute-done | bytes 262176 | tf_op jit(solution)/shard_map/ppermute | solution.py:621
  105.3 5.1 %collective-permute-done.18.refs_2_ = f32[2,128,256]{2,1,0:T(8,128)S(1)} collective-permute-done((f32[2,128,256]{2,1,0:T(8,128)S(1)}, f32[2,128,256]{2,1,0:T(8,128)S(1)}, u32[]{:S(2)}, u32[]{:S(2)}) %collective-permute-start.18) | collective-permute-done | bytes 262176 | tf_op jit(solution)/shard_map/ppermute | solution.py:621
  110.4 4.8 %collective-permute-done.19.refs_3_ = f32[2,128,256]{2,1,0:T(8,128)S(1)} collective-permute-done((f32[2,128,256]{2,1,0:T(8,128)S(1)}, f32[2,128,256]{2,1,0:T(8,128)S(1)}, u32[]{:S(2)}, u32[]{:S(2)}) %collective-permute-start.19) | collective-permute-done | bytes 262176 | tf_op jit(solution)/shard_map/ppermute | solution.py:621
  118.3 4.5 %shard_map.134 = f32[1,2,128,2048]{3,2,1,0:T(8,128)} custom-call(s32[11]{0:T(128)S(1)} %pad_add_fusion.1.info, bf16[2,256,256]{2,1,0:T(8,128)(2,1)S(1)} %copy-done.4, f32[8,128]{1,0:T(8,128)S(1)} %copy-done.8, f32[2,128,256]{2,1,0:T(8,128)S(1)} %collective-permute-done.16.refs_0_, f32[2,128,256]{2,1,0:T(8,128)S(1)} %collective-permute-done.17.refs_1_, ...), custom_call_target="tpu_custom_call" | custom-call | tf_op jit(solution)/shard_map/pallas_call | solution.py:820
  (71 shorter events, 18.0 us)
Async XLA Ops:
  1.1 11.7 %collective-permute-start.2 = (f32[2,64,512]{2,1,0:T(8,128)S(1)}, f32[2,64,512]{2,1,0:T(8,128)S(1)}, u32[]{:S(2)}, u32[]{:S(2)}) collective-permute-start(f32[2,64,512]{2,1,0:T(8,128)S(1)} %slice_select_fusion), channel_id=1, source_target_pairs={{0,4},{4,8},{8,12},{12,0},{1,5},{5,9},{9,13},{13,1},{2,6},{6,10},{... | collective-permute-start | bytes 786440 | tf_op jit(solution)/shard_map/ppermute | solution.py:632
  4.9 3.3 %collective-permute-start = (s32[4]{0:T(128)S(1)}, s32[4]{0:T(128)S(1)}, u32[]{:S(2)}, u32[]{:S(2)}) collective-permute-start(s32[4]{0:T(128)S(1)} %pad_add_fusion.2), channel_id=1, source_target_pairs={{0,1},{1,0},{2,3},{3,2},{4,5},{5,4},{6,7},{7,6},{8,9},{9,8},{10,11... | collective-permute-start | bytes 56 | tf_op jit(solution)/shard_map/ppermute | solution.py:624
  7.6 6.8 %collective-permute-start.4 = (f32[2,64,512]{2,1,0:T(8,128)S(1)}, f32[2,64,512]{2,1,0:T(8,128)S(1)}, u32[]{:S(2)}, u32[]{:S(2)}) collective-permute-start(f32[2,64,512]{2,1,0:T(8,128)S(1)} %get-tuple-element.56), channel_id=1, source_target_pairs={{0,1},{1,0},{2,3},{3,2},{4,5},{5,4},{6,7},{7,6},{8,9},{9,8},{10,11... | collective-permute-start | bytes 786440 | tf_op jit(solution)/shard_map/ppermute | solution.py:624
  12.8 1.6 %collective-permute-start.3 = (f32[2,64,512]{2,1,0:T(8,128)S(1)}, f32[2,64,512]{2,1,0:T(8,128)S(1)}, u32[]{:S(2)}, u32[]{:S(2)}) collective-permute-start(f32[2,64,512]{2,1,0:T(8,128)S(1)} %collective-permute-done.2.above), channel_id=1, source_target_pairs={{0,1},{1,0},{2,3},{3,2},{4,5},{5,4},{6,7},{7,6},{8,9},{9,8},{10,11... | collective-permute-start | bytes 786440 | tf_op jit(solution)/shard_map/ppermute | solution.py:624
  12.9 14.6 %collective-permute-start.1 = (f32[3,64,512]{2,1,0:T(8,128)S(1)}, f32[3,64,512]{2,1,0:T(8,128)S(1)}, u32[]{:S(2)}, u32[]{:S(2)}) collective-permute-start(f32[3,64,512]{2,1,0:T(8,128)S(1)} %shard_map.119), channel_id=1, source_target_pairs={{6,4},{7,5},{14,6},{15,7},{10,8},{11,9},{2,10},{3,11},{22,20},{23,... | collective-permute-start | bytes 1179656 | tf_op jit(solution)/shard_map/ppermute | solution.py:621
  13.7 14.4 %collective-permute-start.5 = (f32[3,64,512]{2,1,0:T(8,128)S(1)}, f32[3,64,512]{2,1,0:T(8,128)S(1)}, u32[]{:S(2)}, u32[]{:S(2)}) collective-permute-start(f32[3,64,512]{2,1,0:T(8,128)S(1)} %shard_map.120), channel_id=1, source_target_pairs={{10,4},{11,5},{2,6},{3,7},{14,8},{15,9},{6,10},{7,11},{26,20},{27,... | collective-permute-start | bytes 1179656 | tf_op jit(solution)/shard_map/ppermute | solution.py:621
  15.8 17.9 %collective-permute-start.8 = (f32[3,128,256]{2,1,0:T(8,128)S(1)}, f32[3,128,256]{2,1,0:T(8,128)S(1)}, u32[]{:S(2)}, u32[]{:S(2)}) collective-permute-start(f32[3,128,256]{2,1,0:T(8,128)S(1)} %get-tuple-element.57), channel_id=1, source_target_pairs={{4,4},{5,5},{12,6},{13,7},{8,8},{9,9},{0,10},{1,11},{20,20},{21,21... | collective-permute-start | bytes 1179656 | tf_op jit(solution)/shard_map/ppermute | solution.py:621
  25.6 16.9 %collective-permute-start.9 = (f32[3,128,256]{2,1,0:T(8,128)S(1)}, f32[3,128,256]{2,1,0:T(8,128)S(1)}, u32[]{:S(2)}, u32[]{:S(2)}) collective-permute-start(f32[3,128,256]{2,1,0:T(8,128)S(1)} %get-tuple-element.59), channel_id=1, source_target_pairs={{8,4},{9,5},{0,6},{1,7},{12,8},{13,9},{4,10},{5,11},{24,20},{25,21... | collective-permute-start | bytes 1179656 | tf_op jit(solution)/shard_map/ppermute | solution.py:621
  27.4 23.9 %collective-permute-start.6 = (f32[3,64,512]{2,1,0:T(8,128)S(1)}, f32[3,64,512]{2,1,0:T(8,128)S(1)}, u32[]{:S(2)}, u32[]{:S(2)}) collective-permute-start(f32[3,64,512]{2,1,0:T(8,128)S(1)} %shard_map.121), channel_id=1, source_target_pairs={{14,4},{15,5},{6,6},{7,7},{2,8},{3,9},{10,10},{11,11},{30,20},{31,... | collective-permute-start | bytes 1179656 | tf_op jit(solution)/shard_map/ppermute | solution.py:621
  28.1 23.2 %collective-permute-start.7 = (f32[3,64,512]{2,1,0:T(8,128)S(1)}, f32[3,64,512]{2,1,0:T(8,128)S(1)}, u32[]{:S(2)}, u32[]{:S(2)}) collective-permute-start(f32[3,64,512]{2,1,0:T(8,128)S(1)} %shard_map.122), channel_id=1, source_target_pairs={{2,4},{3,5},{10,6},{11,7},{6,8},{7,9},{14,10},{15,11},{18,20},{19,... | collective-permute-start | bytes 1179656 | tf_op jit(solution)/shard_map/ppermute | solution.py:621
  42.5 11.8 %collective-permute-start.11 = (f32[3,128,256]{2,1,0:T(8,128)S(1)}, f32[3,128,256]{2,1,0:T(8,128)S(1)}, u32[]{:S(2)}, u32[]{:S(2)}) collective-permute-start(f32[3,128,256]{2,1,0:T(8,128)S(1)} %get-tuple-element.68), channel_id=1, source_target_pairs={{0,4},{1,5},{8,6},{9,7},{4,8},{5,9},{12,10},{13,11},{16,20},{17,21... | collective-permute-start | bytes 1179656 | tf_op jit(solution)/shard_map/ppermute | solution.py:621
  44.8 17.0 %collective-permute-start.10 = (f32[3,128,256]{2,1,0:T(8,128)S(1)}, f32[3,128,256]{2,1,0:T(8,128)S(1)}, u32[]{:S(2)}, u32[]{:S(2)}) collective-permute-start(f32[3,128,256]{2,1,0:T(8,128)S(1)} %get-tuple-element.67), channel_id=1, source_target_pairs={{12,4},{13,5},{4,6},{5,7},{0,8},{1,9},{8,10},{9,11},{28,20},{29,21... | collective-permute-start | bytes 1179656 | tf_op jit(solution)/shard_map/ppermute | solution.py:621
  64.1 2.0 %collective-permute-start.12 = (f32[2,256,256]{2,1,0:T(8,128)S(1)}, f32[2,256,256]{2,1,0:T(8,128)S(1)}, u32[]{:S(2)}, u32[]{:S(2)}) collective-permute-start(f32[2,256,256]{2,1,0:T(8,128)S(1)} %get-tuple-element.74), channel_id=1, source_target_pairs={{0,1},{1,0},{2,3},{3,2},{4,5},{5,4},{6,7},{7,6},{8,9},{9,8},{10,11... | collective-permute-start | bytes 1572872 | tf_op jit(solution)/shard_map/ppermute | solution.py:624
  68.1 2.0 %collective-permute-start.13 = (f32[2,256,256]{2,1,0:T(8,128)S(1)}, f32[2,256,256]{2,1,0:T(8,128)S(1)}, u32[]{:S(2)}, u32[]{:S(2)}) collective-permute-start(f32[2,256,256]{2,1,0:T(8,128)S(1)} %get-tuple-element.77), channel_id=1, source_target_pairs={{0,1},{1,0},{2,3},{3,2},{4,5},{5,4},{6,7},{7,6},{8,9},{9,8},{10,11... | collective-permute-start | bytes 1572872 | tf_op jit(solution)/shard_map/ppermute | solution.py:624
  72.5 2.0 %collective-permute-start.14 = (f32[2,256,256]{2,1,0:T(8,128)S(1)}, f32[2,256,256]{2,1,0:T(8,128)S(1)}, u32[]{:S(2)}, u32[]{:S(2)}) collective-permute-start(f32[2,256,256]{2,1,0:T(8,128)S(1)} %get-tuple-element.79), channel_id=1, source_target_pairs={{0,1},{1,0},{2,3},{3,2},{4,5},{5,4},{6,7},{7,6},{8,9},{9,8},{10,11... | collective-permute-start | bytes 1572872 | tf_op jit(solution)/shard_map/ppermute | solution.py:624
  76.6 2.0 %collective-permute-start.15 = (f32[2,256,256]{2,1,0:T(8,128)S(1)}, f32[2,256,256]{2,1,0:T(8,128)S(1)}, u32[]{:S(2)}, u32[]{:S(2)}) collective-permute-start(f32[2,256,256]{2,1,0:T(8,128)S(1)} %get-tuple-element.82), channel_id=1, source_target_pairs={{0,1},{1,0},{2,3},{3,2},{4,5},{5,4},{6,7},{7,6},{8,9},{9,8},{10,11... | collective-permute-start | bytes 1572872 | tf_op jit(solution)/shard_map/ppermute | solution.py:624
  78.5 6.4 %collective-permute-start.24 = (f32[2,64,512]{2,1,0:T(8,128)S(1)}, f32[2,64,512]{2,1,0:T(8,128)S(1)}, u32[]{:S(2)}, u32[]{:S(2)}) collective-permute-start(f32[2,64,512]{2,1,0:T(8,128)S(1)} %get-tuple-element.88), channel_id=1, source_target_pairs={{4,6},{5,7},{6,14},{7,15},{8,10},{9,11},{10,2},{11,3},{20,22},{21,... | collective-permute-start | bytes 786440 | tf_op jit(solution)/shard_map/ppermute | solution.py:621
  81.6 4.7 %collective-permute-start.25 = (f32[2,64,512]{2,1,0:T(8,128)S(1)}, f32[2,64,512]{2,1,0:T(8,128)S(1)}, u32[]{:S(2)}, u32[]{:S(2)}) collective-permute-start(f32[2,64,512]{2,1,0:T(8,128)S(1)} %get-tuple-element.90), channel_id=1, source_target_pairs={{4,10},{5,11},{6,2},{7,3},{8,14},{9,15},{10,6},{11,7},{20,26},{21,... | collective-permute-start | bytes 786440 | tf_op jit(solution)/shard_map/ppermute | solution.py:621
  82.2 5.3 %collective-permute-start.26 = (f32[2,64,512]{2,1,0:T(8,128)S(1)}, f32[2,64,512]{2,1,0:T(8,128)S(1)}, u32[]{:S(2)}, u32[]{:S(2)}) collective-permute-start(f32[2,64,512]{2,1,0:T(8,128)S(1)} %get-tuple-element.92), channel_id=1, source_target_pairs={{4,14},{5,15},{6,6},{7,7},{8,2},{9,3},{10,10},{11,11},{20,30},{21,... | collective-permute-start | bytes 786440 | tf_op jit(solution)/shard_map/ppermute | solution.py:621
  82.9 5.9 %collective-permute-start.27 = (f32[2,64,512]{2,1,0:T(8,128)S(1)}, f32[2,64,512]{2,1,0:T(8,128)S(1)}, u32[]{:S(2)}, u32[]{:S(2)}) collective-permute-start(f32[2,64,512]{2,1,0:T(8,128)S(1)} %get-tuple-element.94), channel_id=1, source_target_pairs={{4,2},{5,3},{6,10},{7,11},{8,6},{9,7},{10,14},{11,15},{20,18},{21,... | collective-permute-start | bytes 786440 | tf_op jit(solution)/shard_map/ppermute | solution.py:621
  83.6 21.7 %collective-permute-start.17 = (f32[2,128,256]{2,1,0:T(8,128)S(1)}, f32[2,128,256]{2,1,0:T(8,128)S(1)}, u32[]{:S(2)}, u32[]{:S(2)}) collective-permute-start(f32[2,128,256]{2,1,0:T(8,128)S(1)} %get-tuple-element.84), channel_id=1, source_target_pairs={{4,8},{5,9},{6,0},{7,1},{8,12},{9,13},{10,4},{11,5},{20,24},{21,25... | collective-permute-start | bytes 786440 | tf_op jit(solution)/shard_map/ppermute | solution.py:621
  84.9 25.5 %collective-permute-start.18 = (f32[2,128,256]{2,1,0:T(8,128)S(1)}, f32[2,128,256]{2,1,0:T(8,128)S(1)}, u32[]{:S(2)}, u32[]{:S(2)}) collective-permute-start(f32[2,128,256]{2,1,0:T(8,128)S(1)} %get-tuple-element.85), channel_id=1, source_target_pairs={{4,12},{5,13},{6,4},{7,5},{8,0},{9,1},{10,8},{11,9},{20,28},{21,29... | collective-permute-start | bytes 786440 | tf_op jit(solution)/shard_map/ppermute | solution.py:621
  86.2 29.0 %collective-permute-start.19 = (f32[2,128,256]{2,1,0:T(8,128)S(1)}, f32[2,128,256]{2,1,0:T(8,128)S(1)}, u32[]{:S(2)}, u32[]{:S(2)}) collective-permute-start(f32[2,128,256]{2,1,0:T(8,128)S(1)} %get-tuple-element.86), channel_id=1, source_target_pairs={{4,0},{5,1},{6,8},{7,9},{8,4},{9,5},{10,12},{11,13},{20,16},{21,17... | collective-permute-start | bytes 786440 | tf_op jit(solution)/shard_map/ppermute | solution.py:621
  87.6 27.7 %collective-permute-start.16 = (f32[2,128,256]{2,1,0:T(8,128)S(1)}, f32[2,128,256]{2,1,0:T(8,128)S(1)}, u32[]{:S(2)}, u32[]{:S(2)}) collective-permute-start(f32[2,128,256]{2,1,0:T(8,128)S(1)} %get-tuple-element.83), channel_id=1, source_target_pairs={{4,4},{5,5},{6,12},{7,13},{8,8},{9,9},{10,0},{11,1},{20,20},{21,21... | collective-permute-start | bytes 786440 | tf_op jit(solution)/shard_map/ppermute | solution.py:621
  88.9 26.9 %collective-permute-start.28 = (f32[2,64,512]{2,1,0:T(8,128)S(1)}, f32[2,64,512]{2,1,0:T(8,128)S(1)}, u32[]{:S(2)}, u32[]{:S(2)}) collective-permute-start(f32[2,64,512]{2,1,0:T(8,128)S(1)} %collective-permute-done.24.refs_8_), channel_id=1, source_target_pairs={{0,1},{1,0},{2,3},{3,2},{4,5},{5,4},{6,7},{7,6},{8,9},{9,8},{10,11... | collective-permute-start | bytes 786440 | tf_op jit(solution)/shard_map/ppermute | solution.py:624
  105.3 10.5 %collective-permute-start.29 = (f32[2,64,512]{2,1,0:T(8,128)S(1)}, f32[2,64,512]{2,1,0:T(8,128)S(1)}, u32[]{:S(2)}, u32[]{:S(2)}) collective-permute-start(f32[2,64,512]{2,1,0:T(8,128)S(1)} %collective-permute-done.25.refs_9_), channel_id=1, source_target_pairs={{0,1},{1,0},{2,3},{3,2},{4,5},{5,4},{6,7},{7,6},{8,9},{9,8},{10,11... | collective-permute-start | bytes 786440 | tf_op jit(solution)/shard_map/ppermute | solution.py:624
  110.4 5.9 %collective-permute-start.30 = (f32[2,64,512]{2,1,0:T(8,128)S(1)}, f32[2,64,512]{2,1,0:T(8,128)S(1)}, u32[]{:S(2)}, u32[]{:S(2)}) collective-permute-start(f32[2,64,512]{2,1,0:T(8,128)S(1)} %collective-permute-done.26.refs_10_), channel_id=1, source_target_pairs={{0,1},{1,0},{2,3},{3,2},{4,5},{5,4},{6,7},{7,6},{8,9},{9,8},{10,11... | collective-permute-start | bytes 786440 | tf_op jit(solution)/shard_map/ppermute | solution.py:624
  115.2 1.5 %collective-permute-start.31 = (f32[2,64,512]{2,1,0:T(8,128)S(1)}, f32[2,64,512]{2,1,0:T(8,128)S(1)}, u32[]{:S(2)}, u32[]{:S(2)}) collective-permute-start(f32[2,64,512]{2,1,0:T(8,128)S(1)} %collective-permute-done.27.refs_11_), channel_id=1, source_target_pairs={{0,1},{1,0},{2,3},{3,2},{4,5},{5,4},{6,7},{7,6},{8,9},{9,8},{10,11... | collective-permute-start | bytes 786440 | tf_op jit(solution)/shard_map/ppermute | solution.py:624
  115.3 1.9 %collective-permute-start.21 = (f32[2,128,256]{2,1,0:T(8,128)S(1)}, f32[2,128,256]{2,1,0:T(8,128)S(1)}, u32[]{:S(2)}, u32[]{:S(2)}) collective-permute-start(f32[2,128,256]{2,1,0:T(8,128)S(1)} %collective-permute-done.17.refs_1_), channel_id=1, source_target_pairs={{0,1},{1,0},{2,3},{3,2},{4,5},{5,4},{6,7},{7,6},{8,9},{9,8},{10,11... | collective-permute-start | bytes 786440 | tf_op jit(solution)/shard_map/ppermute | solution.py:624
  115.7 1.8 %collective-permute-start.22 = (f32[2,128,256]{2,1,0:T(8,128)S(1)}, f32[2,128,256]{2,1,0:T(8,128)S(1)}, u32[]{:S(2)}, u32[]{:S(2)}) collective-permute-start(f32[2,128,256]{2,1,0:T(8,128)S(1)} %collective-permute-done.18.refs_2_), channel_id=1, source_target_pairs={{0,1},{1,0},{2,3},{3,2},{4,5},{5,4},{6,7},{7,6},{8,9},{9,8},{10,11... | collective-permute-start | bytes 786440 | tf_op jit(solution)/shard_map/ppermute | solution.py:624
  115.8 2.1 %collective-permute-start.23 = (f32[2,128,256]{2,1,0:T(8,128)S(1)}, f32[2,128,256]{2,1,0:T(8,128)S(1)}, u32[]{:S(2)}, u32[]{:S(2)}) collective-permute-start(f32[2,128,256]{2,1,0:T(8,128)S(1)} %collective-permute-done.19.refs_3_), channel_id=1, source_target_pairs={{0,1},{1,0},{2,3},{3,2},{4,5},{5,4},{6,7},{7,6},{8,9},{9,8},{10,11... | collective-permute-start | bytes 786440 | tf_op jit(solution)/shard_map/ppermute | solution.py:624
  116.3 2.0 %collective-permute-start.20 = (f32[2,128,256]{2,1,0:T(8,128)S(1)}, f32[2,128,256]{2,1,0:T(8,128)S(1)}, u32[]{:S(2)}, u32[]{:S(2)}) collective-permute-start(f32[2,128,256]{2,1,0:T(8,128)S(1)} %collective-permute-done.16.refs_0_), channel_id=1, source_target_pairs={{0,1},{1,0},{2,3},{3,2},{4,5},{5,4},{6,7},{7,6},{8,9},{9,8},{10,11... | collective-permute-start | bytes 786440 | tf_op jit(solution)/shard_map/ppermute | solution.py:624
  (9 other events, 73.6 us)

commit v3 on v2

--- a/solution.py
+++ b/solution.py
@@ -200,6 +200,7 @@
         assert self.stride >= cores
         self.top = (number - cores) // 2
         self.total = cores * own_probes
+        self.order = [j for pair in zip(range(number // 2), range(number // 2, number)) for j in pair]
 
     def home(self, q):
         return self.top + q // self.sections, q % self.sections
@@ -227,13 +228,17 @@
         return near, far, lax.rem(column, self.breadth)
 
 
-def prepare_kernel(info, phase, measured, phase_piece, own_pieces, other_pieces, scratch):
+def prepare_kernel(info, phase_hbm, measured_hbm, phase_piece, own_pieces, other_pieces, phase, measured, scratch, sems):
     rows = phase.shape[0] // 4
     width = scratch.shape[2]
-    tasks = [(phase, (phase_piece,))]
-    for probe in range(measured.shape[1]):
-        tasks.append((measured.at[0, probe], (own_pieces.at[probe], other_pieces.at[probe])))
-    for source, targets in tasks:
+    tasks = [(pltpu.make_async_copy(phase_hbm, phase, sems.at[0]), phase, (phase_piece,))]
+    for probe in range(measured.shape[0]):
+        copy = pltpu.make_async_copy(measured_hbm.at[0, probe], measured.at[probe], sems.at[1 + probe])
+        tasks.append((copy, measured.at[probe], (own_pieces.at[probe], other_pieces.at[probe])))
+    for copy, _, _ in tasks:
+        copy.start()
+    for copy, source, targets in tasks:
+        copy.wait()
         for tile in range(phase.shape[1] // width):
             columns = slice(width * tile, width * (tile + 1))
             scratch[tile] = source[:, columns]
@@ -275,60 +280,65 @@
     return result
 
 
-def filter_kernel(plan, info, *refs):
+def filter_kernel(info, *refs):
     pieces, field = refs[:-1], refs[-1]
     cosine, sine = circle_polynomials(3.1416)
     quarter = field.shape[2] // 2
+    rows = pieces[0].shape[0] // 2
+    shift = lax.rem((info[1] + 1) * rows, quarter)
+    for index in range(2):
+        columns = slice(quarter * index, quarter * (index + 1))
+        phase = pltpu.roll(exact_turn(class_rows(pieces, index)), shift, 1)
+        square = phase * phase
+        field[0, :, columns] = polynomial(cosine, square)
+        field[1, :, columns] = polynomial(sine, square) * phase
+
+
+def target_kernel(plan, info, *refs):
+    pieces, target = refs[:-1], refs[-1]
+    quarter = target.shape[1] // 2
     shift = plan.own_base(info) * (pieces[0].shape[1] // 2)
     for index in range(2):
         columns = slice(quarter * index, quarter * (index + 1))
-        phase = pltpu.roll(exact_turn(class_rows([piece.at[2] for piece in pieces], index)), shift, 1)
-        square = phase * phase
-        field[0, :, columns] = polynomial(cosine, square)
-        field[1, :, columns] = polynomial(sine, square) * phase
-
-
-def target_kernel(plan, info, *refs):
-    pieces, target = refs[:-1], refs[-1]
-    quarter = target.shape[1] // 2
-    rows = pieces[0].shape[1] // 4
-    shift = plan.own_base(info) * rows
-    for index in range(2):
-        columns = slice(quarter * index, quarter * (index + 1))
-        first, second = slice(rows * index, rows * (index + 1)), slice(rows * (index + 2), rows * (index + 3))
-        lines = [jnp.concatenate([piece[2, first], piece[2, second]], axis=1) for piece in pieces]
-        target[:, columns] = pltpu.roll(exact_turn(joined(lines, 0)), shift, 1)
+        lines = class_rows([piece.at[2] for piece in pieces], index)
+        target[:, columns] = pltpu.roll(exact_turn(lines), shift, 1)
 
 
 def window_delta(info, plan, j, near, far):
-    height, breadth = near.shape[2], near.shape[3]
+    height, breadth = near.shape[1], near.shape[2]
     offset_y = plan.offsets(info, j)[0]
     column = plan.blocks(info, j)[2]
     lane = lax.broadcasted_iota(jnp.int32, (height, breadth), 1)
     line = lax.broadcasted_iota(jnp.int32, (height, breadth), 0)
     vacuum = (line < offset_y) & (info[1] == 0)
     use_near = lane >= column
-    return [
-        jnp.where(vacuum, 0.0, jnp.where(use_near, near[0, part], far[0, part])) for part in range(2)
-    ]
-
-
-def patch_kernel(plan, j, info, near, far, phase_piece, patch, scratch):
-    height = near.shape[2]
+    return [jnp.where(vacuum, 0.0, jnp.where(use_near, near[part], far[part])) for part in range(2)]
+
+
+def patch_kernel(plan, j, info, delta, own_pieces, other_pieces, patch, near, far, scratch, sems):
+    height, breadth = near.shape[1], near.shape[2]
+    copies = []
+    for index, target in enumerate((near, far)):
+        first = pl.multiple_of(plan.blocks(info, j)[index] * breadth, breadth)
+        copies.append(pltpu.make_async_copy(delta.at[0, :, :, pl.ds(first, breadth)], target, sems.at[index]))
+        copies[-1].start()
+    for copy in copies:
+        copy.wait()
     real, imag = window_delta(info, plan, j, near, far)
     scratch[0] = real + 1.0
     scratch[1] = imag
     first = pl.multiple_of(info[0] * (height // 2), height // 2)
     patch[:2] = scratch[:, pl.ds(first, height // 2), :]
-    patch[2] = phase_piece[...]
+    batch, probe = plan.served(info, j)
+    patch[2] = jnp.where(batch == info[0], own_pieces[probe], other_pieces[probe])
 
 
 def launch_kernel(
-    plan, j, info, near, far, above, above_other, probe, own_piece, other_piece, table, twiddle, message, rolled
+    plan, j, info, near, far, above, above_other, probe, table, twiddle, message, rolled
 ):
     height, breadth = near.shape[2], near.shape[3]
     quarter = breadth // 4
-    real, imag = window_delta(info, plan, j, near, far)
+    real, imag = window_delta(info, plan, j, near.at[0], far.at[0])
     transmit = (real + 1.0, imag)
     offset_y = plan.offsets(info, j)[0]
     column = plan.blocks(info, j)[2]
@@ -354,9 +364,6 @@
         block = result[height * index : height * (index + 1)]
         message[0, :, quarter * index : quarter * (index + 1)] = block[:, :quarter]
         message[1, :, quarter * index : quarter * (index + 1)] = block[:, quarter:]
-    piece = jnp.where(plan.served(info, j)[0] == info[0], own_piece[0], other_piece[0])
-    message[2, : height // 2] = piece[:, : breadth // 2]
-    message[2, height // 2 :] = piece[:, breadth // 2 :]
 
 
 def settle_kernel(plan, info, table, twiddle, *refs):
@@ -560,9 +567,9 @@
         lanes_out(forward_lanes(quarters, forward, twiddle), lower, rows, keep, send)
 
 
-def grade_kernel(plan, info, forward, inverse, twiddle, own, other, entering, *refs):
+def grade_kernel(plan, info, inverse, twiddle, own, other, entering, *refs):
     number = plan.number
-    patches, terms, (keep, send) = refs[:number], refs[number : 2 * number], refs[2 * number :]
+    patches, terms, leaving = refs[:number], refs[number : 2 * number], refs[2 * number]
     lower = info[0] == 0
     count = number // 4
     lines = own.shape[1] // 4
@@ -572,7 +579,6 @@
         rows = slice(lines * m, lines * (m + 1))
         group = patches[count * m : count * (m + 1)]
         inner = inverse_lanes(lane_classes(own, other, lower, rows), inverse, twiddle)
-        quarters = []
         for piece in range(4):
             columns = slice(quarter * piece, quarter * (piece + 1))
             transmit = tuple(joined([patch[part, :, columns] for patch in group], 0) for part in range(2))
@@ -581,7 +587,21 @@
             for i in range(count):
                 for part in range(2):
                     terms[count * m + i][part, :, columns] = term[part][height * i : height * (i + 1)]
-            quarters.append(conj_times(transmit, inner[piece]))
+            behind = conj_times(transmit, inner[piece])
+            leaving[0, rows, columns] = behind[0]
+            leaving[1, rows, columns] = behind[1]
+
+
+def onward_kernel(info, forward, twiddle, leaving, keep, send):
+    lower = info[0] == 0
+    lines = leaving.shape[1] // 4
+    quarter = leaving.shape[2] // 4
+    for m in range(4):
+        rows = slice(lines * m, lines * (m + 1))
+        quarters = [
+            tuple(leaving[part, rows, quarter * piece : quarter * (piece + 1)] for part in range(2))
+            for piece in range(4)
+        ]
         lanes_out(forward_lanes(quarters, forward, twiddle), lower, rows, keep, send)
 
 
@@ -628,8 +648,6 @@
     lane_factors, line_factors = (jnp.asarray(table) for table in twiddles(breadth))
 
     params = pltpu.CompilerParams(vmem_limit_bytes=vmem_bytes)
-    part = jnp.where(core == 0, probe[:, :half], probe[:, half:])
-    above = lax.ppermute(part, "row", [(i, (i + 1) % number) for i in range(number)])
     def beside(*vectors):
         sizes = [value.shape[0] for value in vectors]
         return sum(
@@ -639,6 +657,8 @@
     own_positions = beside(pos_y[0], pos_x[0])
     about = jnp.stack([core, place, section]).astype(jnp.int32)
     info = beside(about, own_positions, swap(own_positions))
+    part = jnp.where(after(core, own_positions) == 0, probe[:, :half], probe[:, half:])
+    above = lax.ppermute(part, "row", [(i, (i + 1) % number) for i in range(number)])
 
     def whole(shape):
         return pl.BlockSpec(tuple(shape), lambda i, *_: (0,) * len(shape))
@@ -647,23 +667,36 @@
         return jax.ShapeDtypeStruct(shape, jnp.float32)
 
     pieces_shape = (plan.own_probes, half, breadth)
+    hbm = pl.BlockSpec(memory_space=pltpu.MemorySpace.HBM)
     phase_piece, own_pieces, other_pieces = pl.pallas_call(
         prepare_kernel,
         out_shape=[floats(half, breadth), floats(*pieces_shape), floats(*pieces_shape)],
-        grid_spec=pltpu.PrefetchScalarGridSpec(
-            num_scalar_prefetch=1,
-            grid=(1,),
-            in_specs=[
-                whole(prop_phase.shape),
-                whole(measured.shape),
-            ],
-            out_specs=[whole((half, breadth)), whole(pieces_shape), whole(pieces_shape)],
-            scratch_shapes=[pltpu.VMEM((breadth // 128, height, 128), jnp.float32)],
-        ),
+        in_specs=[pl.BlockSpec(memory_space=smem), hbm, hbm],
+        out_specs=[pl.BlockSpec(memory_space=pltpu.VMEM)] * 3,
+        scratch_shapes=[
+            pltpu.VMEM((height, breadth), jnp.float32),
+            pltpu.VMEM((plan.own_probes, height, breadth), jnp.float32),
+            pltpu.VMEM((breadth // 128, height, 128), jnp.float32),
+            pltpu.SemaphoreType.DMA((1 + plan.own_probes,)),
+        ],
         cost_estimate=light,
-            compiler_params=params,
+        compiler_params=params,
     )(after(about, part), prop_phase, measured)
     other_pieces = swap(other_pieces)
+
+    phases = [phase_piece]
+    while len(phases) < number:
+        step = len(phases)
+        if step > 1:
+            moved = jnp.stack(phases)
+        else:
+            moved = phases[0][None]
+        if 2 * step < number:
+            moved = lax.ppermute(moved, "row", [(i, (i + step) % number) for i in range(number)])
+        else:
+            moved = move(moved, [(spot((home_z[q] - step) % number, home_x[q], c), spot(home_z[q], home_x[q], c)) for q, c in every])
+        phases = phases + [moved[i] for i in range(step)]
+    phases = phases[::-1]
 
     def near_spec(j, far):
         return pl.BlockSpec(
@@ -674,22 +707,17 @@
         return pl.pallas_call(
             functools.partial(patch_kernel, plan, j),
             out_shape=floats(3, half, breadth),
-            grid_spec=pltpu.PrefetchScalarGridSpec(
-                num_scalar_prefetch=1,
-                grid=(1,),
-                in_specs=[near_spec(j, False), near_spec(j, True), whole(phase_piece.shape)],
-                out_specs=whole((3, half, breadth)),
-                scratch_shapes=[pltpu.VMEM((2, height, breadth), jnp.float32)],
-            ),
+            in_specs=[pl.BlockSpec(memory_space=smem), hbm] + [pl.BlockSpec(memory_space=pltpu.VMEM)] * 2,
+            out_specs=pl.BlockSpec(memory_space=pltpu.VMEM),
+            scratch_shapes=[pltpu.VMEM((2, height, breadth), jnp.float32)] * 3 + [pltpu.SemaphoreType.DMA((2,))],
             cost_estimate=light,
             compiler_params=params,
-        )(info, object_delta, object_delta, phase_piece)
+        )(info, object_delta, own_pieces, other_pieces)
 
     def launch_of(j, info):
-        piece_spec = pl.BlockSpec((1, half, breadth), lambda i, info: (plan.served(info, j)[1], 0, 0))
         return pl.pallas_call(
             functools.partial(launch_kernel, plan, j),
-            out_shape=[floats(3, height, wide), floats(2, height, breadth)],
+            out_shape=[floats(2, height, wide), floats(2, height, breadth)],
             grid_spec=pltpu.PrefetchScalarGridSpec(
                 num_scalar_prefetch=1,
                 grid=(1,),
@@ -699,12 +727,10 @@
                     whole(above.shape),
                     whole(above.shape),
                     whole(probe.shape),
-                    piece_spec,
-                    piece_spec,
                     whole(row_forward.shape),
                     whole(lane_factors.shape),
                 ],
-                out_specs=[whole((3, height, wide)), whole((2, height, breadth))],
+                out_specs=[whole((2, height, wide)), whole((2, height, breadth))],
             ),
             cost_estimate=light,
             compiler_params=params,
@@ -715,30 +741,36 @@
             above,
             above_other,
             probe,
-            own_pieces,
-            other_pieces,
             row_forward,
             lane_factors,
         )
 
     later = range(1, sections)
-    own_patches = [patch_of(j, info) for j in range(number)]
+    own_patches = []
+    for j in range(number):
+        own_patches.append(patch_of(j, info if j == 0 else after(info, own_patches[-1])))
+    above_other = swap(above)
+    launched = []
+    for j in range(number):
+        ready = [launched[j - 1][0]] if j else []
+        if j == number - 1:
+            ready.append(phases[0])
+        launched.append(launch_of(j, after(info, *ready) if ready else info))
     patches = {layer: [] for layer in later}
-    above_other = swap(after(above, *own_patches))
-    launched, blocks = [], []
+    blocks = []
     for j in range(number):
-        value = own_patches[j]
+        value, message = own_patches[j], launched[j][0]
+        if j == 0:
+            value = after(value, message)
         if j >= 2:
-            value = after(value, *(patches[layer][j - 2] for layer in later))
+            value = after(value, launched[-1][0], *(patches[layer][j - 2] for layer in later))
+            message = after(message, blocks[j - 2])
         for layer in later:
             patches[layer].append(move(value, inward(j, layer)))
-        launched.append(launch_of(j, info if j == 0 else after(info, launched[j - 1][0])))
-        message = launched[j][0]
-        if j >= 2:
-            message = after(message, blocks[j - 2])
         blocks.append(move(message, inward(j, 0)))
-    rolled = [item[1] for item in launched]
-    blocks = lax.optimization_barrier((*blocks, *(patches[layer][j] for layer in later for j in range(number))))[:number]
+    rolled = [launched[j][1] for j in range(number)]
+    arrived = (*blocks, *(patches[layer][j] for layer in later for j in range(number)))
+    blocks = lax.optimization_barrier(arrived)[:number]
 
     traded = (2, wide, wide)
     column_set = (column_forward, column_inverse, line_factors)
@@ -759,13 +791,11 @@
         return at_home(kernel, [traded, traded], *column_set, field, own, other)
 
     entries = {}
-    field = at_home(
-        functools.partial(filter_kernel, plan), [(2, breadth, wide)], after(patches[1][0], launched[-1][0]), *patches[1][1:]
-    )[0]
+    field = at_home(filter_kernel, [(2, breadth, wide)], after(phases[0], launched[-1][0]), *phases[1:])[0]
     keep, send = at_home(
         functools.partial(enter_kernel, number), [traded, traded], *column_set, field, *blocks
     )
-    target = at_home(functools.partial(target_kernel, plan), [(breadth, wide)], *blocks)[0]
+    target = at_home(functools.partial(target_kernel, plan), [(breadth, wide)], *patches[1])[0]
     for layer in later:
         other = swap(send)
         entries[layer], keep, send = at_home(
@@ -773,7 +803,7 @@
             [(2, wide, breadth), traded, traded],
             *row_set,
             keep,
-            after(other, target) if layer == 1 else other,
+            other,
             *patches[layer],
         )
         other = swap(send)
@@ -788,24 +818,28 @@
         other = swap(send)
         found = at_home(
             functools.partial(grade_kernel, plan),
-            [(2, half, breadth)] * number + [traded, traded],
-            *row_set,
+            [(2, half, breadth)] * number + [(2, wide, breadth)],
+            row_inverse,
+            lane_factors,
             keep,
             other,
             entries[layer],
             *patches[layer],
         )
-        keep, send = found[number:]
+        keep, send = at_home(onward_kernel, [traded, traded], row_forward, lane_factors, found[number])
         other = swap(send)
         if layer > 1:
-            came = [move(after(found[j], other), outward(j, layer)) for j in range(number)]
+            came = [move(found[j], outward(j, layer)) for j in range(number)]
             terms = came if terms is None else [first + second for first, second in zip(terms, came)]
             keep, send = through(True, keep, other)
     leaving = at_home(
         functools.partial(leave_kernel, number), [(2, height, wide)] * number, *column_set, field, keep, other
     )
-    came = [move(after(found[j], other if j < 2 else leaving[0]), outward(j, 1)) for j in range(number)]
-    spectra = [move(leaving[j], outward(j, 0)) for j in range(number)]
+    came, spectra = [None] * number, [None] * number
+    for j in plan.order:
+        came[j] = move(after(found[j], other), outward(j, 1))
+    for j in plan.order:
+        spectra[j] = move(leaving[j], outward(j, 0))
     terms = came if terms is None else [first + second for first, second in zip(terms, came)]
 
     operands = [

time: 123 us -> 115 us (0.935)
  waiting for transfers between devices: 52.5 us -> 42.9 us
  starting transfers between devices: 36 us -> 37.7 us
  local copies, waits for them, and re-layouts: 3.63 us -> 2.05 us
    ppermute x16 -> x17, waiting for transfers between devices: 45.2 us -> 29.7 us  [move(): return lax.ppermute(value, line_axes, pairs)]
    ppermute x1, waiting for transfers between devices: 0.01 us -> 4.67 us  [on_device(): lax.ppermute(part, 'row', [(i, (i + 1) % number) for i in range(number)])]
    ppermute x0 -> x1, starting transfers between devices: none -> 1.63 us  [on_device(): lax.ppermute(moved, 'row', [(i, (i + step) % number) for i in range(numbe...]
    unnamed x18 -> x16, local copies, waits for them, and re-layouts: 3.63 us -> 2.03 us
    ppermute x0 -> x1, waiting for transfers between devices: none -> 1.47 us  [on_device(): lax.ppermute(moved, 'row', [(i, (i + step) % number) for i in range(numbe...]
    pallas_call x7 -> x8, Pallas kernels: 14.9 us -> 15.4 us  [at_home(): pl.pallas_call(kernel, out_shape=[floats(*shape) for shape in outs], in_s...]
    ppermute x16 -> x17, starting transfers between devices: 29.9 us -> 29.8 us  [move(): return lax.ppermute(value, line_axes, pairs)]
  transfers between devices with their start and end apart: 32 -> 34, of which waited for: 16 -> 15; matrix products, arithmetic and copies ran while one was open for 1% -> 0% of each run, Pallas kernels for 12% -> 13%
where the time goes in v3:
time: 115 us
  waiting for transfers between devices  42.9 us (37%)
  starting transfers between devices  37.7 us (33%)
  Pallas kernels  29.3 us (25%)
  other arithmetic  2.13 us (2%)
  local copies, waits for them, and re-layouts  2.05 us (2%)
    ppermute x17, starting transfers between devices, move(): return lax.ppermute(value, line_axes, pairs)  29.8 us
    ppermute x17, waiting for transfers between devices, move(): return lax.ppermute(value, line_axes, pairs)  29.7 us
    pallas_call x8, Pallas kernels, at_home(): pl.pallas_call(kernel, out_shape=[floats(*shape) for shape in outs], in_s...  15.4 us
    ppermute x15, waiting for transfers between devices, swap(): lax.ppermute(value, 'batch', [(i, (i + 1) % cores) for i in range(cores)])  7.05 us
    pallas_call x4, Pallas kernels, launch_of(): pl.pallas_call(functools.partial(launch_kernel, plan, j), out_shape=[floa...  5.31 us
    ppermute x1, waiting for transfers between devices, on_device(): lax.ppermute(part, 'row', [(i, (i + 1) % number) for i in range(number)])  4.67 us
    pallas_call x1, Pallas kernels, on_device(): pl.pallas_call(functools.partial(settle_kernel, plan), out_shape=jax.Shap...  4.46 us
    pallas_call x4, Pallas kernels, patch_of(): pl.pallas_call(functools.partial(patch_kernel, plan, j), out_shape=floats...  3.26 us
  transfers between devices with their start and end apart: 34, of which 15 were waited for; matrix products, arithmetic and copies ran while one was open for 0% of the time, Pallas kernels for 13%

profile of v3, /device:TPU:0, one launch (start us, length us, event | category | flops | bytes accessed | tf_op | source)
XLA Modules:
  0.0 114.5 jit_solution(1390222610254832360)
XLA Ops:
  2.0 3.1 %collective-permute-start.3 = (f32[2,64,512]{2,1,0:T(8,128)S(1)}, f32[2,64,512]{2,1,0:T(8,128)S(1)}, u32[]{:S(2)}, u32[]{:S(2)}) collective-permute-start(f32[2,64,512]{2,1,0:T(8,128)S(1)} %slice_select_fusion), channel_id=1, source_target_pairs={{0,4},{4,8},{8,12},{12,0},{1,5},{5,9},{9,13},{13,1},{2,6},{6,10},{... | collective-permute-start | bytes 786440 | tf_op jit(solution)/shard_map/ppermute | solution.py:661
  7.9 1.6 %collective-permute-start.1 = (f32[1,64,512]{2,1,0:T(8,128)S(1)}, f32[1,64,512]{2,1,0:T(8,128)S(1)}, u32[]{:S(2)}, u32[]{:S(2)}) collective-permute-start(f32[1,64,512]{2,1,0:T(8,128)S(1)} %bitcast.11), channel_id=1, source_target_pairs={{0,4},{4,8},{8,12},{12,0},{1,5},{5,9},{9,13},{13,1},{2,6},{6,10},{... | collective-permute-start | bytes 393224 | tf_op jit(solution)/shard_map/ppermute | solution.py:695
  9.5 4.7 %collective-permute-done.3.above = f32[2,64,512]{2,1,0:T(8,128)S(1)} collective-permute-done((f32[2,64,512]{2,1,0:T(8,128)S(1)}, f32[2,64,512]{2,1,0:T(8,128)S(1)}, u32[]{:S(2)}, u32[]{:S(2)}) %collective-permute-start.3) | collective-permute-done | bytes 262176 | tf_op jit(solution)/shard_map/ppermute | solution.py:661
  14.7 1.5 %collective-permute-done.1 = f32[1,64,512]{2,1,0:T(8,128)S(1)} collective-permute-done((f32[1,64,512]{2,1,0:T(8,128)S(1)}, f32[1,64,512]{2,1,0:T(8,128)S(1)}, u32[]{:S(2)}, u32[]{:S(2)}) %collective-permute-start.1) | collective-permute-done | bytes 131104 | tf_op jit(solution)/shard_map/ppermute | solution.py:695
  16.2 2.6 %collective-permute-start.2 = (f32[2,64,512]{2,1,0:T(8,128)S(1)}, f32[2,64,512]{2,1,0:T(8,128)S(1)}, u32[]{:S(2)}, u32[]{:S(2)}) collective-permute-start(f32[2,64,512]{2,1,0:T(8,128)S(1)} %pad_maximum_fusion), channel_id=1, source_target_pairs={{12,4},{13,5},{14,6},{15,7},{0,8},{1,9},{2,10},{3,11},{28,20},{29,... | collective-permute-start | bytes 786440 | tf_op jit(solution)/shard_map/ppermute | solution.py:641
  21.4 1.3 %shard_map.119 = (f32[2,128,256]{2,1,0:T(8,128)S(1)}, f32[2,128,512]{2,1,0:T(8,128)S(1)}) custom-call(s32[11]{0:T(128)S(1)} %pad_add_fusion.1.info, f32[1,2,128,2048]{3,2,1,0:T(8,128)S(1)} %copy-done, f32[1,2,128,2048]{3,2,1,0:T(8,128)S(1)} %copy-done, f32[2,64,512]{2,1,0:T(8,128)S(1)} %collective-permute-done.3.above, ...), custom_call_target="tpu_custom_call" | custom-call | tf_op jit(solution)/shard_map/pallas_call | solution.py:718
  25.1 5.1 %collective-permute-start.10 = (f32[2,128,256]{2,1,0:T(8,128)S(1)}, f32[2,128,256]{2,1,0:T(8,128)S(1)}, u32[]{:S(2)}, u32[]{:S(2)}) collective-permute-start(f32[2,128,256]{2,1,0:T(8,128)S(1)} %get-tuple-element.59), channel_id=1, source_target_pairs={{4,4},{5,5},{12,6},{13,7},{8,8},{9,9},{0,10},{1,11},{20,20},{21,21... | collective-permute-start | bytes 786440 | tf_op jit(solution)/shard_map/ppermute | solution.py:641
  30.2 1.3 %shard_map.120 = (f32[2,128,256]{2,1,0:T(8,128)S(1)}, f32[2,128,512]{2,1,0:T(8,128)S(1)}) custom-call(s32[11]{0:T(128)S(1)} %pad_add_fusion.1.info, f32[1,2,128,2048]{3,2,1,0:T(8,128)S(1)} %copy-done, f32[1,2,128,2048]{3,2,1,0:T(8,128)S(1)} %copy-done, f32[2,64,512]{2,1,0:T(8,128)S(1)} %collective-permute-done.3.above, ...), custom_call_target="tpu_custom_call" | custom-call | tf_op jit(solution)/shard_map/pallas_call | solution.py:718
  31.5 1.4 %collective-permute-start.11 = (f32[2,128,256]{2,1,0:T(8,128)S(1)}, f32[2,128,256]{2,1,0:T(8,128)S(1)}, u32[]{:S(2)}, u32[]{:S(2)}) collective-permute-start(f32[2,128,256]{2,1,0:T(8,128)S(1)} %get-tuple-element.61), channel_id=1, source_target_pairs={{8,4},{9,5},{0,6},{1,7},{12,8},{13,9},{4,10},{5,11},{24,20},{25,21... | collective-permute-start | bytes 786440 | tf_op jit(solution)/shard_map/ppermute | solution.py:641
  33.0 1.3 %shard_map.121 = (f32[2,128,256]{2,1,0:T(8,128)S(1)}, f32[2,128,512]{2,1,0:T(8,128)S(1)}) custom-call(s32[11]{0:T(128)S(1)} %pad_add_fusion.1.info, f32[1,2,128,2048]{3,2,1,0:T(8,128)S(1)} %copy-done, f32[1,2,128,2048]{3,2,1,0:T(8,128)S(1)} %copy-done, f32[2,64,512]{2,1,0:T(8,128)S(1)} %collective-permute-done.3.above, ...), custom_call_target="tpu_custom_call" | custom-call | tf_op jit(solution)/shard_map/pallas_call | solution.py:718
  34.3 1.3 %shard_map.122 = (f32[2,128,256]{2,1,0:T(8,128)S(1)}, f32[2,128,512]{2,1,0:T(8,128)S(1)}) custom-call(s32[11]{0:T(128)S(1)} %pad_add_fusion.1.info, f32[1,2,128,2048]{3,2,1,0:T(8,128)S(1)} %copy-done, f32[1,2,128,2048]{3,2,1,0:T(8,128)S(1)} %copy-done, f32[2,64,512]{2,1,0:T(8,128)S(1)} %collective-permute-done.3.above, ...), custom_call_target="tpu_custom_call" | custom-call | tf_op jit(solution)/shard_map/pallas_call | solution.py:718
  37.1 4.1 %collective-permute-done.11.refs_1_ = f32[2,128,256]{2,1,0:T(8,128)S(1)} collective-permute-done((f32[2,128,256]{2,1,0:T(8,128)S(1)}, f32[2,128,256]{2,1,0:T(8,128)S(1)}, u32[]{:S(2)}, u32[]{:S(2)}) %collective-permute-start.11) | collective-permute-done | bytes 262176 | tf_op jit(solution)/shard_map/ppermute | solution.py:641
  41.2 4.9 %collective-permute-start.13 = (f32[2,128,256]{2,1,0:T(8,128)S(1)}, f32[2,128,256]{2,1,0:T(8,128)S(1)}, u32[]{:S(2)}, u32[]{:S(2)}) collective-permute-start(f32[2,128,256]{2,1,0:T(8,128)S(1)} %get-tuple-element.76), channel_id=1, source_target_pairs={{0,4},{1,5},{8,6},{9,7},{4,8},{5,9},{12,10},{13,11},{16,20},{17,21... | collective-permute-start | bytes 786440 | tf_op jit(solution)/shard_map/ppermute | solution.py:641
  46.2 5.1 %collective-permute-start.12 = (f32[2,128,256]{2,1,0:T(8,128)S(1)}, f32[2,128,256]{2,1,0:T(8,128)S(1)}, u32[]{:S(2)}, u32[]{:S(2)}) collective-permute-start(f32[2,128,256]{2,1,0:T(8,128)S(1)} %get-tuple-element.75), channel_id=1, source_target_pairs={{12,4},{13,5},{4,6},{5,7},{0,8},{1,9},{8,10},{9,11},{28,20},{29,21... | collective-permute-start | bytes 786440 | tf_op jit(solution)/shard_map/ppermute | solution.py:641
  51.3 2.1 %shard_map.123.field = f32[2,512,256]{2,1,0:T(8,128)S(1)} custom-call(s32[3]{0:T(128)S(1)} %pad_add_fusion.info, f32[64,512]{1,0:T(8,128)S(1)} %get-tuple-element.66.refs_0_, f32[64,512]{1,0:T(8,128)S(1)} %get-tuple-element.107.refs_1_, f32[64,512]{1,0:T(8,128)S(1)} %bitcast.13, f32[64,512]{1,0:T(8,128)S(1)} %get-tuple-element.58.refs_3_), custom_call_target="tpu_custom_call" | custom-call | tf_op jit(solution)/shard_map/pallas_call | solution.py:780
  53.4 2.8 %collective-permute-done.12.refs_2_ = f32[2,128,256]{2,1,0:T(8,128)S(1)} collective-permute-done((f32[2,128,256]{2,1,0:T(8,128)S(1)}, f32[2,128,256]{2,1,0:T(8,128)S(1)}, u32[]{:S(2)}, u32[]{:S(2)}) %collective-permute-start.12) | collective-permute-done | bytes 262176 | tf_op jit(solution)/shard_map/ppermute | solution.py:641
  56.2 2.3 %shard_map.129 = (f32[2,256,256]{2,1,0:T(8,128)S(1)}, f32[2,256,256]{2,1,0:T(8,128)S(1)}) custom-call(s32[3]{0:T(128)S(1)} %pad_add_fusion.info, bf16[2,256,256]{2,1,0:T(8,128)(2,1)S(1)} %copy-done.3, bf16[2,256,256]{2,1,0:T(8,128)(2,1)S(1)} %copy-done.1, f32[4,2,128,128]{3,2,1,0:T(8,128)S(1)} %copy-done.4, f32[2,512,256]{2,1,0:T(8,128)S(1)} %shard_map.123.field, ...), custom_call_target="tpu_custom_call" | custom-call | tf_op jit(solution)/shard_map/pallas_call | solution.py:780
  58.6 1.9 %collective-permute-done.14.other = f32[2,256,256]{2,1,0:T(8,128)S(1)} collective-permute-done((f32[2,256,256]{2,1,0:T(8,128)S(1)}, f32[2,256,256]{2,1,0:T(8,128)S(1)}, u32[]{:S(2)}, u32[]{:S(2)}) %collective-permute-start.14) | collective-permute-done | bytes 524320 | tf_op jit(solution)/shard_map/ppermute | solution.py:644
  60.5 2.0 %shard_map.130 = (f32[2,256,512]{2,1,0:T(8,128)S(1)}, f32[2,256,256]{2,1,0:T(8,128)S(1)}, f32[2,256,256]{2,1,0:T(8,128)S(1)}) custom-call(s32[3]{0:T(128)S(1)} %pad_add_fusion.info, bf16[2,256,256]{2,1,0:T(8,128)(2,1)S(1)} %copy-done.1, bf16[2,256,256]{2,1,0:T(8,128)(2,1)S(1)} %copy-done.3, f32[8,128]{1,0:T(8,128)S(1)} %copy-done.6, ...), custom_call_target="tpu_custom_call" | custom-call | tf_op jit(solution)/shard_map/pallas_call | solution.py:780
  62.8 1.6 %shard_map.128.target = f32[512,256]{1,0:T(8,128)S(1)} custom-call(s32[3]{0:T(128)S(1)} %pad_add_fusion.info, f32[3,64,512]{2,1,0:T(8,128)S(1)} %collective-permute-done.6.refs_0_, f32[3,64,512]{2,1,0:T(8,128)S(1)} %collective-permute-done.7.refs_1_, f32[3,64,512]{2,1,0:T(8,128)S(1)} %collective-permute-done.8.refs_2_, ...), custom_call_target="tpu_custom_call" | custom-call | tf_op jit(solution)/shard_map/pallas_call | solution.py:780
  64.5 2.4 %shard_map.131 = (f32[2,256,256]{2,1,0:T(8,128)S(1)}, f32[2,256,256]{2,1,0:T(8,128)S(1)}) custom-call(s32[3]{0:T(128)S(1)} %pad_add_fusion.info, bf16[2,256,256]{2,1,0:T(8,128)(2,1)S(1)} %copy-done.3, bf16[2,256,256]{2,1,0:T(8,128)(2,1)S(1)} %copy-done.1, f32[4,2,128,128]{3,2,1,0:T(8,128)S(1)} %copy-done.4, f32[512,256]{1,0:T(8,128)S(1)} %shard_map.128.target, ...), custom_call_target="tpu_custom_call" | custom-call | tf_op jit(solution)/shard_map/pallas_call | solution.py:780
  67.3 1.7 %collective-permute-done.16.other = f32[2,256,256]{2,1,0:T(8,128)S(1)} collective-permute-done((f32[2,256,256]{2,1,0:T(8,128)S(1)}, f32[2,256,256]{2,1,0:T(8,128)S(1)}, u32[]{:S(2)}, u32[]{:S(2)}) %collective-permute-start.16) | collective-permute-done | bytes 524320 | tf_op jit(solution)/shard_map/ppermute | solution.py:644
  68.9 1.4 %shard_map.132 = (f32[2,64,512]{2,1,0:T(8,128)S(1)}, f32[2,64,512]{2,1,0:T(8,128)S(1)}, f32[2,64,512]{2,1,0:T(8,128)S(1)}, f32[2,64,512]{2,1,0:T(8,128)S(1)}, f32[2,256,512]{2,1,0:T(8,128)S(1)}) custom-call(s32[3]{0:T(128)S(1)} %pad_add_fusion.info, bf16[2,256,256]{2,1,0:T(8,128)(2,1)S(1)} %copy-done.3, f32[8,128]{1,0:T(8,128)S(1)} %copy-done.6, ...), custom_call_target="tpu_custom_call" | custom-call | tf_op jit(solution)/shard_map/pallas_call | solution.py:780
  71.9 1.7 %collective-permute-done.17.other = f32[2,256,256]{2,1,0:T(8,128)S(1)} collective-permute-done((f32[2,256,256]{2,1,0:T(8,128)S(1)}, f32[2,256,256]{2,1,0:T(8,128)S(1)}, u32[]{:S(2)}, u32[]{:S(2)}) %collective-permute-start.17) | collective-permute-done | bytes 524320 | tf_op jit(solution)/shard_map/ppermute | solution.py:644
  76.3 2.3 %shard_map.134 = (f32[2,128,256]{2,1,0:T(8,128)S(1)}, f32[2,128,256]{2,1,0:T(8,128)S(1)}, f32[2,128,256]{2,1,0:T(8,128)S(1)}, f32[2,128,256]{2,1,0:T(8,128)S(1)}) custom-call(s32[3]{0:T(128)S(1)} %pad_add_fusion.info, bf16[2,256,256]{2,1,0:T(8,128)(2,1)S(1)} %copy-done.3, bf16[2,256,256]{2,1,0:T(8,128)(2,1)S(1)} %copy-done.1, ...), custom_call_target="tpu_custom_call" | custom-call | tf_op jit(solution)/shard_map/pallas_call | solution.py:780
  78.6 1.3 %collective-permute-start.18 = (f32[2,128,256]{2,1,0:T(8,128)S(1)}, f32[2,128,256]{2,1,0:T(8,128)S(1)}, u32[]{:S(2)}, u32[]{:S(2)}) collective-permute-start(f32[2,128,256]{2,1,0:T(8,128)S(1)} %get-tuple-element.91), channel_id=1, source_target_pairs={{4,4},{5,5},{6,12},{7,13},{8,8},{9,9},{10,0},{11,1},{20,20},{21,21... | collective-permute-start | bytes 786440 | tf_op jit(solution)/shard_map/ppermute | solution.py:641
  79.9 1.3 %collective-permute-start.19 = (f32[2,128,256]{2,1,0:T(8,128)S(1)}, f32[2,128,256]{2,1,0:T(8,128)S(1)}, u32[]{:S(2)}, u32[]{:S(2)}) collective-permute-start(f32[2,128,256]{2,1,0:T(8,128)S(1)} %get-tuple-element.92), channel_id=1, source_target_pairs={{4,8},{5,9},{6,0},{7,1},{8,12},{9,13},{10,4},{11,5},{20,24},{21,25... | collective-permute-start | bytes 786440 | tf_op jit(solution)/shard_map/ppermute | solution.py:641
  82.6 1.3 %collective-permute-start.21 = (f32[2,128,256]{2,1,0:T(8,128)S(1)}, f32[2,128,256]{2,1,0:T(8,128)S(1)}, u32[]{:S(2)}, u32[]{:S(2)}) collective-permute-start(f32[2,128,256]{2,1,0:T(8,128)S(1)} %get-tuple-element.94), channel_id=1, source_target_pairs={{4,0},{5,1},{6,8},{7,9},{8,4},{9,5},{10,12},{11,13},{20,16},{21,17... | collective-permute-start | bytes 786440 | tf_op jit(solution)/shard_map/ppermute | solution.py:641
  84.2 14.6 %collective-permute-done.18.refs_0_ = f32[2,128,256]{2,1,0:T(8,128)S(1)} collective-permute-done((f32[2,128,256]{2,1,0:T(8,128)S(1)}, f32[2,128,256]{2,1,0:T(8,128)S(1)}, u32[]{:S(2)}, u32[]{:S(2)}) %collective-permute-start.18) | collective-permute-done | bytes 262176 | tf_op jit(solution)/shard_map/ppermute | solution.py:641
  98.8 4.8 %collective-permute-done.19.refs_1_ = f32[2,128,256]{2,1,0:T(8,128)S(1)} collective-permute-done((f32[2,128,256]{2,1,0:T(8,128)S(1)}, f32[2,128,256]{2,1,0:T(8,128)S(1)}, u32[]{:S(2)}, u32[]{:S(2)}) %collective-permute-start.19) | collective-permute-done | bytes 262176 | tf_op jit(solution)/shard_map/ppermute | solution.py:641
  104.1 3.3 %collective-permute-done.21.refs_3_ = f32[2,128,256]{2,1,0:T(8,128)S(1)} collective-permute-done((f32[2,128,256]{2,1,0:T(8,128)S(1)}, f32[2,128,256]{2,1,0:T(8,128)S(1)}, u32[]{:S(2)}, u32[]{:S(2)}) %collective-permute-start.21) | collective-permute-done | bytes 262176 | tf_op jit(solution)/shard_map/ppermute | solution.py:641
  110.0 4.5 %shard_map.135 = f32[1,2,128,2048]{3,2,1,0:T(8,128)} custom-call(s32[11]{0:T(128)S(1)} %pad_add_fusion.1.info, bf16[2,256,256]{2,1,0:T(8,128)(2,1)S(1)} %copy-done.3, f32[8,128]{1,0:T(8,128)S(1)} %copy-done.6, f32[2,128,256]{2,1,0:T(8,128)S(1)} %collective-permute-done.18.refs_0_, f32[2,128,256]{2,1,0:T(8,128)S(1)} %collective-permute-done.19.refs_1_, ...), custom_call_target="tpu_custom_call" | custom-call | tf_op jit(solution)/shard_map/pallas_call | solution.py:854
  (76 shorter events, 21.2 us)
Async XLA Ops:
  2.0 12.2 %collective-permute-start.3 = (f32[2,64,512]{2,1,0:T(8,128)S(1)}, f32[2,64,512]{2,1,0:T(8,128)S(1)}, u32[]{:S(2)}, u32[]{:S(2)}) collective-permute-start(f32[2,64,512]{2,1,0:T(8,128)S(1)} %slice_select_fusion), channel_id=1, source_target_pairs={{0,4},{4,8},{8,12},{12,0},{1,5},{5,9},{9,13},{13,1},{2,6},{6,10},{... | collective-permute-start | bytes 786440 | tf_op jit(solution)/shard_map/ppermute | solution.py:661
  7.9 8.3 %collective-permute-start.1 = (f32[1,64,512]{2,1,0:T(8,128)S(1)}, f32[1,64,512]{2,1,0:T(8,128)S(1)}, u32[]{:S(2)}, u32[]{:S(2)}) collective-permute-start(f32[1,64,512]{2,1,0:T(8,128)S(1)} %bitcast.11), channel_id=1, source_target_pairs={{0,4},{4,8},{8,12},{12,0},{1,5},{5,9},{9,13},{13,1},{2,6},{6,10},{... | collective-permute-start | bytes 393224 | tf_op jit(solution)/shard_map/ppermute | solution.py:695
  9.5 9.4 %collective-permute-start.5 = (f32[2,64,512]{2,1,0:T(8,128)S(1)}, f32[2,64,512]{2,1,0:T(8,128)S(1)}, u32[]{:S(2)}, u32[]{:S(2)}) collective-permute-start(f32[2,64,512]{2,1,0:T(8,128)S(1)} %get-tuple-element.68), channel_id=1, source_target_pairs={{0,1},{1,0},{2,3},{3,2},{4,5},{5,4},{6,7},{7,6},{8,9},{9,8},{10,11... | collective-permute-start | bytes 786440 | tf_op jit(solution)/shard_map/ppermute | solution.py:644
  14.2 7.1 %collective-permute-start.4 = (f32[2,64,512]{2,1,0:T(8,128)S(1)}, f32[2,64,512]{2,1,0:T(8,128)S(1)}, u32[]{:S(2)}, u32[]{:S(2)}) collective-permute-start(f32[2,64,512]{2,1,0:T(8,128)S(1)} %collective-permute-done.3.above), channel_id=1, source_target_pairs={{0,1},{1,0},{2,3},{3,2},{4,5},{5,4},{6,7},{7,6},{8,9},{9,8},{10,11... | collective-permute-start | bytes 786440 | tf_op jit(solution)/shard_map/ppermute | solution.py:644
  14.2 4.7 %collective-permute-start = (s32[4]{0:T(128)S(1)}, s32[4]{0:T(128)S(1)}, u32[]{:S(2)}, u32[]{:S(2)}) collective-permute-start(s32[4]{0:T(128)S(1)} %pad_add_fusion.2), channel_id=1, source_target_pairs={{0,1},{1,0},{2,3},{3,2},{4,5},{5,4},{6,7},{7,6},{8,9},{9,8},{10,11... | collective-permute-start | bytes 56 | tf_op jit(solution)/shard_map/ppermute | solution.py:644
  16.2 16.7 %collective-permute-start.2 = (f32[2,64,512]{2,1,0:T(8,128)S(1)}, f32[2,64,512]{2,1,0:T(8,128)S(1)}, u32[]{:S(2)}, u32[]{:S(2)}) collective-permute-start(f32[2,64,512]{2,1,0:T(8,128)S(1)} %pad_maximum_fusion), channel_id=1, source_target_pairs={{12,4},{13,5},{14,6},{15,7},{0,8},{1,9},{2,10},{3,11},{28,20},{29,... | collective-permute-start | bytes 786440 | tf_op jit(solution)/shard_map/ppermute | solution.py:641
  20.6 15.0 %collective-permute-start.7 = (f32[3,64,512]{2,1,0:T(8,128)S(1)}, f32[3,64,512]{2,1,0:T(8,128)S(1)}, u32[]{:S(2)}, u32[]{:S(2)}) collective-permute-start(f32[3,64,512]{2,1,0:T(8,128)S(1)} %shard_map.125), channel_id=1, source_target_pairs={{10,4},{11,5},{2,6},{3,7},{14,8},{15,9},{6,10},{7,11},{26,20},{27,... | collective-permute-start | bytes 1179656 | tf_op jit(solution)/shard_map/ppermute | solution.py:641
  22.7 13.7 %collective-permute-start.6 = (f32[3,64,512]{2,1,0:T(8,128)S(1)}, f32[3,64,512]{2,1,0:T(8,128)S(1)}, u32[]{:S(2)}, u32[]{:S(2)}) collective-permute-start(f32[3,64,512]{2,1,0:T(8,128)S(1)} %shard_map.124), channel_id=1, source_target_pairs={{6,4},{7,5},{14,6},{15,7},{10,8},{11,9},{2,10},{3,11},{22,20},{23,... | collective-permute-start | bytes 1179656 | tf_op jit(solution)/shard_map/ppermute | solution.py:641
  25.1 12.0 %collective-permute-start.10 = (f32[2,128,256]{2,1,0:T(8,128)S(1)}, f32[2,128,256]{2,1,0:T(8,128)S(1)}, u32[]{:S(2)}, u32[]{:S(2)}) collective-permute-start(f32[2,128,256]{2,1,0:T(8,128)S(1)} %get-tuple-element.59), channel_id=1, source_target_pairs={{4,4},{5,5},{12,6},{13,7},{8,8},{9,9},{0,10},{1,11},{20,20},{21,21... | collective-permute-start | bytes 786440 | tf_op jit(solution)/shard_map/ppermute | solution.py:641
  31.5 9.7 %collective-permute-start.11 = (f32[2,128,256]{2,1,0:T(8,128)S(1)}, f32[2,128,256]{2,1,0:T(8,128)S(1)}, u32[]{:S(2)}, u32[]{:S(2)}) collective-permute-start(f32[2,128,256]{2,1,0:T(8,128)S(1)} %get-tuple-element.61), channel_id=1, source_target_pairs={{8,4},{9,5},{0,6},{1,7},{12,8},{13,9},{4,10},{5,11},{24,20},{25,21... | collective-permute-start | bytes 786440 | tf_op jit(solution)/shard_map/ppermute | solution.py:641
  35.7 20.5 %collective-permute-start.9 = (f32[3,64,512]{2,1,0:T(8,128)S(1)}, f32[3,64,512]{2,1,0:T(8,128)S(1)}, u32[]{:S(2)}, u32[]{:S(2)}) collective-permute-start(f32[3,64,512]{2,1,0:T(8,128)S(1)} %shard_map.127), channel_id=1, source_target_pairs={{2,4},{3,5},{10,6},{11,7},{6,8},{7,9},{14,10},{15,11},{18,20},{19,... | collective-permute-start | bytes 1179656 | tf_op jit(solution)/shard_map/ppermute | solution.py:641
  36.4 19.8 %collective-permute-start.8 = (f32[3,64,512]{2,1,0:T(8,128)S(1)}, f32[3,64,512]{2,1,0:T(8,128)S(1)}, u32[]{:S(2)}, u32[]{:S(2)}) collective-permute-start(f32[3,64,512]{2,1,0:T(8,128)S(1)} %shard_map.126), channel_id=1, source_target_pairs={{14,4},{15,5},{6,6},{7,7},{2,8},{3,9},{10,10},{11,11},{30,20},{31,... | collective-permute-start | bytes 1179656 | tf_op jit(solution)/shard_map/ppermute | solution.py:641
  41.2 12.2 %collective-permute-start.13 = (f32[2,128,256]{2,1,0:T(8,128)S(1)}, f32[2,128,256]{2,1,0:T(8,128)S(1)}, u32[]{:S(2)}, u32[]{:S(2)}) collective-permute-start(f32[2,128,256]{2,1,0:T(8,128)S(1)} %get-tuple-element.76), channel_id=1, source_target_pairs={{0,4},{1,5},{8,6},{9,7},{4,8},{5,9},{12,10},{13,11},{16,20},{17,21... | collective-permute-start | bytes 786440 | tf_op jit(solution)/shard_map/ppermute | solution.py:641
  46.2 10.0 %collective-permute-start.12 = (f32[2,128,256]{2,1,0:T(8,128)S(1)}, f32[2,128,256]{2,1,0:T(8,128)S(1)}, u32[]{:S(2)}, u32[]{:S(2)}) collective-permute-start(f32[2,128,256]{2,1,0:T(8,128)S(1)} %get-tuple-element.75), channel_id=1, source_target_pairs={{12,4},{13,5},{4,6},{5,7},{0,8},{1,9},{8,10},{9,11},{28,20},{29,21... | collective-permute-start | bytes 786440 | tf_op jit(solution)/shard_map/ppermute | solution.py:641
  58.6 2.0 %collective-permute-start.14 = (f32[2,256,256]{2,1,0:T(8,128)S(1)}, f32[2,256,256]{2,1,0:T(8,128)S(1)}, u32[]{:S(2)}, u32[]{:S(2)}) collective-permute-start(f32[2,256,256]{2,1,0:T(8,128)S(1)} %get-tuple-element.82), channel_id=1, source_target_pairs={{0,1},{1,0},{2,3},{3,2},{4,5},{5,4},{6,7},{7,6},{8,9},{9,8},{10,11... | collective-permute-start | bytes 1572872 | tf_op jit(solution)/shard_map/ppermute | solution.py:644
  62.6 2.0 %collective-permute-start.15 = (f32[2,256,256]{2,1,0:T(8,128)S(1)}, f32[2,256,256]{2,1,0:T(8,128)S(1)}, u32[]{:S(2)}, u32[]{:S(2)}) collective-permute-start(f32[2,256,256]{2,1,0:T(8,128)S(1)} %get-tuple-element.84), channel_id=1, source_target_pairs={{0,1},{1,0},{2,3},{3,2},{4,5},{5,4},{6,7},{7,6},{8,9},{9,8},{10,11... | collective-permute-start | bytes 1572872 | tf_op jit(solution)/shard_map/ppermute | solution.py:644
  67.0 2.0 %collective-permute-start.16 = (f32[2,256,256]{2,1,0:T(8,128)S(1)}, f32[2,256,256]{2,1,0:T(8,128)S(1)}, u32[]{:S(2)}, u32[]{:S(2)}) collective-permute-start(f32[2,256,256]{2,1,0:T(8,128)S(1)} %get-tuple-element.86), channel_id=1, source_target_pairs={{0,1},{1,0},{2,3},{3,2},{4,5},{5,4},{6,7},{7,6},{8,9},{9,8},{10,11... | collective-permute-start | bytes 1572872 | tf_op jit(solution)/shard_map/ppermute | solution.py:644
  71.6 2.0 %collective-permute-start.17 = (f32[2,256,256]{2,1,0:T(8,128)S(1)}, f32[2,256,256]{2,1,0:T(8,128)S(1)}, u32[]{:S(2)}, u32[]{:S(2)}) collective-permute-start(f32[2,256,256]{2,1,0:T(8,128)S(1)} %get-tuple-element.90), channel_id=1, source_target_pairs={{0,1},{1,0},{2,3},{3,2},{4,5},{5,4},{6,7},{7,6},{8,9},{9,8},{10,11... | collective-permute-start | bytes 1572872 | tf_op jit(solution)/shard_map/ppermute | solution.py:644
  73.5 6.4 %collective-permute-start.26 = (f32[2,64,512]{2,1,0:T(8,128)S(1)}, f32[2,64,512]{2,1,0:T(8,128)S(1)}, u32[]{:S(2)}, u32[]{:S(2)}) collective-permute-start(f32[2,64,512]{2,1,0:T(8,128)S(1)} %get-tuple-element.96), channel_id=1, source_target_pairs={{4,6},{5,7},{6,14},{7,15},{8,10},{9,11},{10,2},{11,3},{20,22},{21,... | collective-permute-start | bytes 786440 | tf_op jit(solution)/shard_map/ppermute | solution.py:641
  74.2 7.0 %collective-permute-start.27 = (f32[2,64,512]{2,1,0:T(8,128)S(1)}, f32[2,64,512]{2,1,0:T(8,128)S(1)}, u32[]{:S(2)}, u32[]{:S(2)}) collective-permute-start(f32[2,64,512]{2,1,0:T(8,128)S(1)} %get-tuple-element.98), channel_id=1, source_target_pairs={{4,10},{5,11},{6,2},{7,3},{8,14},{9,15},{10,6},{11,7},{20,26},{21,... | collective-permute-start | bytes 786440 | tf_op jit(solution)/shard_map/ppermute | solution.py:641
  74.9 7.7 %collective-permute-start.28 = (f32[2,64,512]{2,1,0:T(8,128)S(1)}, f32[2,64,512]{2,1,0:T(8,128)S(1)}, u32[]{:S(2)}, u32[]{:S(2)}) collective-permute-start(f32[2,64,512]{2,1,0:T(8,128)S(1)} %get-tuple-element.100), channel_id=1, source_target_pairs={{4,14},{5,15},{6,6},{7,7},{8,2},{9,3},{10,10},{11,11},{20,30},{21,... | collective-permute-start | bytes 786440 | tf_op jit(solution)/shard_map/ppermute | solution.py:641
  75.6 8.3 %collective-permute-start.29 = (f32[2,64,512]{2,1,0:T(8,128)S(1)}, f32[2,64,512]{2,1,0:T(8,128)S(1)}, u32[]{:S(2)}, u32[]{:S(2)}) collective-permute-start(f32[2,64,512]{2,1,0:T(8,128)S(1)} %get-tuple-element.102), channel_id=1, source_target_pairs={{4,2},{5,3},{6,10},{7,11},{8,6},{9,7},{10,14},{11,15},{20,18},{21,... | collective-permute-start | bytes 786440 | tf_op jit(solution)/shard_map/ppermute | solution.py:641
  78.6 20.1 %collective-permute-start.18 = (f32[2,128,256]{2,1,0:T(8,128)S(1)}, f32[2,128,256]{2,1,0:T(8,128)S(1)}, u32[]{:S(2)}, u32[]{:S(2)}) collective-permute-start(f32[2,128,256]{2,1,0:T(8,128)S(1)} %get-tuple-element.91), channel_id=1, source_target_pairs={{4,4},{5,5},{6,12},{7,13},{8,8},{9,9},{10,0},{11,1},{20,20},{21,21... | collective-permute-start | bytes 786440 | tf_op jit(solution)/shard_map/ppermute | solution.py:641
  79.9 23.6 %collective-permute-start.19 = (f32[2,128,256]{2,1,0:T(8,128)S(1)}, f32[2,128,256]{2,1,0:T(8,128)S(1)}, u32[]{:S(2)}, u32[]{:S(2)}) collective-permute-start(f32[2,128,256]{2,1,0:T(8,128)S(1)} %get-tuple-element.92), channel_id=1, source_target_pairs={{4,8},{5,9},{6,0},{7,1},{8,12},{9,13},{10,4},{11,5},{20,24},{21,25... | collective-permute-start | bytes 786440 | tf_op jit(solution)/shard_map/ppermute | solution.py:641
  81.3 22.4 %collective-permute-start.20 = (f32[2,128,256]{2,1,0:T(8,128)S(1)}, f32[2,128,256]{2,1,0:T(8,128)S(1)}, u32[]{:S(2)}, u32[]{:S(2)}) collective-permute-start(f32[2,128,256]{2,1,0:T(8,128)S(1)} %get-tuple-element.93), channel_id=1, source_target_pairs={{4,12},{5,13},{6,4},{7,5},{8,0},{9,1},{10,8},{11,9},{20,28},{21,29... | collective-permute-start | bytes 786440 | tf_op jit(solution)/shard_map/ppermute | solution.py:641
  82.6 24.8 %collective-permute-start.21 = (f32[2,128,256]{2,1,0:T(8,128)S(1)}, f32[2,128,256]{2,1,0:T(8,128)S(1)}, u32[]{:S(2)}, u32[]{:S(2)}) collective-permute-start(f32[2,128,256]{2,1,0:T(8,128)S(1)} %get-tuple-element.94), channel_id=1, source_target_pairs={{4,0},{5,1},{6,8},{7,9},{8,4},{9,5},{10,12},{11,13},{20,16},{21,17... | collective-permute-start | bytes 786440 | tf_op jit(solution)/shard_map/ppermute | solution.py:641
  83.9 23.5 %collective-permute-start.30 = (f32[2,64,512]{2,1,0:T(8,128)S(1)}, f32[2,64,512]{2,1,0:T(8,128)S(1)}, u32[]{:S(2)}, u32[]{:S(2)}) collective-permute-start(f32[2,64,512]{2,1,0:T(8,128)S(1)} %collective-permute-done.26.refs_8_), channel_id=1, source_target_pairs={{0,1},{1,0},{2,3},{3,2},{4,5},{5,4},{6,7},{7,6},{8,9},{9,8},{10,11... | collective-permute-start | bytes 786440 | tf_op jit(solution)/shard_map/ppermute | solution.py:644
  98.8 9.1 %collective-permute-start.31 = (f32[2,64,512]{2,1,0:T(8,128)S(1)}, f32[2,64,512]{2,1,0:T(8,128)S(1)}, u32[]{:S(2)}, u32[]{:S(2)}) collective-permute-start(f32[2,64,512]{2,1,0:T(8,128)S(1)} %collective-permute-done.27.refs_9_), channel_id=1, source_target_pairs={{0,1},{1,0},{2,3},{3,2},{4,5},{5,4},{6,7},{7,6},{8,9},{9,8},{10,11... | collective-permute-start | bytes 786440 | tf_op jit(solution)/shard_map/ppermute | solution.py:644
  103.6 4.4 %collective-permute-start.32 = (f32[2,64,512]{2,1,0:T(8,128)S(1)}, f32[2,64,512]{2,1,0:T(8,128)S(1)}, u32[]{:S(2)}, u32[]{:S(2)}) collective-permute-start(f32[2,64,512]{2,1,0:T(8,128)S(1)} %collective-permute-done.28.refs_10_), channel_id=1, source_target_pairs={{0,1},{1,0},{2,3},{3,2},{4,5},{5,4},{6,7},{7,6},{8,9},{9,8},{10,11... | collective-permute-start | bytes 786440 | tf_op jit(solution)/shard_map/ppermute | solution.py:644
  103.6 4.8 %collective-permute-start.33 = (f32[2,64,512]{2,1,0:T(8,128)S(1)}, f32[2,64,512]{2,1,0:T(8,128)S(1)}, u32[]{:S(2)}, u32[]{:S(2)}) collective-permute-start(f32[2,64,512]{2,1,0:T(8,128)S(1)} %collective-permute-done.29.refs_11_), channel_id=1, source_target_pairs={{0,1},{1,0},{2,3},{3,2},{4,5},{5,4},{6,7},{7,6},{8,9},{9,8},{10,11... | collective-permute-start | bytes 786440 | tf_op jit(solution)/shard_map/ppermute | solution.py:644
  107.4 1.9 %collective-permute-start.23 = (f32[2,128,256]{2,1,0:T(8,128)S(1)}, f32[2,128,256]{2,1,0:T(8,128)S(1)}, u32[]{:S(2)}, u32[]{:S(2)}) collective-permute-start(f32[2,128,256]{2,1,0:T(8,128)S(1)} %collective-permute-done.19.refs_1_), channel_id=1, source_target_pairs={{0,1},{1,0},{2,3},{3,2},{4,5},{5,4},{6,7},{7,6},{8,9},{9,8},{10,11... | collective-permute-start | bytes 786440 | tf_op jit(solution)/shard_map/ppermute | solution.py:644
  108.0 2.1 %collective-permute-start.25 = (f32[2,128,256]{2,1,0:T(8,128)S(1)}, f32[2,128,256]{2,1,0:T(8,128)S(1)}, u32[]{:S(2)}, u32[]{:S(2)}) collective-permute-start(f32[2,128,256]{2,1,0:T(8,128)S(1)} %collective-permute-done.21.refs_3_), channel_id=1, source_target_pairs={{0,1},{1,0},{2,3},{3,2},{4,5},{5,4},{6,7},{7,6},{8,9},{9,8},{10,11... | collective-permute-start | bytes 786440 | tf_op jit(solution)/shard_map/ppermute | solution.py:644
  (10 other events, 72.8 us)

commit v4 on v3

--- a/solution.py
+++ b/solution.py
@@ -17,11 +17,11 @@
 smem = pltpu.MemorySpace.SMEM
 
 
-def halves(table):
+def halves(table, axis):
     table = table.astype(np.float64)
     upper = table.astype(ml_dtypes.bfloat16)
     lower = (table - upper.astype(np.float64)).astype(ml_dtypes.bfloat16)
-    return np.stack([upper, lower])
+    return np.concatenate([upper, upper, lower], axis=axis)
 
 
 def circle(length):
@@ -36,14 +36,14 @@
     cosine, sine = circle(length)
     forward = np.block([[cosine, sine], [-sine, cosine]])
     inverse = np.block([[cosine, -sine], [sine, cosine]])
-    return halves(forward), halves(inverse)
+    return halves(forward, 1), halves(inverse, 1)
 
 
 def row_tables(length):
     cosine, sine = circle(length)
     forward = np.block([[cosine, -sine], [sine, cosine]])
     inverse = np.block([[cosine.T, sine.T], [-sine.T, cosine.T]])
-    return halves(forward), halves(inverse)
+    return halves(forward, 0), halves(inverse, 0)
 
 
 def twiddles(length):
@@ -78,12 +78,12 @@
 
 def right_dot(value, table):
     upper, lower = split(value)
-    return dot(upper, table[0]) + dot(lower, table[0]) + dot(upper, table[1])
+    return dot(jnp.concatenate([upper, lower, upper], axis=1), table[...])
 
 
 def left_dot(table, value):
     upper, lower = split(value)
-    return dot(table[0], upper) + dot(table[0], lower) + dot(table[1], upper)
+    return dot(table[...], jnp.concatenate([upper, lower, upper], axis=0))
 
 
 def times(first, second):

time: 115 us -> 115 us (level)
  no operation moved by 1% of the time
where the time goes in v4:
time: 115 us
  waiting for transfers between devices  42.9 us (37%)
  starting transfers between devices  37.7 us (33%)
  Pallas kernels  29.4 us (26%)
  other arithmetic  2.13 us (2%)
  local copies, waits for them, and re-layouts  2.06 us (2%)
    ppermute x17, starting transfers between devices, move(): return lax.ppermute(value, line_axes, pairs)  29.8 us
    ppermute x17, waiting for transfers between devices, move(): return lax.ppermute(value, line_axes, pairs)  29.7 us
    pallas_call x8, Pallas kernels, at_home(): pl.pallas_call(kernel, out_shape=[floats(*shape) for shape in outs], in_s...  15.5 us
    ppermute x15, waiting for transfers between devices, swap(): lax.ppermute(value, 'batch', [(i, (i + 1) % cores) for i in range(cores)])  7.07 us
    pallas_call x4, Pallas kernels, launch_of(): pl.pallas_call(functools.partial(launch_kernel, plan, j), out_shape=[floa...  5.37 us
    ppermute x1, waiting for transfers between devices, on_device(): lax.ppermute(part, 'row', [(i, (i + 1) % number) for i in range(number)])  4.69 us
    pallas_call x1, Pallas kernels, on_device(): pl.pallas_call(functools.partial(settle_kernel, plan), out_shape=jax.Shap...  4.46 us
    pallas_call x4, Pallas kernels, patch_of(): pl.pallas_call(functools.partial(patch_kernel, plan, j), out_shape=floats...  3.26 us
  transfers between devices with their start and end apart: 34, of which 15 were waited for; matrix products, arithmetic and copies ran while one was open for 0% of the time, Pallas kernels for 13%

profile of v4, /device:TPU:0, one launch (start us, length us, event | category | flops | bytes accessed | tf_op | source)
XLA Modules:
  0.0 114.7 jit_solution(14487321035748455279)
XLA Ops:
  2.0 3.1 %collective-permute-start.3 = (f32[2,64,512]{2,1,0:T(8,128)S(1)}, f32[2,64,512]{2,1,0:T(8,128)S(1)}, u32[]{:S(2)}, u32[]{:S(2)}) collective-permute-start(f32[2,64,512]{2,1,0:T(8,128)S(1)} %slice_select_fusion), channel_id=1, source_target_pairs={{0,4},{4,8},{8,12},{12,0},{1,5},{5,9},{9,13},{13,1},{2,6},{6,10},{... | collective-permute-start | bytes 786440 | tf_op jit(solution)/shard_map/ppermute | solution.py:661
  7.9 1.6 %collective-permute-start.1 = (f32[1,64,512]{2,1,0:T(8,128)S(1)}, f32[1,64,512]{2,1,0:T(8,128)S(1)}, u32[]{:S(2)}, u32[]{:S(2)}) collective-permute-start(f32[1,64,512]{2,1,0:T(8,128)S(1)} %bitcast.11), channel_id=1, source_target_pairs={{0,4},{4,8},{8,12},{12,0},{1,5},{5,9},{9,13},{13,1},{2,6},{6,10},{... | collective-permute-start | bytes 393224 | tf_op jit(solution)/shard_map/ppermute | solution.py:695
  9.5 4.7 %collective-permute-done.3.above = f32[2,64,512]{2,1,0:T(8,128)S(1)} collective-permute-done((f32[2,64,512]{2,1,0:T(8,128)S(1)}, f32[2,64,512]{2,1,0:T(8,128)S(1)}, u32[]{:S(2)}, u32[]{:S(2)}) %collective-permute-start.3) | collective-permute-done | bytes 262176 | tf_op jit(solution)/shard_map/ppermute | solution.py:661
  14.7 1.5 %collective-permute-done.1 = f32[1,64,512]{2,1,0:T(8,128)S(1)} collective-permute-done((f32[1,64,512]{2,1,0:T(8,128)S(1)}, f32[1,64,512]{2,1,0:T(8,128)S(1)}, u32[]{:S(2)}, u32[]{:S(2)}) %collective-permute-start.1) | collective-permute-done | bytes 131104 | tf_op jit(solution)/shard_map/ppermute | solution.py:695
  16.2 2.6 %collective-permute-start.2 = (f32[2,64,512]{2,1,0:T(8,128)S(1)}, f32[2,64,512]{2,1,0:T(8,128)S(1)}, u32[]{:S(2)}, u32[]{:S(2)}) collective-permute-start(f32[2,64,512]{2,1,0:T(8,128)S(1)} %pad_maximum_fusion), channel_id=1, source_target_pairs={{12,4},{13,5},{14,6},{15,7},{0,8},{1,9},{2,10},{3,11},{28,20},{29,... | collective-permute-start | bytes 786440 | tf_op jit(solution)/shard_map/ppermute | solution.py:641
  21.4 1.3 %shard_map.119 = (f32[2,128,256]{2,1,0:T(8,128)S(1)}, f32[2,128,512]{2,1,0:T(8,128)S(1)}) custom-call(s32[11]{0:T(128)S(1)} %pad_add_fusion.1.info, f32[1,2,128,2048]{3,2,1,0:T(8,128)S(1)} %copy-done, f32[1,2,128,2048]{3,2,1,0:T(8,128)S(1)} %copy-done, f32[2,64,512]{2,1,0:T(8,128)S(1)} %collective-permute-done.3.above, ...), custom_call_target="tpu_custom_call" | custom-call | tf_op jit(solution)/shard_map/pallas_call | solution.py:718
  25.1 5.1 %collective-permute-start.10 = (f32[2,128,256]{2,1,0:T(8,128)S(1)}, f32[2,128,256]{2,1,0:T(8,128)S(1)}, u32[]{:S(2)}, u32[]{:S(2)}) collective-permute-start(f32[2,128,256]{2,1,0:T(8,128)S(1)} %get-tuple-element.59), channel_id=1, source_target_pairs={{4,4},{5,5},{12,6},{13,7},{8,8},{9,9},{0,10},{1,11},{20,20},{21,21... | collective-permute-start | bytes 786440 | tf_op jit(solution)/shard_map/ppermute | solution.py:641
  30.2 1.3 %shard_map.120 = (f32[2,128,256]{2,1,0:T(8,128)S(1)}, f32[2,128,512]{2,1,0:T(8,128)S(1)}) custom-call(s32[11]{0:T(128)S(1)} %pad_add_fusion.1.info, f32[1,2,128,2048]{3,2,1,0:T(8,128)S(1)} %copy-done, f32[1,2,128,2048]{3,2,1,0:T(8,128)S(1)} %copy-done, f32[2,64,512]{2,1,0:T(8,128)S(1)} %collective-permute-done.3.above, ...), custom_call_target="tpu_custom_call" | custom-call | tf_op jit(solution)/shard_map/pallas_call | solution.py:718
  31.5 1.4 %collective-permute-start.11 = (f32[2,128,256]{2,1,0:T(8,128)S(1)}, f32[2,128,256]{2,1,0:T(8,128)S(1)}, u32[]{:S(2)}, u32[]{:S(2)}) collective-permute-start(f32[2,128,256]{2,1,0:T(8,128)S(1)} %get-tuple-element.61), channel_id=1, source_target_pairs={{8,4},{9,5},{0,6},{1,7},{12,8},{13,9},{4,10},{5,11},{24,20},{25,21... | collective-permute-start | bytes 786440 | tf_op jit(solution)/shard_map/ppermute | solution.py:641
  33.0 1.3 %shard_map.121 = (f32[2,128,256]{2,1,0:T(8,128)S(1)}, f32[2,128,512]{2,1,0:T(8,128)S(1)}) custom-call(s32[11]{0:T(128)S(1)} %pad_add_fusion.1.info, f32[1,2,128,2048]{3,2,1,0:T(8,128)S(1)} %copy-done, f32[1,2,128,2048]{3,2,1,0:T(8,128)S(1)} %copy-done, f32[2,64,512]{2,1,0:T(8,128)S(1)} %collective-permute-done.3.above, ...), custom_call_target="tpu_custom_call" | custom-call | tf_op jit(solution)/shard_map/pallas_call | solution.py:718
  34.4 1.3 %shard_map.122 = (f32[2,128,256]{2,1,0:T(8,128)S(1)}, f32[2,128,512]{2,1,0:T(8,128)S(1)}) custom-call(s32[11]{0:T(128)S(1)} %pad_add_fusion.1.info, f32[1,2,128,2048]{3,2,1,0:T(8,128)S(1)} %copy-done, f32[1,2,128,2048]{3,2,1,0:T(8,128)S(1)} %copy-done, f32[2,64,512]{2,1,0:T(8,128)S(1)} %collective-permute-done.3.above, ...), custom_call_target="tpu_custom_call" | custom-call | tf_op jit(solution)/shard_map/pallas_call | solution.py:718
  37.2 4.1 %collective-permute-done.11.refs_1_ = f32[2,128,256]{2,1,0:T(8,128)S(1)} collective-permute-done((f32[2,128,256]{2,1,0:T(8,128)S(1)}, f32[2,128,256]{2,1,0:T(8,128)S(1)}, u32[]{:S(2)}, u32[]{:S(2)}) %collective-permute-start.11) | collective-permute-done | bytes 262176 | tf_op jit(solution)/shard_map/ppermute | solution.py:641
  41.3 4.9 %collective-permute-start.13 = (f32[2,128,256]{2,1,0:T(8,128)S(1)}, f32[2,128,256]{2,1,0:T(8,128)S(1)}, u32[]{:S(2)}, u32[]{:S(2)}) collective-permute-start(f32[2,128,256]{2,1,0:T(8,128)S(1)} %get-tuple-element.76), channel_id=1, source_target_pairs={{0,4},{1,5},{8,6},{9,7},{4,8},{5,9},{12,10},{13,11},{16,20},{17,21... | collective-permute-start | bytes 786440 | tf_op jit(solution)/shard_map/ppermute | solution.py:641
  46.2 5.1 %collective-permute-start.12 = (f32[2,128,256]{2,1,0:T(8,128)S(1)}, f32[2,128,256]{2,1,0:T(8,128)S(1)}, u32[]{:S(2)}, u32[]{:S(2)}) collective-permute-start(f32[2,128,256]{2,1,0:T(8,128)S(1)} %get-tuple-element.75), channel_id=1, source_target_pairs={{12,4},{13,5},{4,6},{5,7},{0,8},{1,9},{8,10},{9,11},{28,20},{29,21... | collective-permute-start | bytes 786440 | tf_op jit(solution)/shard_map/ppermute | solution.py:641
  51.3 2.1 %shard_map.123.field = f32[2,512,256]{2,1,0:T(8,128)S(1)} custom-call(s32[3]{0:T(128)S(1)} %pad_add_fusion.info, f32[64,512]{1,0:T(8,128)S(1)} %get-tuple-element.66.refs_0_, f32[64,512]{1,0:T(8,128)S(1)} %get-tuple-element.107.refs_1_, f32[64,512]{1,0:T(8,128)S(1)} %bitcast.13, f32[64,512]{1,0:T(8,128)S(1)} %get-tuple-element.58.refs_3_), custom_call_target="tpu_custom_call" | custom-call | tf_op jit(solution)/shard_map/pallas_call | solution.py:780
  53.4 2.8 %collective-permute-done.12.refs_2_ = f32[2,128,256]{2,1,0:T(8,128)S(1)} collective-permute-done((f32[2,128,256]{2,1,0:T(8,128)S(1)}, f32[2,128,256]{2,1,0:T(8,128)S(1)}, u32[]{:S(2)}, u32[]{:S(2)}) %collective-permute-start.12) | collective-permute-done | bytes 262176 | tf_op jit(solution)/shard_map/ppermute | solution.py:641
  56.3 2.3 %shard_map.129 = (f32[2,256,256]{2,1,0:T(8,128)S(1)}, f32[2,256,256]{2,1,0:T(8,128)S(1)}) custom-call(s32[3]{0:T(128)S(1)} %pad_add_fusion.info, bf16[256,768]{1,0:T(8,128)(2,1)S(1)} %copy-done.6, bf16[256,768]{1,0:T(8,128)(2,1)S(1)} %copy-done.5, f32[4,2,128,128]{3,2,1,0:T(8,128)S(1)} %copy-done.3, f32[2,512,256]{2,1,0:T(8,128)S(1)} %shard_map.123.field, ...), custom_call_target="tpu_custom_call" | custom-call | tf_op jit(solution)/shard_map/pallas_call | solution.py:780
  58.7 1.9 %collective-permute-done.14.other = f32[2,256,256]{2,1,0:T(8,128)S(1)} collective-permute-done((f32[2,256,256]{2,1,0:T(8,128)S(1)}, f32[2,256,256]{2,1,0:T(8,128)S(1)}, u32[]{:S(2)}, u32[]{:S(2)}) %collective-permute-start.14) | collective-permute-done | bytes 524320 | tf_op jit(solution)/shard_map/ppermute | solution.py:644
  60.6 2.2 %shard_map.130 = (f32[2,256,512]{2,1,0:T(8,128)S(1)}, f32[2,256,256]{2,1,0:T(8,128)S(1)}, f32[2,256,256]{2,1,0:T(8,128)S(1)}) custom-call(s32[3]{0:T(128)S(1)} %pad_add_fusion.info, bf16[768,256]{1,0:T(8,128)(2,1)S(1)} %copy-done.1, bf16[768,256]{1,0:T(8,128)(2,1)S(1)} %copy-done.4, f32[8,128]{1,0:T(8,128)S(1)} %copy-done.8, ...), custom_call_target="tpu_custom_call" | custom-call | tf_op jit(solution)/shard_map/pallas_call | solution.py:780
  62.9 1.6 %shard_map.128.target = f32[512,256]{1,0:T(8,128)S(1)} custom-call(s32[3]{0:T(128)S(1)} %pad_add_fusion.info, f32[3,64,512]{2,1,0:T(8,128)S(1)} %collective-permute-done.6.refs_0_, f32[3,64,512]{2,1,0:T(8,128)S(1)} %collective-permute-done.7.refs_1_, f32[3,64,512]{2,1,0:T(8,128)S(1)} %collective-permute-done.8.refs_2_, ...), custom_call_target="tpu_custom_call" | custom-call | tf_op jit(solution)/shard_map/pallas_call | solution.py:780
  64.7 2.3 %shard_map.131 = (f32[2,256,256]{2,1,0:T(8,128)S(1)}, f32[2,256,256]{2,1,0:T(8,128)S(1)}) custom-call(s32[3]{0:T(128)S(1)} %pad_add_fusion.info, bf16[256,768]{1,0:T(8,128)(2,1)S(1)} %copy-done.6, bf16[256,768]{1,0:T(8,128)(2,1)S(1)} %copy-done.5, f32[4,2,128,128]{3,2,1,0:T(8,128)S(1)} %copy-done.3, f32[512,256]{1,0:T(8,128)S(1)} %shard_map.128.target, ...), custom_call_target="tpu_custom_call" | custom-call | tf_op jit(solution)/shard_map/pallas_call | solution.py:780
  67.3 1.7 %collective-permute-done.16.other = f32[2,256,256]{2,1,0:T(8,128)S(1)} collective-permute-done((f32[2,256,256]{2,1,0:T(8,128)S(1)}, f32[2,256,256]{2,1,0:T(8,128)S(1)}, u32[]{:S(2)}, u32[]{:S(2)}) %collective-permute-start.16) | collective-permute-done | bytes 524320 | tf_op jit(solution)/shard_map/ppermute | solution.py:644
  69.0 1.5 %shard_map.132 = (f32[2,64,512]{2,1,0:T(8,128)S(1)}, f32[2,64,512]{2,1,0:T(8,128)S(1)}, f32[2,64,512]{2,1,0:T(8,128)S(1)}, f32[2,64,512]{2,1,0:T(8,128)S(1)}, f32[2,256,512]{2,1,0:T(8,128)S(1)}) custom-call(s32[3]{0:T(128)S(1)} %pad_add_fusion.info, bf16[768,256]{1,0:T(8,128)(2,1)S(1)} %copy-done.4, f32[8,128]{1,0:T(8,128)S(1)} %copy-done.8, ...), custom_call_target="tpu_custom_call" | custom-call | tf_op jit(solution)/shard_map/pallas_call | solution.py:780
  72.0 1.7 %collective-permute-done.17.other = f32[2,256,256]{2,1,0:T(8,128)S(1)} collective-permute-done((f32[2,256,256]{2,1,0:T(8,128)S(1)}, f32[2,256,256]{2,1,0:T(8,128)S(1)}, u32[]{:S(2)}, u32[]{:S(2)}) %collective-permute-start.17) | collective-permute-done | bytes 524320 | tf_op jit(solution)/shard_map/ppermute | solution.py:644
  76.4 2.3 %shard_map.134 = (f32[2,128,256]{2,1,0:T(8,128)S(1)}, f32[2,128,256]{2,1,0:T(8,128)S(1)}, f32[2,128,256]{2,1,0:T(8,128)S(1)}, f32[2,128,256]{2,1,0:T(8,128)S(1)}) custom-call(s32[3]{0:T(128)S(1)} %pad_add_fusion.info, bf16[256,768]{1,0:T(8,128)(2,1)S(1)} %copy-done.6, bf16[256,768]{1,0:T(8,128)(2,1)S(1)} %copy-done.5, f32[4,2,128,128]{3,2,1,0:T(8,128)S(1)} %copy-done.3, ...), custom_call_target="tpu_custom_call" | custom-call | tf_op jit(solution)/shard_map/pallas_call | solution.py:780
  78.7 1.3 %collective-permute-start.18 = (f32[2,128,256]{2,1,0:T(8,128)S(1)}, f32[2,128,256]{2,1,0:T(8,128)S(1)}, u32[]{:S(2)}, u32[]{:S(2)}) collective-permute-start(f32[2,128,256]{2,1,0:T(8,128)S(1)} %get-tuple-element.91), channel_id=1, source_target_pairs={{4,4},{5,5},{6,12},{7,13},{8,8},{9,9},{10,0},{11,1},{20,20},{21,21... | collective-permute-start | bytes 786440 | tf_op jit(solution)/shard_map/ppermute | solution.py:641
  80.0 1.3 %collective-permute-start.19 = (f32[2,128,256]{2,1,0:T(8,128)S(1)}, f32[2,128,256]{2,1,0:T(8,128)S(1)}, u32[]{:S(2)}, u32[]{:S(2)}) collective-permute-start(f32[2,128,256]{2,1,0:T(8,128)S(1)} %get-tuple-element.92), channel_id=1, source_target_pairs={{4,8},{5,9},{6,0},{7,1},{8,12},{9,13},{10,4},{11,5},{20,24},{21,25... | collective-permute-start | bytes 786440 | tf_op jit(solution)/shard_map/ppermute | solution.py:641
  81.4 1.3 %collective-permute-start.20 = (f32[2,128,256]{2,1,0:T(8,128)S(1)}, f32[2,128,256]{2,1,0:T(8,128)S(1)}, u32[]{:S(2)}, u32[]{:S(2)}) collective-permute-start(f32[2,128,256]{2,1,0:T(8,128)S(1)} %get-tuple-element.93), channel_id=1, source_target_pairs={{4,12},{5,13},{6,4},{7,5},{8,0},{9,1},{10,8},{11,9},{20,28},{21,29... | collective-permute-start | bytes 786440 | tf_op jit(solution)/shard_map/ppermute | solution.py:641
  84.3 14.7 %collective-permute-done.18.refs_0_ = f32[2,128,256]{2,1,0:T(8,128)S(1)} collective-permute-done((f32[2,128,256]{2,1,0:T(8,128)S(1)}, f32[2,128,256]{2,1,0:T(8,128)S(1)}, u32[]{:S(2)}, u32[]{:S(2)}) %collective-permute-start.18) | collective-permute-done | bytes 262176 | tf_op jit(solution)/shard_map/ppermute | solution.py:641
  98.9 4.8 %collective-permute-done.19.refs_1_ = f32[2,128,256]{2,1,0:T(8,128)S(1)} collective-permute-done((f32[2,128,256]{2,1,0:T(8,128)S(1)}, f32[2,128,256]{2,1,0:T(8,128)S(1)}, u32[]{:S(2)}, u32[]{:S(2)}) %collective-permute-start.19) | collective-permute-done | bytes 262176 | tf_op jit(solution)/shard_map/ppermute | solution.py:641
  104.3 3.3 %collective-permute-done.21.refs_3_ = f32[2,128,256]{2,1,0:T(8,128)S(1)} collective-permute-done((f32[2,128,256]{2,1,0:T(8,128)S(1)}, f32[2,128,256]{2,1,0:T(8,128)S(1)}, u32[]{:S(2)}, u32[]{:S(2)}) %collective-permute-start.21) | collective-permute-done | bytes 262176 | tf_op jit(solution)/shard_map/ppermute | solution.py:641
  110.2 4.5 %shard_map.135 = f32[1,2,128,2048]{3,2,1,0:T(8,128)} custom-call(s32[11]{0:T(128)S(1)} %pad_add_fusion.1.info, bf16[768,256]{1,0:T(8,128)(2,1)S(1)} %copy-done.4, f32[8,128]{1,0:T(8,128)S(1)} %copy-done.8, f32[2,128,256]{2,1,0:T(8,128)S(1)} %collective-permute-done.18.refs_0_, f32[2,128,256]{2,1,0:T(8,128)S(1)} %collective-permute-done.19.refs_1_, ...), custom_call_target="tpu_custom_call" | custom-call | tf_op jit(solution)/shard_map/pallas_call | solution.py:854
  (80 shorter events, 21.2 us)
Async XLA Ops:
  2.0 12.2 %collective-permute-start.3 = (f32[2,64,512]{2,1,0:T(8,128)S(1)}, f32[2,64,512]{2,1,0:T(8,128)S(1)}, u32[]{:S(2)}, u32[]{:S(2)}) collective-permute-start(f32[2,64,512]{2,1,0:T(8,128)S(1)} %slice_select_fusion), channel_id=1, source_target_pairs={{0,4},{4,8},{8,12},{12,0},{1,5},{5,9},{9,13},{13,1},{2,6},{6,10},{... | collective-permute-start | bytes 786440 | tf_op jit(solution)/shard_map/ppermute | solution.py:661
  7.9 8.3 %collective-permute-start.1 = (f32[1,64,512]{2,1,0:T(8,128)S(1)}, f32[1,64,512]{2,1,0:T(8,128)S(1)}, u32[]{:S(2)}, u32[]{:S(2)}) collective-permute-start(f32[1,64,512]{2,1,0:T(8,128)S(1)} %bitcast.11), channel_id=1, source_target_pairs={{0,4},{4,8},{8,12},{12,0},{1,5},{5,9},{9,13},{13,1},{2,6},{6,10},{... | collective-permute-start | bytes 393224 | tf_op jit(solution)/shard_map/ppermute | solution.py:695
  9.5 9.4 %collective-permute-start.5 = (f32[2,64,512]{2,1,0:T(8,128)S(1)}, f32[2,64,512]{2,1,0:T(8,128)S(1)}, u32[]{:S(2)}, u32[]{:S(2)}) collective-permute-start(f32[2,64,512]{2,1,0:T(8,128)S(1)} %get-tuple-element.68), channel_id=1, source_target_pairs={{0,1},{1,0},{2,3},{3,2},{4,5},{5,4},{6,7},{7,6},{8,9},{9,8},{10,11... | collective-permute-start | bytes 786440 | tf_op jit(solution)/shard_map/ppermute | solution.py:644
  14.2 7.1 %collective-permute-start.4 = (f32[2,64,512]{2,1,0:T(8,128)S(1)}, f32[2,64,512]{2,1,0:T(8,128)S(1)}, u32[]{:S(2)}, u32[]{:S(2)}) collective-permute-start(f32[2,64,512]{2,1,0:T(8,128)S(1)} %collective-permute-done.3.above), channel_id=1, source_target_pairs={{0,1},{1,0},{2,3},{3,2},{4,5},{5,4},{6,7},{7,6},{8,9},{9,8},{10,11... | collective-permute-start | bytes 786440 | tf_op jit(solution)/shard_map/ppermute | solution.py:644
  14.2 4.7 %collective-permute-start = (s32[4]{0:T(128)S(1)}, s32[4]{0:T(128)S(1)}, u32[]{:S(2)}, u32[]{:S(2)}) collective-permute-start(s32[4]{0:T(128)S(1)} %pad_add_fusion.2), channel_id=1, source_target_pairs={{0,1},{1,0},{2,3},{3,2},{4,5},{5,4},{6,7},{7,6},{8,9},{9,8},{10,11... | collective-permute-start | bytes 56 | tf_op jit(solution)/shard_map/ppermute | solution.py:644
  16.2 16.8 %collective-permute-start.2 = (f32[2,64,512]{2,1,0:T(8,128)S(1)}, f32[2,64,512]{2,1,0:T(8,128)S(1)}, u32[]{:S(2)}, u32[]{:S(2)}) collective-permute-start(f32[2,64,512]{2,1,0:T(8,128)S(1)} %pad_maximum_fusion), channel_id=1, source_target_pairs={{12,4},{13,5},{14,6},{15,7},{0,8},{1,9},{2,10},{3,11},{28,20},{29,... | collective-permute-start | bytes 786440 | tf_op jit(solution)/shard_map/ppermute | solution.py:641
  20.6 15.1 %collective-permute-start.7 = (f32[3,64,512]{2,1,0:T(8,128)S(1)}, f32[3,64,512]{2,1,0:T(8,128)S(1)}, u32[]{:S(2)}, u32[]{:S(2)}) collective-permute-start(f32[3,64,512]{2,1,0:T(8,128)S(1)} %shard_map.125), channel_id=1, source_target_pairs={{10,4},{11,5},{2,6},{3,7},{14,8},{15,9},{6,10},{7,11},{26,20},{27,... | collective-permute-start | bytes 1179656 | tf_op jit(solution)/shard_map/ppermute | solution.py:641
  22.7 13.7 %collective-permute-start.6 = (f32[3,64,512]{2,1,0:T(8,128)S(1)}, f32[3,64,512]{2,1,0:T(8,128)S(1)}, u32[]{:S(2)}, u32[]{:S(2)}) collective-permute-start(f32[3,64,512]{2,1,0:T(8,128)S(1)} %shard_map.124), channel_id=1, source_target_pairs={{6,4},{7,5},{14,6},{15,7},{10,8},{11,9},{2,10},{3,11},{22,20},{23,... | collective-permute-start | bytes 1179656 | tf_op jit(solution)/shard_map/ppermute | solution.py:641
  25.1 12.1 %collective-permute-start.10 = (f32[2,128,256]{2,1,0:T(8,128)S(1)}, f32[2,128,256]{2,1,0:T(8,128)S(1)}, u32[]{:S(2)}, u32[]{:S(2)}) collective-permute-start(f32[2,128,256]{2,1,0:T(8,128)S(1)} %get-tuple-element.59), channel_id=1, source_target_pairs={{4,4},{5,5},{12,6},{13,7},{8,8},{9,9},{0,10},{1,11},{20,20},{21,21... | collective-permute-start | bytes 786440 | tf_op jit(solution)/shard_map/ppermute | solution.py:641
  31.5 9.7 %collective-permute-start.11 = (f32[2,128,256]{2,1,0:T(8,128)S(1)}, f32[2,128,256]{2,1,0:T(8,128)S(1)}, u32[]{:S(2)}, u32[]{:S(2)}) collective-permute-start(f32[2,128,256]{2,1,0:T(8,128)S(1)} %get-tuple-element.61), channel_id=1, source_target_pairs={{8,4},{9,5},{0,6},{1,7},{12,8},{13,9},{4,10},{5,11},{24,20},{25,21... | collective-permute-start | bytes 786440 | tf_op jit(solution)/shard_map/ppermute | solution.py:641
  35.8 20.5 %collective-permute-start.9 = (f32[3,64,512]{2,1,0:T(8,128)S(1)}, f32[3,64,512]{2,1,0:T(8,128)S(1)}, u32[]{:S(2)}, u32[]{:S(2)}) collective-permute-start(f32[3,64,512]{2,1,0:T(8,128)S(1)} %shard_map.127), channel_id=1, source_target_pairs={{2,4},{3,5},{10,6},{11,7},{6,8},{7,9},{14,10},{15,11},{18,20},{19,... | collective-permute-start | bytes 1179656 | tf_op jit(solution)/shard_map/ppermute | solution.py:641
  36.5 19.8 %collective-permute-start.8 = (f32[3,64,512]{2,1,0:T(8,128)S(1)}, f32[3,64,512]{2,1,0:T(8,128)S(1)}, u32[]{:S(2)}, u32[]{:S(2)}) collective-permute-start(f32[3,64,512]{2,1,0:T(8,128)S(1)} %shard_map.126), channel_id=1, source_target_pairs={{14,4},{15,5},{6,6},{7,7},{2,8},{3,9},{10,10},{11,11},{30,20},{31,... | collective-permute-start | bytes 1179656 | tf_op jit(solution)/shard_map/ppermute | solution.py:641
  41.3 12.2 %collective-permute-start.13 = (f32[2,128,256]{2,1,0:T(8,128)S(1)}, f32[2,128,256]{2,1,0:T(8,128)S(1)}, u32[]{:S(2)}, u32[]{:S(2)}) collective-permute-start(f32[2,128,256]{2,1,0:T(8,128)S(1)} %get-tuple-element.76), channel_id=1, source_target_pairs={{0,4},{1,5},{8,6},{9,7},{4,8},{5,9},{12,10},{13,11},{16,20},{17,21... | collective-permute-start | bytes 786440 | tf_op jit(solution)/shard_map/ppermute | solution.py:641
  46.2 10.0 %collective-permute-start.12 = (f32[2,128,256]{2,1,0:T(8,128)S(1)}, f32[2,128,256]{2,1,0:T(8,128)S(1)}, u32[]{:S(2)}, u32[]{:S(2)}) collective-permute-start(f32[2,128,256]{2,1,0:T(8,128)S(1)} %get-tuple-element.75), channel_id=1, source_target_pairs={{12,4},{13,5},{4,6},{5,7},{0,8},{1,9},{8,10},{9,11},{28,20},{29,21... | collective-permute-start | bytes 786440 | tf_op jit(solution)/shard_map/ppermute | solution.py:641
  58.6 2.0 %collective-permute-start.14 = (f32[2,256,256]{2,1,0:T(8,128)S(1)}, f32[2,256,256]{2,1,0:T(8,128)S(1)}, u32[]{:S(2)}, u32[]{:S(2)}) collective-permute-start(f32[2,256,256]{2,1,0:T(8,128)S(1)} %get-tuple-element.82), channel_id=1, source_target_pairs={{0,1},{1,0},{2,3},{3,2},{4,5},{5,4},{6,7},{7,6},{8,9},{9,8},{10,11... | collective-permute-start | bytes 1572872 | tf_op jit(solution)/shard_map/ppermute | solution.py:644
  62.7 2.0 %collective-permute-start.15 = (f32[2,256,256]{2,1,0:T(8,128)S(1)}, f32[2,256,256]{2,1,0:T(8,128)S(1)}, u32[]{:S(2)}, u32[]{:S(2)}) collective-permute-start(f32[2,256,256]{2,1,0:T(8,128)S(1)} %get-tuple-element.84), channel_id=1, source_target_pairs={{0,1},{1,0},{2,3},{3,2},{4,5},{5,4},{6,7},{7,6},{8,9},{9,8},{10,11... | collective-permute-start | bytes 1572872 | tf_op jit(solution)/shard_map/ppermute | solution.py:644
  67.0 2.0 %collective-permute-start.16 = (f32[2,256,256]{2,1,0:T(8,128)S(1)}, f32[2,256,256]{2,1,0:T(8,128)S(1)}, u32[]{:S(2)}, u32[]{:S(2)}) collective-permute-start(f32[2,256,256]{2,1,0:T(8,128)S(1)} %get-tuple-element.86), channel_id=1, source_target_pairs={{0,1},{1,0},{2,3},{3,2},{4,5},{5,4},{6,7},{7,6},{8,9},{9,8},{10,11... | collective-permute-start | bytes 1572872 | tf_op jit(solution)/shard_map/ppermute | solution.py:644
  71.7 2.0 %collective-permute-start.17 = (f32[2,256,256]{2,1,0:T(8,128)S(1)}, f32[2,256,256]{2,1,0:T(8,128)S(1)}, u32[]{:S(2)}, u32[]{:S(2)}) collective-permute-start(f32[2,256,256]{2,1,0:T(8,128)S(1)} %get-tuple-element.90), channel_id=1, source_target_pairs={{0,1},{1,0},{2,3},{3,2},{4,5},{5,4},{6,7},{7,6},{8,9},{9,8},{10,11... | collective-permute-start | bytes 1572872 | tf_op jit(solution)/shard_map/ppermute | solution.py:644
  73.7 6.3 %collective-permute-start.26 = (f32[2,64,512]{2,1,0:T(8,128)S(1)}, f32[2,64,512]{2,1,0:T(8,128)S(1)}, u32[]{:S(2)}, u32[]{:S(2)}) collective-permute-start(f32[2,64,512]{2,1,0:T(8,128)S(1)} %get-tuple-element.96), channel_id=1, source_target_pairs={{4,6},{5,7},{6,14},{7,15},{8,10},{9,11},{10,2},{11,3},{20,22},{21,... | collective-permute-start | bytes 786440 | tf_op jit(solution)/shard_map/ppermute | solution.py:641
  74.4 7.0 %collective-permute-start.27 = (f32[2,64,512]{2,1,0:T(8,128)S(1)}, f32[2,64,512]{2,1,0:T(8,128)S(1)}, u32[]{:S(2)}, u32[]{:S(2)}) collective-permute-start(f32[2,64,512]{2,1,0:T(8,128)S(1)} %get-tuple-element.98), channel_id=1, source_target_pairs={{4,10},{5,11},{6,2},{7,3},{8,14},{9,15},{10,6},{11,7},{20,26},{21,... | collective-permute-start | bytes 786440 | tf_op jit(solution)/shard_map/ppermute | solution.py:641
  75.1 7.6 %collective-permute-start.28 = (f32[2,64,512]{2,1,0:T(8,128)S(1)}, f32[2,64,512]{2,1,0:T(8,128)S(1)}, u32[]{:S(2)}, u32[]{:S(2)}) collective-permute-start(f32[2,64,512]{2,1,0:T(8,128)S(1)} %get-tuple-element.100), channel_id=1, source_target_pairs={{4,14},{5,15},{6,6},{7,7},{8,2},{9,3},{10,10},{11,11},{20,30},{21,... | collective-permute-start | bytes 786440 | tf_op jit(solution)/shard_map/ppermute | solution.py:641
  75.8 8.2 %collective-permute-start.29 = (f32[2,64,512]{2,1,0:T(8,128)S(1)}, f32[2,64,512]{2,1,0:T(8,128)S(1)}, u32[]{:S(2)}, u32[]{:S(2)}) collective-permute-start(f32[2,64,512]{2,1,0:T(8,128)S(1)} %get-tuple-element.102), channel_id=1, source_target_pairs={{4,2},{5,3},{6,10},{7,11},{8,6},{9,7},{10,14},{11,15},{20,18},{21,... | collective-permute-start | bytes 786440 | tf_op jit(solution)/shard_map/ppermute | solution.py:641
  78.7 20.2 %collective-permute-start.18 = (f32[2,128,256]{2,1,0:T(8,128)S(1)}, f32[2,128,256]{2,1,0:T(8,128)S(1)}, u32[]{:S(2)}, u32[]{:S(2)}) collective-permute-start(f32[2,128,256]{2,1,0:T(8,128)S(1)} %get-tuple-element.91), channel_id=1, source_target_pairs={{4,4},{5,5},{6,12},{7,13},{8,8},{9,9},{10,0},{11,1},{20,20},{21,21... | collective-permute-start | bytes 786440 | tf_op jit(solution)/shard_map/ppermute | solution.py:641
  80.0 23.7 %collective-permute-start.19 = (f32[2,128,256]{2,1,0:T(8,128)S(1)}, f32[2,128,256]{2,1,0:T(8,128)S(1)}, u32[]{:S(2)}, u32[]{:S(2)}) collective-permute-start(f32[2,128,256]{2,1,0:T(8,128)S(1)} %get-tuple-element.92), channel_id=1, source_target_pairs={{4,8},{5,9},{6,0},{7,1},{8,12},{9,13},{10,4},{11,5},{20,24},{21,25... | collective-permute-start | bytes 786440 | tf_op jit(solution)/shard_map/ppermute | solution.py:641
  81.4 22.4 %collective-permute-start.20 = (f32[2,128,256]{2,1,0:T(8,128)S(1)}, f32[2,128,256]{2,1,0:T(8,128)S(1)}, u32[]{:S(2)}, u32[]{:S(2)}) collective-permute-start(f32[2,128,256]{2,1,0:T(8,128)S(1)} %get-tuple-element.93), channel_id=1, source_target_pairs={{4,12},{5,13},{6,4},{7,5},{8,0},{9,1},{10,8},{11,9},{20,28},{21,29... | collective-permute-start | bytes 786440 | tf_op jit(solution)/shard_map/ppermute | solution.py:641
  82.7 24.9 %collective-permute-start.21 = (f32[2,128,256]{2,1,0:T(8,128)S(1)}, f32[2,128,256]{2,1,0:T(8,128)S(1)}, u32[]{:S(2)}, u32[]{:S(2)}) collective-permute-start(f32[2,128,256]{2,1,0:T(8,128)S(1)} %get-tuple-element.94), channel_id=1, source_target_pairs={{4,0},{5,1},{6,8},{7,9},{8,4},{9,5},{10,12},{11,13},{20,16},{21,17... | collective-permute-start | bytes 786440 | tf_op jit(solution)/shard_map/ppermute | solution.py:641
  84.0 23.6 %collective-permute-start.30 = (f32[2,64,512]{2,1,0:T(8,128)S(1)}, f32[2,64,512]{2,1,0:T(8,128)S(1)}, u32[]{:S(2)}, u32[]{:S(2)}) collective-permute-start(f32[2,64,512]{2,1,0:T(8,128)S(1)} %collective-permute-done.26.refs_8_), channel_id=1, source_target_pairs={{0,1},{1,0},{2,3},{3,2},{4,5},{5,4},{6,7},{7,6},{8,9},{9,8},{10,11... | collective-permute-start | bytes 786440 | tf_op jit(solution)/shard_map/ppermute | solution.py:644
  98.9 9.1 %collective-permute-start.31 = (f32[2,64,512]{2,1,0:T(8,128)S(1)}, f32[2,64,512]{2,1,0:T(8,128)S(1)}, u32[]{:S(2)}, u32[]{:S(2)}) collective-permute-start(f32[2,64,512]{2,1,0:T(8,128)S(1)} %collective-permute-done.27.refs_9_), channel_id=1, source_target_pairs={{0,1},{1,0},{2,3},{3,2},{4,5},{5,4},{6,7},{7,6},{8,9},{9,8},{10,11... | collective-permute-start | bytes 786440 | tf_op jit(solution)/shard_map/ppermute | solution.py:644
  103.7 4.4 %collective-permute-start.32 = (f32[2,64,512]{2,1,0:T(8,128)S(1)}, f32[2,64,512]{2,1,0:T(8,128)S(1)}, u32[]{:S(2)}, u32[]{:S(2)}) collective-permute-start(f32[2,64,512]{2,1,0:T(8,128)S(1)} %collective-permute-done.28.refs_10_), channel_id=1, source_target_pairs={{0,1},{1,0},{2,3},{3,2},{4,5},{5,4},{6,7},{7,6},{8,9},{9,8},{10,11... | collective-permute-start | bytes 786440 | tf_op jit(solution)/shard_map/ppermute | solution.py:644
  103.8 4.8 %collective-permute-start.33 = (f32[2,64,512]{2,1,0:T(8,128)S(1)}, f32[2,64,512]{2,1,0:T(8,128)S(1)}, u32[]{:S(2)}, u32[]{:S(2)}) collective-permute-start(f32[2,64,512]{2,1,0:T(8,128)S(1)} %collective-permute-done.29.refs_11_), channel_id=1, source_target_pairs={{0,1},{1,0},{2,3},{3,2},{4,5},{5,4},{6,7},{7,6},{8,9},{9,8},{10,11... | collective-permute-start | bytes 786440 | tf_op jit(solution)/shard_map/ppermute | solution.py:644
  107.6 1.9 %collective-permute-start.23 = (f32[2,128,256]{2,1,0:T(8,128)S(1)}, f32[2,128,256]{2,1,0:T(8,128)S(1)}, u32[]{:S(2)}, u32[]{:S(2)}) collective-permute-start(f32[2,128,256]{2,1,0:T(8,128)S(1)} %collective-permute-done.19.refs_1_), channel_id=1, source_target_pairs={{0,1},{1,0},{2,3},{3,2},{4,5},{5,4},{6,7},{7,6},{8,9},{9,8},{10,11... | collective-permute-start | bytes 786440 | tf_op jit(solution)/shard_map/ppermute | solution.py:644
  108.1 2.1 %collective-permute-start.25 = (f32[2,128,256]{2,1,0:T(8,128)S(1)}, f32[2,128,256]{2,1,0:T(8,128)S(1)}, u32[]{:S(2)}, u32[]{:S(2)}) collective-permute-start(f32[2,128,256]{2,1,0:T(8,128)S(1)} %collective-permute-done.21.refs_3_), channel_id=1, source_target_pairs={{0,1},{1,0},{2,3},{3,2},{4,5},{5,4},{6,7},{7,6},{8,9},{9,8},{10,11... | collective-permute-start | bytes 786440 | tf_op jit(solution)/shard_map/ppermute | solution.py:644
  (12 other events, 101.7 us)

commit v5 on v4

--- a/solution.py
+++ b/solution.py
@@ -378,7 +378,7 @@
     lane = lax.broadcasted_iota(jnp.int32, (height, breadth), 1)
     line = lax.broadcasted_iota(jnp.int32, (height, breadth), 0)
     out[...] = jnp.zeros_like(out)
-    for j in range(number):
+    for i, j in enumerate(plan.order):
 
         @pl.when(info[2] == 0)
         def _():
@@ -387,21 +387,21 @@
                 first = quarter * (index % 2)
                 pair = []
                 for part in range(2):
-                    own = own_spectra[j][part, :, first : first + quarter]
-                    other = other_spectra[j][part, :, first : first + quarter]
+                    own = own_spectra[i][part, :, first : first + quarter]
+                    other = other_spectra[i][part, :, first : first + quarter]
                     pair.append(jnp.where(lower, own, other) if index < 2 else jnp.where(lower, other, own))
                 classes.append(tuple(pair))
             inner = inverse_lanes(classes, table, twiddle)
             for m in range(4):
                 columns = slice(quarter * m, quarter * (m + 1))
-                entering = (rolled[j][0, :, columns], rolled[j][1, :, columns])
+                entering = (rolled[i][0, :, columns], rolled[i][1, :, columns])
                 term = conj_times(entering, inner[m])
                 scratch[0, :, columns] = term[0]
                 scratch[1, :, columns] = term[1]
 
         @pl.when(info[2] != 0)
         def _():
-            own, other = own_terms[j][...], other_terms[j][...]
+            own, other = own_terms[i][...], other_terms[i][...]
             scratch[:, : height // 2, :] = jnp.where(lower, own, other)
             scratch[:, height // 2 :, :] = jnp.where(lower, other, own)
 
@@ -837,7 +837,8 @@
     )
     came, spectra = [None] * number, [None] * number
     for j in plan.order:
-        came[j] = move(after(found[j], other), outward(j, 1))
+        value = found[j] if j == plan.order[0] else after(found[j], other)
+        came[j] = move(value, outward(j, 1))
     for j in plan.order:
         spectra[j] = move(leaving[j], outward(j, 0))
     terms = came if terms is None else [first + second for first, second in zip(terms, came)]
@@ -845,11 +846,11 @@
     operands = [
         row_inverse,
         lane_factors,
-        *spectra,
-        *(swap(value) for value in spectra),
-        *terms,
-        *(swap(value) for value in terms),
-        *rolled,
+        *(spectra[j] for j in plan.order),
+        *(swap(spectra[j]) for j in plan.order),
+        *(terms[j] for j in plan.order),
+        *(swap(after(terms[j], leaving[0])) for j in plan.order),
+        *(rolled[j] for j in plan.order),
     ]
     return pl.pallas_call(
         functools.partial(settle_kernel, plan),

time: 115 us -> 112 us (0.974)
  waiting for transfers between devices: 42.9 us -> 39.6 us
    ppermute x17, waiting for transfers between devices: 29.7 us -> 26.9 us  [move(): return lax.ppermute(value, line_axes, pairs)]
  transfers between devices with their start and end apart: 34 -> 34, of which waited for: 15 -> 16; matrix products, arithmetic and copies ran while one was open for 0% -> 0% of each run, Pallas kernels for 13% -> 14%
where the time goes in v5:
time: 112 us; the launch traced here: 111 us
  waiting for transfers between devices  39.6 us (35%)
  starting transfers between devices  37.5 us (33%)
  Pallas kernels  29.4 us (26%)
  other arithmetic  2.13 us (2%)
  local copies, waits for them, and re-layouts  2.06 us (2%)
    ppermute x17, starting transfers between devices, move(): return lax.ppermute(value, line_axes, pairs)  29.8 us
    ppermute x17, waiting for transfers between devices, move(): return lax.ppermute(value, line_axes, pairs)  26.9 us
    pallas_call x8, Pallas kernels, at_home(): pl.pallas_call(kernel, out_shape=[floats(*shape) for shape in outs], in_s...  15.5 us
    ppermute x15, waiting for transfers between devices, swap(): lax.ppermute(value, 'batch', [(i, (i + 1) % cores) for i in range(cores)])  6.54 us
    pallas_call x4, Pallas kernels, launch_of(): pl.pallas_call(functools.partial(launch_kernel, plan, j), out_shape=[floa...  5.37 us
    ppermute x1, waiting for transfers between devices, on_device(): lax.ppermute(part, 'row', [(i, (i + 1) % number) for i in range(number)])  4.69 us
    pallas_call x1, Pallas kernels, on_device(): pl.pallas_call(functools.partial(settle_kernel, plan), out_shape=jax.Shap...  4.48 us
    pallas_call x4, Pallas kernels, patch_of(): pl.pallas_call(functools.partial(patch_kernel, plan, j), out_shape=floats...  3.26 us
  transfers between devices with their start and end apart: 34, of which 16 were waited for; matrix products, arithmetic and copies ran while one was open for 0% of the time, Pallas kernels for 14%

profile of v5, /device:TPU:0, one launch (start us, length us, event | category | flops | bytes accessed | tf_op | source)
XLA Modules:
  0.0 111.2 jit_solution(16848302080163773948)
XLA Ops:
  2.0 3.1 %collective-permute-start.3 = (f32[2,64,512]{2,1,0:T(8,128)S(1)}, f32[2,64,512]{2,1,0:T(8,128)S(1)}, u32[]{:S(2)}, u32[]{:S(2)}) collective-permute-start(f32[2,64,512]{2,1,0:T(8,128)S(1)} %slice_select_fusion), channel_id=1, source_target_pairs={{0,4},{4,8},{8,12},{12,0},{1,5},{5,9},{9,13},{13,1},{2,6},{6,10},{... | collective-permute-start | bytes 786440 | tf_op jit(solution)/shard_map/ppermute | solution.py:661
  7.9 1.6 %collective-permute-start.1 = (f32[1,64,512]{2,1,0:T(8,128)S(1)}, f32[1,64,512]{2,1,0:T(8,128)S(1)}, u32[]{:S(2)}, u32[]{:S(2)}) collective-permute-start(f32[1,64,512]{2,1,0:T(8,128)S(1)} %bitcast.11), channel_id=1, source_target_pairs={{0,4},{4,8},{8,12},{12,0},{1,5},{5,9},{9,13},{13,1},{2,6},{6,10},{... | collective-permute-start | bytes 393224 | tf_op jit(solution)/shard_map/ppermute | solution.py:695
  9.5 4.7 %collective-permute-done.3.above = f32[2,64,512]{2,1,0:T(8,128)S(1)} collective-permute-done((f32[2,64,512]{2,1,0:T(8,128)S(1)}, f32[2,64,512]{2,1,0:T(8,128)S(1)}, u32[]{:S(2)}, u32[]{:S(2)}) %collective-permute-start.3) | collective-permute-done | bytes 262176 | tf_op jit(solution)/shard_map/ppermute | solution.py:661
  14.7 1.5 %collective-permute-done.1 = f32[1,64,512]{2,1,0:T(8,128)S(1)} collective-permute-done((f32[1,64,512]{2,1,0:T(8,128)S(1)}, f32[1,64,512]{2,1,0:T(8,128)S(1)}, u32[]{:S(2)}, u32[]{:S(2)}) %collective-permute-start.1) | collective-permute-done | bytes 131104 | tf_op jit(solution)/shard_map/ppermute | solution.py:695
  16.2 2.6 %collective-permute-start.2 = (f32[2,64,512]{2,1,0:T(8,128)S(1)}, f32[2,64,512]{2,1,0:T(8,128)S(1)}, u32[]{:S(2)}, u32[]{:S(2)}) collective-permute-start(f32[2,64,512]{2,1,0:T(8,128)S(1)} %pad_maximum_fusion), channel_id=1, source_target_pairs={{12,4},{13,5},{14,6},{15,7},{0,8},{1,9},{2,10},{3,11},{28,20},{29,... | collective-permute-start | bytes 786440 | tf_op jit(solution)/shard_map/ppermute | solution.py:641
  21.4 1.3 %shard_map.119 = (f32[2,128,256]{2,1,0:T(8,128)S(1)}, f32[2,128,512]{2,1,0:T(8,128)S(1)}) custom-call(s32[11]{0:T(128)S(1)} %pad_add_fusion.1.info, f32[1,2,128,2048]{3,2,1,0:T(8,128)S(1)} %copy-done, f32[1,2,128,2048]{3,2,1,0:T(8,128)S(1)} %copy-done, f32[2,64,512]{2,1,0:T(8,128)S(1)} %collective-permute-done.3.above, ...), custom_call_target="tpu_custom_call" | custom-call | tf_op jit(solution)/shard_map/pallas_call | solution.py:718
  25.1 5.1 %collective-permute-start.10 = (f32[2,128,256]{2,1,0:T(8,128)S(1)}, f32[2,128,256]{2,1,0:T(8,128)S(1)}, u32[]{:S(2)}, u32[]{:S(2)}) collective-permute-start(f32[2,128,256]{2,1,0:T(8,128)S(1)} %get-tuple-element.62), channel_id=1, source_target_pairs={{4,4},{5,5},{12,6},{13,7},{8,8},{9,9},{0,10},{1,11},{20,20},{21,21... | collective-permute-start | bytes 786440 | tf_op jit(solution)/shard_map/ppermute | solution.py:641
  30.2 1.3 %shard_map.120 = (f32[2,128,256]{2,1,0:T(8,128)S(1)}, f32[2,128,512]{2,1,0:T(8,128)S(1)}) custom-call(s32[11]{0:T(128)S(1)} %pad_add_fusion.1.info, f32[1,2,128,2048]{3,2,1,0:T(8,128)S(1)} %copy-done, f32[1,2,128,2048]{3,2,1,0:T(8,128)S(1)} %copy-done, f32[2,64,512]{2,1,0:T(8,128)S(1)} %collective-permute-done.3.above, ...), custom_call_target="tpu_custom_call" | custom-call | tf_op jit(solution)/shard_map/pallas_call | solution.py:718
  31.5 1.4 %collective-permute-start.11 = (f32[2,128,256]{2,1,0:T(8,128)S(1)}, f32[2,128,256]{2,1,0:T(8,128)S(1)}, u32[]{:S(2)}, u32[]{:S(2)}) collective-permute-start(f32[2,128,256]{2,1,0:T(8,128)S(1)} %get-tuple-element.64), channel_id=1, source_target_pairs={{8,4},{9,5},{0,6},{1,7},{12,8},{13,9},{4,10},{5,11},{24,20},{25,21... | collective-permute-start | bytes 786440 | tf_op jit(solution)/shard_map/ppermute | solution.py:641
  33.0 1.3 %shard_map.121 = (f32[2,128,256]{2,1,0:T(8,128)S(1)}, f32[2,128,512]{2,1,0:T(8,128)S(1)}) custom-call(s32[11]{0:T(128)S(1)} %pad_add_fusion.1.info, f32[1,2,128,2048]{3,2,1,0:T(8,128)S(1)} %copy-done, f32[1,2,128,2048]{3,2,1,0:T(8,128)S(1)} %copy-done, f32[2,64,512]{2,1,0:T(8,128)S(1)} %collective-permute-done.3.above, ...), custom_call_target="tpu_custom_call" | custom-call | tf_op jit(solution)/shard_map/pallas_call | solution.py:718
  34.4 1.3 %shard_map.122 = (f32[2,128,256]{2,1,0:T(8,128)S(1)}, f32[2,128,512]{2,1,0:T(8,128)S(1)}) custom-call(s32[11]{0:T(128)S(1)} %pad_add_fusion.1.info, f32[1,2,128,2048]{3,2,1,0:T(8,128)S(1)} %copy-done, f32[1,2,128,2048]{3,2,1,0:T(8,128)S(1)} %copy-done, f32[2,64,512]{2,1,0:T(8,128)S(1)} %collective-permute-done.3.above, ...), custom_call_target="tpu_custom_call" | custom-call | tf_op jit(solution)/shard_map/pallas_call | solution.py:718
  37.2 4.1 %collective-permute-done.11.refs_1_ = f32[2,128,256]{2,1,0:T(8,128)S(1)} collective-permute-done((f32[2,128,256]{2,1,0:T(8,128)S(1)}, f32[2,128,256]{2,1,0:T(8,128)S(1)}, u32[]{:S(2)}, u32[]{:S(2)}) %collective-permute-start.11) | collective-permute-done | bytes 262176 | tf_op jit(solution)/shard_map/ppermute | solution.py:641
  41.3 4.9 %collective-permute-start.13 = (f32[2,128,256]{2,1,0:T(8,128)S(1)}, f32[2,128,256]{2,1,0:T(8,128)S(1)}, u32[]{:S(2)}, u32[]{:S(2)}) collective-permute-start(f32[2,128,256]{2,1,0:T(8,128)S(1)} %get-tuple-element.79), channel_id=1, source_target_pairs={{0,4},{1,5},{8,6},{9,7},{4,8},{5,9},{12,10},{13,11},{16,20},{17,21... | collective-permute-start | bytes 786440 | tf_op jit(solution)/shard_map/ppermute | solution.py:641
  46.2 5.1 %collective-permute-start.12 = (f32[2,128,256]{2,1,0:T(8,128)S(1)}, f32[2,128,256]{2,1,0:T(8,128)S(1)}, u32[]{:S(2)}, u32[]{:S(2)}) collective-permute-start(f32[2,128,256]{2,1,0:T(8,128)S(1)} %get-tuple-element.78), channel_id=1, source_target_pairs={{12,4},{13,5},{4,6},{5,7},{0,8},{1,9},{8,10},{9,11},{28,20},{29,21... | collective-permute-start | bytes 786440 | tf_op jit(solution)/shard_map/ppermute | solution.py:641
  51.3 2.1 %shard_map.123.field = f32[2,512,256]{2,1,0:T(8,128)S(1)} custom-call(s32[3]{0:T(128)S(1)} %pad_add_fusion.info, f32[64,512]{1,0:T(8,128)S(1)} %get-tuple-element.69.refs_0_, f32[64,512]{1,0:T(8,128)S(1)} %get-tuple-element.113.refs_1_, f32[64,512]{1,0:T(8,128)S(1)} %bitcast.13, f32[64,512]{1,0:T(8,128)S(1)} %get-tuple-element.61.refs_3_), custom_call_target="tpu_custom_call" | custom-call | tf_op jit(solution)/shard_map/pallas_call | solution.py:780
  53.4 2.8 %collective-permute-done.12.refs_2_ = f32[2,128,256]{2,1,0:T(8,128)S(1)} collective-permute-done((f32[2,128,256]{2,1,0:T(8,128)S(1)}, f32[2,128,256]{2,1,0:T(8,128)S(1)}, u32[]{:S(2)}, u32[]{:S(2)}) %collective-permute-start.12) | collective-permute-done | bytes 262176 | tf_op jit(solution)/shard_map/ppermute | solution.py:641
  56.3 2.3 %shard_map.129 = (f32[2,256,256]{2,1,0:T(8,128)S(1)}, f32[2,256,256]{2,1,0:T(8,128)S(1)}) custom-call(s32[3]{0:T(128)S(1)} %pad_add_fusion.info, bf16[256,768]{1,0:T(8,128)(2,1)S(1)} %copy-done.6, bf16[256,768]{1,0:T(8,128)(2,1)S(1)} %copy-done.5, f32[4,2,128,128]{3,2,1,0:T(8,128)S(1)} %copy-done.3, f32[2,512,256]{2,1,0:T(8,128)S(1)} %shard_map.123.field, ...), custom_call_target="tpu_custom_call" | custom-call | tf_op jit(solution)/shard_map/pallas_call | solution.py:780
  58.7 1.9 %collective-permute-done.14.other = f32[2,256,256]{2,1,0:T(8,128)S(1)} collective-permute-done((f32[2,256,256]{2,1,0:T(8,128)S(1)}, f32[2,256,256]{2,1,0:T(8,128)S(1)}, u32[]{:S(2)}, u32[]{:S(2)}) %collective-permute-start.14) | collective-permute-done | bytes 524320 | tf_op jit(solution)/shard_map/ppermute | solution.py:644
  60.6 2.2 %shard_map.130 = (f32[2,256,512]{2,1,0:T(8,128)S(1)}, f32[2,256,256]{2,1,0:T(8,128)S(1)}, f32[2,256,256]{2,1,0:T(8,128)S(1)}) custom-call(s32[3]{0:T(128)S(1)} %pad_add_fusion.info, bf16[768,256]{1,0:T(8,128)(2,1)S(1)} %copy-done.1, bf16[768,256]{1,0:T(8,128)(2,1)S(1)} %copy-done.4, f32[8,128]{1,0:T(8,128)S(1)} %copy-done.8, ...), custom_call_target="tpu_custom_call" | custom-call | tf_op jit(solution)/shard_map/pallas_call | solution.py:780
  62.9 1.6 %shard_map.128.target = f32[512,256]{1,0:T(8,128)S(1)} custom-call(s32[3]{0:T(128)S(1)} %pad_add_fusion.info, f32[3,64,512]{2,1,0:T(8,128)S(1)} %collective-permute-done.6.refs_0_, f32[3,64,512]{2,1,0:T(8,128)S(1)} %collective-permute-done.7.refs_1_, f32[3,64,512]{2,1,0:T(8,128)S(1)} %collective-permute-done.8.refs_2_, ...), custom_call_target="tpu_custom_call" | custom-call | tf_op jit(solution)/shard_map/pallas_call | solution.py:780
  64.7 2.3 %shard_map.131 = (f32[2,256,256]{2,1,0:T(8,128)S(1)}, f32[2,256,256]{2,1,0:T(8,128)S(1)}) custom-call(s32[3]{0:T(128)S(1)} %pad_add_fusion.info, bf16[256,768]{1,0:T(8,128)(2,1)S(1)} %copy-done.6, bf16[256,768]{1,0:T(8,128)(2,1)S(1)} %copy-done.5, f32[4,2,128,128]{3,2,1,0:T(8,128)S(1)} %copy-done.3, f32[512,256]{1,0:T(8,128)S(1)} %shard_map.128.target, ...), custom_call_target="tpu_custom_call" | custom-call | tf_op jit(solution)/shard_map/pallas_call | solution.py:780
  67.3 1.7 %collective-permute-done.16.other = f32[2,256,256]{2,1,0:T(8,128)S(1)} collective-permute-done((f32[2,256,256]{2,1,0:T(8,128)S(1)}, f32[2,256,256]{2,1,0:T(8,128)S(1)}, u32[]{:S(2)}, u32[]{:S(2)}) %collective-permute-start.16) | collective-permute-done | bytes 524320 | tf_op jit(solution)/shard_map/ppermute | solution.py:644
  69.0 1.5 %shard_map.132 = (f32[2,64,512]{2,1,0:T(8,128)S(1)}, f32[2,64,512]{2,1,0:T(8,128)S(1)}, f32[2,64,512]{2,1,0:T(8,128)S(1)}, f32[2,64,512]{2,1,0:T(8,128)S(1)}, f32[2,256,512]{2,1,0:T(8,128)S(1)}) custom-call(s32[3]{0:T(128)S(1)} %pad_add_fusion.info, bf16[768,256]{1,0:T(8,128)(2,1)S(1)} %copy-done.4, f32[8,128]{1,0:T(8,128)S(1)} %copy-done.8, ...), custom_call_target="tpu_custom_call" | custom-call | tf_op jit(solution)/shard_map/pallas_call | solution.py:780
  70.5 1.2 %shard_map.133 = (f32[2,256,256]{2,1,0:T(8,128)S(1)}, f32[2,256,256]{2,1,0:T(8,128)S(1)}) custom-call(s32[3]{0:T(128)S(1)} %pad_add_fusion.info, bf16[768,256]{1,0:T(8,128)(2,1)S(1)} %copy-done.1, f32[8,128]{1,0:T(8,128)S(1)} %copy-done.8, f32[2,256,512]{2,1,0:T(8,128)S(1)} %get-tuple-element.91.leaving), custom_call_target="tpu_custom_call" | custom-call | tf_op jit(solution)/shard_map/pallas_call | solution.py:780
  75.8 2.3 %shard_map.134 = (f32[2,128,256]{2,1,0:T(8,128)S(1)}, f32[2,128,256]{2,1,0:T(8,128)S(1)}, f32[2,128,256]{2,1,0:T(8,128)S(1)}, f32[2,128,256]{2,1,0:T(8,128)S(1)}) custom-call(s32[3]{0:T(128)S(1)} %pad_add_fusion.info, bf16[256,768]{1,0:T(8,128)(2,1)S(1)} %copy-done.6, bf16[256,768]{1,0:T(8,128)(2,1)S(1)} %copy-done.5, f32[4,2,128,128]{3,2,1,0:T(8,128)S(1)} %copy-done.3, ...), custom_call_target="tpu_custom_call" | custom-call | tf_op jit(solution)/shard_map/pallas_call | solution.py:780
  78.3 1.3 %collective-permute-start.19 = (f32[2,128,256]{2,1,0:T(8,128)S(1)}, f32[2,128,256]{2,1,0:T(8,128)S(1)}, u32[]{:S(2)}, u32[]{:S(2)}) collective-permute-start(f32[2,128,256]{2,1,0:T(8,128)S(1)} %get-tuple-element.95), channel_id=1, source_target_pairs={{4,12},{5,13},{6,4},{7,5},{8,0},{9,1},{10,8},{11,9},{20,28},{21,29... | collective-permute-start | bytes 786440 | tf_op jit(solution)/shard_map/ppermute | solution.py:641
  79.6 1.3 %collective-permute-start.18 = (f32[2,128,256]{2,1,0:T(8,128)S(1)}, f32[2,128,256]{2,1,0:T(8,128)S(1)}, u32[]{:S(2)}, u32[]{:S(2)}) collective-permute-start(f32[2,128,256]{2,1,0:T(8,128)S(1)} %get-tuple-element.94), channel_id=1, source_target_pairs={{4,4},{5,5},{6,12},{7,13},{8,8},{9,9},{10,0},{11,1},{20,20},{21,21... | collective-permute-start | bytes 786440 | tf_op jit(solution)/shard_map/ppermute | solution.py:641
  81.0 1.3 %collective-permute-start.20 = (f32[2,128,256]{2,1,0:T(8,128)S(1)}, f32[2,128,256]{2,1,0:T(8,128)S(1)}, u32[]{:S(2)}, u32[]{:S(2)}) collective-permute-start(f32[2,128,256]{2,1,0:T(8,128)S(1)} %get-tuple-element.96), channel_id=1, source_target_pairs={{4,8},{5,9},{6,0},{7,1},{8,12},{9,13},{10,4},{11,5},{20,24},{21,25... | collective-permute-start | bytes 786440 | tf_op jit(solution)/shard_map/ppermute | solution.py:641
  82.3 1.3 %collective-permute-start.21 = (f32[2,128,256]{2,1,0:T(8,128)S(1)}, f32[2,128,256]{2,1,0:T(8,128)S(1)}, u32[]{:S(2)}, u32[]{:S(2)}) collective-permute-start(f32[2,128,256]{2,1,0:T(8,128)S(1)} %get-tuple-element.97), channel_id=1, source_target_pairs={{4,0},{5,1},{6,8},{7,9},{8,4},{9,5},{10,12},{11,13},{20,16},{21,17... | collective-permute-start | bytes 786440 | tf_op jit(solution)/shard_map/ppermute | solution.py:641
  83.9 14.5 %collective-permute-done.19.refs_1_ = f32[2,128,256]{2,1,0:T(8,128)S(1)} collective-permute-done((f32[2,128,256]{2,1,0:T(8,128)S(1)}, f32[2,128,256]{2,1,0:T(8,128)S(1)}, u32[]{:S(2)}, u32[]{:S(2)}) %collective-permute-start.19) | collective-permute-done | bytes 262176 | tf_op jit(solution)/shard_map/ppermute | solution.py:641
  98.4 5.3 %collective-permute-done.20.refs_2_ = f32[2,128,256]{2,1,0:T(8,128)S(1)} collective-permute-done((f32[2,128,256]{2,1,0:T(8,128)S(1)}, f32[2,128,256]{2,1,0:T(8,128)S(1)}, u32[]{:S(2)}, u32[]{:S(2)}) %collective-permute-start.20) | collective-permute-done | bytes 262176 | tf_op jit(solution)/shard_map/ppermute | solution.py:641
  106.7 4.5 %shard_map.135 = f32[1,2,128,2048]{3,2,1,0:T(8,128)} custom-call(s32[11]{0:T(128)S(1)} %pad_add_fusion.1.info, bf16[768,256]{1,0:T(8,128)(2,1)S(1)} %copy-done.4, f32[8,128]{1,0:T(8,128)S(1)} %copy-done.8, f32[2,128,256]{2,1,0:T(8,128)S(1)} %collective-permute-done.18.refs_0_, f32[2,128,256]{2,1,0:T(8,128)S(1)} %collective-permute-done.19.refs_1_, ...), custom_call_target="tpu_custom_call" | custom-call | tf_op jit(solution)/shard_map/pallas_call | solution.py:855
  (80 shorter events, 19.9 us)
Async XLA Ops:
  2.0 12.2 %collective-permute-start.3 = (f32[2,64,512]{2,1,0:T(8,128)S(1)}, f32[2,64,512]{2,1,0:T(8,128)S(1)}, u32[]{:S(2)}, u32[]{:S(2)}) collective-permute-start(f32[2,64,512]{2,1,0:T(8,128)S(1)} %slice_select_fusion), channel_id=1, source_target_pairs={{0,4},{4,8},{8,12},{12,0},{1,5},{5,9},{9,13},{13,1},{2,6},{6,10},{... | collective-permute-start | bytes 786440 | tf_op jit(solution)/shard_map/ppermute | solution.py:661
  7.9 8.3 %collective-permute-start.1 = (f32[1,64,512]{2,1,0:T(8,128)S(1)}, f32[1,64,512]{2,1,0:T(8,128)S(1)}, u32[]{:S(2)}, u32[]{:S(2)}) collective-permute-start(f32[1,64,512]{2,1,0:T(8,128)S(1)} %bitcast.11), channel_id=1, source_target_pairs={{0,4},{4,8},{8,12},{12,0},{1,5},{5,9},{9,13},{13,1},{2,6},{6,10},{... | collective-permute-start | bytes 393224 | tf_op jit(solution)/shard_map/ppermute | solution.py:695
  9.5 9.4 %collective-permute-start.5 = (f32[2,64,512]{2,1,0:T(8,128)S(1)}, f32[2,64,512]{2,1,0:T(8,128)S(1)}, u32[]{:S(2)}, u32[]{:S(2)}) collective-permute-start(f32[2,64,512]{2,1,0:T(8,128)S(1)} %get-tuple-element.71), channel_id=1, source_target_pairs={{0,1},{1,0},{2,3},{3,2},{4,5},{5,4},{6,7},{7,6},{8,9},{9,8},{10,11... | collective-permute-start | bytes 786440 | tf_op jit(solution)/shard_map/ppermute | solution.py:644
  14.2 7.1 %collective-permute-start.4 = (f32[2,64,512]{2,1,0:T(8,128)S(1)}, f32[2,64,512]{2,1,0:T(8,128)S(1)}, u32[]{:S(2)}, u32[]{:S(2)}) collective-permute-start(f32[2,64,512]{2,1,0:T(8,128)S(1)} %collective-permute-done.3.above), channel_id=1, source_target_pairs={{0,1},{1,0},{2,3},{3,2},{4,5},{5,4},{6,7},{7,6},{8,9},{9,8},{10,11... | collective-permute-start | bytes 786440 | tf_op jit(solution)/shard_map/ppermute | solution.py:644
  14.2 4.7 %collective-permute-start = (s32[4]{0:T(128)S(1)}, s32[4]{0:T(128)S(1)}, u32[]{:S(2)}, u32[]{:S(2)}) collective-permute-start(s32[4]{0:T(128)S(1)} %pad_add_fusion.2), channel_id=1, source_target_pairs={{0,1},{1,0},{2,3},{3,2},{4,5},{5,4},{6,7},{7,6},{8,9},{9,8},{10,11... | collective-permute-start | bytes 56 | tf_op jit(solution)/shard_map/ppermute | solution.py:644
  16.2 16.8 %collective-permute-start.2 = (f32[2,64,512]{2,1,0:T(8,128)S(1)}, f32[2,64,512]{2,1,0:T(8,128)S(1)}, u32[]{:S(2)}, u32[]{:S(2)}) collective-permute-start(f32[2,64,512]{2,1,0:T(8,128)S(1)} %pad_maximum_fusion), channel_id=1, source_target_pairs={{12,4},{13,5},{14,6},{15,7},{0,8},{1,9},{2,10},{3,11},{28,20},{29,... | collective-permute-start | bytes 786440 | tf_op jit(solution)/shard_map/ppermute | solution.py:641
  20.6 15.1 %collective-permute-start.7 = (f32[3,64,512]{2,1,0:T(8,128)S(1)}, f32[3,64,512]{2,1,0:T(8,128)S(1)}, u32[]{:S(2)}, u32[]{:S(2)}) collective-permute-start(f32[3,64,512]{2,1,0:T(8,128)S(1)} %shard_map.125), channel_id=1, source_target_pairs={{10,4},{11,5},{2,6},{3,7},{14,8},{15,9},{6,10},{7,11},{26,20},{27,... | collective-permute-start | bytes 1179656 | tf_op jit(solution)/shard_map/ppermute | solution.py:641
  22.7 13.7 %collective-permute-start.6 = (f32[3,64,512]{2,1,0:T(8,128)S(1)}, f32[3,64,512]{2,1,0:T(8,128)S(1)}, u32[]{:S(2)}, u32[]{:S(2)}) collective-permute-start(f32[3,64,512]{2,1,0:T(8,128)S(1)} %shard_map.124), channel_id=1, source_target_pairs={{6,4},{7,5},{14,6},{15,7},{10,8},{11,9},{2,10},{3,11},{22,20},{23,... | collective-permute-start | bytes 1179656 | tf_op jit(solution)/shard_map/ppermute | solution.py:641
  25.1 12.1 %collective-permute-start.10 = (f32[2,128,256]{2,1,0:T(8,128)S(1)}, f32[2,128,256]{2,1,0:T(8,128)S(1)}, u32[]{:S(2)}, u32[]{:S(2)}) collective-permute-start(f32[2,128,256]{2,1,0:T(8,128)S(1)} %get-tuple-element.62), channel_id=1, source_target_pairs={{4,4},{5,5},{12,6},{13,7},{8,8},{9,9},{0,10},{1,11},{20,20},{21,21... | collective-permute-start | bytes 786440 | tf_op jit(solution)/shard_map/ppermute | solution.py:641
  31.5 9.7 %collective-permute-start.11 = (f32[2,128,256]{2,1,0:T(8,128)S(1)}, f32[2,128,256]{2,1,0:T(8,128)S(1)}, u32[]{:S(2)}, u32[]{:S(2)}) collective-permute-start(f32[2,128,256]{2,1,0:T(8,128)S(1)} %get-tuple-element.64), channel_id=1, source_target_pairs={{8,4},{9,5},{0,6},{1,7},{12,8},{13,9},{4,10},{5,11},{24,20},{25,21... | collective-permute-start | bytes 786440 | tf_op jit(solution)/shard_map/ppermute | solution.py:641
  35.7 20.5 %collective-permute-start.9 = (f32[3,64,512]{2,1,0:T(8,128)S(1)}, f32[3,64,512]{2,1,0:T(8,128)S(1)}, u32[]{:S(2)}, u32[]{:S(2)}) collective-permute-start(f32[3,64,512]{2,1,0:T(8,128)S(1)} %shard_map.127), channel_id=1, source_target_pairs={{2,4},{3,5},{10,6},{11,7},{6,8},{7,9},{14,10},{15,11},{18,20},{19,... | collective-permute-start | bytes 1179656 | tf_op jit(solution)/shard_map/ppermute | solution.py:641
  36.5 19.8 %collective-permute-start.8 = (f32[3,64,512]{2,1,0:T(8,128)S(1)}, f32[3,64,512]{2,1,0:T(8,128)S(1)}, u32[]{:S(2)}, u32[]{:S(2)}) collective-permute-start(f32[3,64,512]{2,1,0:T(8,128)S(1)} %shard_map.126), channel_id=1, source_target_pairs={{14,4},{15,5},{6,6},{7,7},{2,8},{3,9},{10,10},{11,11},{30,20},{31,... | collective-permute-start | bytes 1179656 | tf_op jit(solution)/shard_map/ppermute | solution.py:641
  41.3 12.2 %collective-permute-start.13 = (f32[2,128,256]{2,1,0:T(8,128)S(1)}, f32[2,128,256]{2,1,0:T(8,128)S(1)}, u32[]{:S(2)}, u32[]{:S(2)}) collective-permute-start(f32[2,128,256]{2,1,0:T(8,128)S(1)} %get-tuple-element.79), channel_id=1, source_target_pairs={{0,4},{1,5},{8,6},{9,7},{4,8},{5,9},{12,10},{13,11},{16,20},{17,21... | collective-permute-start | bytes 786440 | tf_op jit(solution)/shard_map/ppermute | solution.py:641
  46.2 10.0 %collective-permute-start.12 = (f32[2,128,256]{2,1,0:T(8,128)S(1)}, f32[2,128,256]{2,1,0:T(8,128)S(1)}, u32[]{:S(2)}, u32[]{:S(2)}) collective-permute-start(f32[2,128,256]{2,1,0:T(8,128)S(1)} %get-tuple-element.78), channel_id=1, source_target_pairs={{12,4},{13,5},{4,6},{5,7},{0,8},{1,9},{8,10},{9,11},{28,20},{29,21... | collective-permute-start | bytes 786440 | tf_op jit(solution)/shard_map/ppermute | solution.py:641
  58.6 2.0 %collective-permute-start.14 = (f32[2,256,256]{2,1,0:T(8,128)S(1)}, f32[2,256,256]{2,1,0:T(8,128)S(1)}, u32[]{:S(2)}, u32[]{:S(2)}) collective-permute-start(f32[2,256,256]{2,1,0:T(8,128)S(1)} %get-tuple-element.85), channel_id=1, source_target_pairs={{0,1},{1,0},{2,3},{3,2},{4,5},{5,4},{6,7},{7,6},{8,9},{9,8},{10,11... | collective-permute-start | bytes 1572872 | tf_op jit(solution)/shard_map/ppermute | solution.py:644
  62.7 2.0 %collective-permute-start.15 = (f32[2,256,256]{2,1,0:T(8,128)S(1)}, f32[2,256,256]{2,1,0:T(8,128)S(1)}, u32[]{:S(2)}, u32[]{:S(2)}) collective-permute-start(f32[2,256,256]{2,1,0:T(8,128)S(1)} %get-tuple-element.87), channel_id=1, source_target_pairs={{0,1},{1,0},{2,3},{3,2},{4,5},{5,4},{6,7},{7,6},{8,9},{9,8},{10,11... | collective-permute-start | bytes 1572872 | tf_op jit(solution)/shard_map/ppermute | solution.py:644
  67.0 2.0 %collective-permute-start.16 = (f32[2,256,256]{2,1,0:T(8,128)S(1)}, f32[2,256,256]{2,1,0:T(8,128)S(1)}, u32[]{:S(2)}, u32[]{:S(2)}) collective-permute-start(f32[2,256,256]{2,1,0:T(8,128)S(1)} %get-tuple-element.89), channel_id=1, source_target_pairs={{0,1},{1,0},{2,3},{3,2},{4,5},{5,4},{6,7},{7,6},{8,9},{9,8},{10,11... | collective-permute-start | bytes 1572872 | tf_op jit(solution)/shard_map/ppermute | solution.py:644
  71.7 2.0 %collective-permute-start.17 = (f32[2,256,256]{2,1,0:T(8,128)S(1)}, f32[2,256,256]{2,1,0:T(8,128)S(1)}, u32[]{:S(2)}, u32[]{:S(2)}) collective-permute-start(f32[2,256,256]{2,1,0:T(8,128)S(1)} %get-tuple-element.93), channel_id=1, source_target_pairs={{0,1},{1,0},{2,3},{3,2},{4,5},{5,4},{6,7},{7,6},{8,9},{9,8},{10,11... | collective-permute-start | bytes 1572872 | tf_op jit(solution)/shard_map/ppermute | solution.py:644
  72.0 6.0 %collective-permute-start.26 = (f32[2,64,512]{2,1,0:T(8,128)S(1)}, f32[2,64,512]{2,1,0:T(8,128)S(1)}, u32[]{:S(2)}, u32[]{:S(2)}) collective-permute-start(f32[2,64,512]{2,1,0:T(8,128)S(1)} %get-tuple-element.98), channel_id=1, source_target_pairs={{4,6},{5,7},{6,14},{7,15},{8,10},{9,11},{10,2},{11,3},{20,22},{21,... | collective-permute-start | bytes 786440 | tf_op jit(solution)/shard_map/ppermute | solution.py:641
  73.7 5.9 %collective-permute-start.27 = (f32[2,64,512]{2,1,0:T(8,128)S(1)}, f32[2,64,512]{2,1,0:T(8,128)S(1)}, u32[]{:S(2)}, u32[]{:S(2)}) collective-permute-start(f32[2,64,512]{2,1,0:T(8,128)S(1)} %get-tuple-element.100), channel_id=1, source_target_pairs={{4,14},{5,15},{6,6},{7,7},{8,2},{9,3},{10,10},{11,11},{20,30},{21,... | collective-permute-start | bytes 786440 | tf_op jit(solution)/shard_map/ppermute | solution.py:641
  74.4 6.6 %collective-permute-start.28 = (f32[2,64,512]{2,1,0:T(8,128)S(1)}, f32[2,64,512]{2,1,0:T(8,128)S(1)}, u32[]{:S(2)}, u32[]{:S(2)}) collective-permute-start(f32[2,64,512]{2,1,0:T(8,128)S(1)} %get-tuple-element.102), channel_id=1, source_target_pairs={{4,10},{5,11},{6,2},{7,3},{8,14},{9,15},{10,6},{11,7},{20,26},{21,... | collective-permute-start | bytes 786440 | tf_op jit(solution)/shard_map/ppermute | solution.py:641
  75.1 7.2 %collective-permute-start.29 = (f32[2,64,512]{2,1,0:T(8,128)S(1)}, f32[2,64,512]{2,1,0:T(8,128)S(1)}, u32[]{:S(2)}, u32[]{:S(2)}) collective-permute-start(f32[2,64,512]{2,1,0:T(8,128)S(1)} %get-tuple-element.104), channel_id=1, source_target_pairs={{4,2},{5,3},{6,10},{7,11},{8,6},{9,7},{10,14},{11,15},{20,18},{21,... | collective-permute-start | bytes 786440 | tf_op jit(solution)/shard_map/ppermute | solution.py:641
  78.1 5.5 %collective-permute-start.30 = (f32[2,64,512]{2,1,0:T(8,128)S(1)}, f32[2,64,512]{2,1,0:T(8,128)S(1)}, u32[]{:S(2)}, u32[]{:S(2)}) collective-permute-start(f32[2,64,512]{2,1,0:T(8,128)S(1)} %collective-permute-done.26.refs_8_), channel_id=1, source_target_pairs={{0,1},{1,0},{2,3},{3,2},{4,5},{5,4},{6,7},{7,6},{8,9},{9,8},{10,11... | collective-permute-start | bytes 786440 | tf_op jit(solution)/shard_map/ppermute | solution.py:644
  78.3 20.0 %collective-permute-start.19 = (f32[2,128,256]{2,1,0:T(8,128)S(1)}, f32[2,128,256]{2,1,0:T(8,128)S(1)}, u32[]{:S(2)}, u32[]{:S(2)}) collective-permute-start(f32[2,128,256]{2,1,0:T(8,128)S(1)} %get-tuple-element.95), channel_id=1, source_target_pairs={{4,12},{5,13},{6,4},{7,5},{8,0},{9,1},{10,8},{11,9},{20,28},{21,29... | collective-permute-start | bytes 786440 | tf_op jit(solution)/shard_map/ppermute | solution.py:641
  79.6 24.5 %collective-permute-start.18 = (f32[2,128,256]{2,1,0:T(8,128)S(1)}, f32[2,128,256]{2,1,0:T(8,128)S(1)}, u32[]{:S(2)}, u32[]{:S(2)}) collective-permute-start(f32[2,128,256]{2,1,0:T(8,128)S(1)} %get-tuple-element.94), channel_id=1, source_target_pairs={{4,4},{5,5},{6,12},{7,13},{8,8},{9,9},{10,0},{11,1},{20,20},{21,21... | collective-permute-start | bytes 786440 | tf_op jit(solution)/shard_map/ppermute | solution.py:641
  81.0 22.7 %collective-permute-start.20 = (f32[2,128,256]{2,1,0:T(8,128)S(1)}, f32[2,128,256]{2,1,0:T(8,128)S(1)}, u32[]{:S(2)}, u32[]{:S(2)}) collective-permute-start(f32[2,128,256]{2,1,0:T(8,128)S(1)} %get-tuple-element.96), channel_id=1, source_target_pairs={{4,8},{5,9},{6,0},{7,1},{8,12},{9,13},{10,4},{11,5},{20,24},{21,25... | collective-permute-start | bytes 786440 | tf_op jit(solution)/shard_map/ppermute | solution.py:641
  82.3 21.6 %collective-permute-start.21 = (f32[2,128,256]{2,1,0:T(8,128)S(1)}, f32[2,128,256]{2,1,0:T(8,128)S(1)}, u32[]{:S(2)}, u32[]{:S(2)}) collective-permute-start(f32[2,128,256]{2,1,0:T(8,128)S(1)} %get-tuple-element.97), channel_id=1, source_target_pairs={{4,0},{5,1},{6,8},{7,9},{8,4},{9,5},{10,12},{11,13},{20,16},{21,17... | collective-permute-start | bytes 786440 | tf_op jit(solution)/shard_map/ppermute | solution.py:641
  83.6 20.8 %collective-permute-start.31 = (f32[2,64,512]{2,1,0:T(8,128)S(1)}, f32[2,64,512]{2,1,0:T(8,128)S(1)}, u32[]{:S(2)}, u32[]{:S(2)}) collective-permute-start(f32[2,64,512]{2,1,0:T(8,128)S(1)} %collective-permute-done.27.refs_9_), channel_id=1, source_target_pairs={{0,1},{1,0},{2,3},{3,2},{4,5},{5,4},{6,7},{7,6},{8,9},{9,8},{10,11... | collective-permute-start | bytes 786440 | tf_op jit(solution)/shard_map/ppermute | solution.py:644
  98.4 6.3 %collective-permute-start.32 = (f32[2,64,512]{2,1,0:T(8,128)S(1)}, f32[2,64,512]{2,1,0:T(8,128)S(1)}, u32[]{:S(2)}, u32[]{:S(2)}) collective-permute-start(f32[2,64,512]{2,1,0:T(8,128)S(1)} %collective-permute-done.28.refs_10_), channel_id=1, source_target_pairs={{0,1},{1,0},{2,3},{3,2},{4,5},{5,4},{6,7},{7,6},{8,9},{9,8},{10,11... | collective-permute-start | bytes 786440 | tf_op jit(solution)/shard_map/ppermute | solution.py:644
  104.2 1.8 %collective-permute-start.24 = (f32[2,128,256]{2,1,0:T(8,128)S(1)}, f32[2,128,256]{2,1,0:T(8,128)S(1)}, u32[]{:S(2)}, u32[]{:S(2)}) collective-permute-start(f32[2,128,256]{2,1,0:T(8,128)S(1)} %collective-permute-done.20.refs_2_), channel_id=1, source_target_pairs={{0,1},{1,0},{2,3},{3,2},{4,5},{5,4},{6,7},{7,6},{8,9},{9,8},{10,11... | collective-permute-start | bytes 786440 | tf_op jit(solution)/shard_map/ppermute | solution.py:644
  104.4 1.9 %collective-permute-start.25 = (f32[2,128,256]{2,1,0:T(8,128)S(1)}, f32[2,128,256]{2,1,0:T(8,128)S(1)}, u32[]{:S(2)}, u32[]{:S(2)}) collective-permute-start(f32[2,128,256]{2,1,0:T(8,128)S(1)} %collective-permute-done.21.refs_3_), channel_id=1, source_target_pairs={{0,1},{1,0},{2,3},{3,2},{4,5},{5,4},{6,7},{7,6},{8,9},{9,8},{10,11... | collective-permute-start | bytes 786440 | tf_op jit(solution)/shard_map/ppermute | solution.py:644
  104.7 2.0 %collective-permute-start.22 = (f32[2,128,256]{2,1,0:T(8,128)S(1)}, f32[2,128,256]{2,1,0:T(8,128)S(1)}, u32[]{:S(2)}, u32[]{:S(2)}) collective-permute-start(f32[2,128,256]{2,1,0:T(8,128)S(1)} %collective-permute-done.18.refs_0_), channel_id=1, source_target_pairs={{0,1},{1,0},{2,3},{3,2},{4,5},{5,4},{6,7},{7,6},{8,9},{9,8},{10,11... | collective-permute-start | bytes 786440 | tf_op jit(solution)/shard_map/ppermute | solution.py:644
  (12 other events, 101.7 us)

commit v6 on v5

--- a/solution.py
+++ b/solution.py
@@ -200,7 +200,8 @@
         assert self.stride >= cores
         self.top = (number - cores) // 2
         self.total = cores * own_probes
-        self.order = [j for pair in zip(range(number // 2), range(number // 2, number)) for j in pair]
+        half = number // 2
+        self.order = [j for i in range(half) for j in ((i, i + half) if i % 2 == 0 else (i + half, i))]
 
     def home(self, q):
         return self.top + q // self.sections, q % self.sections
@@ -382,22 +383,15 @@
 
         @pl.when(info[2] == 0)
         def _():
-            classes = []
-            for index in range(4):
-                first = quarter * (index % 2)
-                pair = []
-                for part in range(2):
-                    own = own_spectra[i][part, :, first : first + quarter]
-                    other = other_spectra[i][part, :, first : first + quarter]
-                    pair.append(jnp.where(lower, own, other) if index < 2 else jnp.where(lower, other, own))
-                classes.append(tuple(pair))
-            inner = inverse_lanes(classes, table, twiddle)
-            for m in range(4):
-                columns = slice(quarter * m, quarter * (m + 1))
-                entering = (rolled[i][0, :, columns], rolled[i][1, :, columns])
-                term = conj_times(entering, inner[m])
-                scratch[0, :, columns] = term[0]
-                scratch[1, :, columns] = term[1]
+            for first in range(0, height, min(height, 32)):
+                rows = slice(first, first + min(height, 32))
+                inner = inverse_lanes(lane_classes(own_spectra[i], other_spectra[i], lower, rows), table, twiddle)
+                for m in range(4):
+                    columns = slice(quarter * m, quarter * (m + 1))
+                    entering = (rolled[i][0, rows, columns], rolled[i][1, rows, columns])
+                    term = conj_times(entering, inner[m])
+                    scratch[0, rows, columns] = term[0]
+                    scratch[1, rows, columns] = term[1]
 
         @pl.when(info[2] != 0)
         def _():

time: 112 us -> 112 us (level)
  transfers between devices with their start and end apart: 34 -> 34, of which waited for: 16 -> 15; matrix products, arithmetic and copies ran while one was open for 0% -> 0% of each run, Pallas kernels for 14% -> 14%
where the time goes in v6:
time: 112 us; the launch traced here: 111 us
  waiting for transfers between devices  39.7 us (35%)
  starting transfers between devices  37.6 us (34%)
  Pallas kernels  29.3 us (26%)
  other arithmetic  2.13 us (2%)
  local copies, waits for them, and re-layouts  2.06 us (2%)
    ppermute x17, starting transfers between devices, move(): return lax.ppermute(value, line_axes, pairs)  29.8 us
    ppermute x17, waiting for transfers between devices, move(): return lax.ppermute(value, line_axes, pairs)  26.9 us
    pallas_call x8, Pallas kernels, at_home(): pl.pallas_call(kernel, out_shape=[floats(*shape) for shape in outs], in_s...  15.5 us
    ppermute x15, waiting for transfers between devices, swap(): lax.ppermute(value, 'batch', [(i, (i + 1) % cores) for i in range(cores)])  6.7 us
    pallas_call x4, Pallas kernels, launch_of(): pl.pallas_call(functools.partial(launch_kernel, plan, j), out_shape=[floa...  5.37 us
    ppermute x1, waiting for transfers between devices, on_device(): lax.ppermute(part, 'row', [(i, (i + 1) % number) for i in range(number)])  4.69 us
    pallas_call x1, Pallas kernels, on_device(): pl.pallas_call(functools.partial(settle_kernel, plan), out_shape=jax.Shap...  4.43 us
    pallas_call x4, Pallas kernels, patch_of(): pl.pallas_call(functools.partial(patch_kernel, plan, j), out_shape=floats...  3.26 us
  transfers between devices with their start and end apart: 34, of which 15 were waited for; matrix products, arithmetic and copies ran while one was open for 0% of the time, Pallas kernels for 14%

profile of v6, /device:TPU:0, one launch (start us, length us, event | category | flops | bytes accessed | tf_op | source)
XLA Modules:
  0.0 111.4 jit_solution(14135417895930080734)
XLA Ops:
  2.0 3.1 %collective-permute-start.3 = (f32[2,64,512]{2,1,0:T(8,128)S(1)}, f32[2,64,512]{2,1,0:T(8,128)S(1)}, u32[]{:S(2)}, u32[]{:S(2)}) collective-permute-start(f32[2,64,512]{2,1,0:T(8,128)S(1)} %slice_select_fusion), channel_id=1, source_target_pairs={{0,4},{4,8},{8,12},{12,0},{1,5},{5,9},{9,13},{13,1},{2,6},{6,10},{... | collective-permute-start | bytes 786440 | tf_op jit(solution)/shard_map/ppermute | solution.py:655
  7.9 1.6 %collective-permute-start.1 = (f32[1,64,512]{2,1,0:T(8,128)S(1)}, f32[1,64,512]{2,1,0:T(8,128)S(1)}, u32[]{:S(2)}, u32[]{:S(2)}) collective-permute-start(f32[1,64,512]{2,1,0:T(8,128)S(1)} %bitcast.11), channel_id=1, source_target_pairs={{0,4},{4,8},{8,12},{12,0},{1,5},{5,9},{9,13},{13,1},{2,6},{6,10},{... | collective-permute-start | bytes 393224 | tf_op jit(solution)/shard_map/ppermute | solution.py:689
  9.5 4.7 %collective-permute-done.3.above = f32[2,64,512]{2,1,0:T(8,128)S(1)} collective-permute-done((f32[2,64,512]{2,1,0:T(8,128)S(1)}, f32[2,64,512]{2,1,0:T(8,128)S(1)}, u32[]{:S(2)}, u32[]{:S(2)}) %collective-permute-start.3) | collective-permute-done | bytes 262176 | tf_op jit(solution)/shard_map/ppermute | solution.py:655
  14.7 1.5 %collective-permute-done.1 = f32[1,64,512]{2,1,0:T(8,128)S(1)} collective-permute-done((f32[1,64,512]{2,1,0:T(8,128)S(1)}, f32[1,64,512]{2,1,0:T(8,128)S(1)}, u32[]{:S(2)}, u32[]{:S(2)}) %collective-permute-start.1) | collective-permute-done | bytes 131104 | tf_op jit(solution)/shard_map/ppermute | solution.py:689
  16.2 2.6 %collective-permute-start.2 = (f32[2,64,512]{2,1,0:T(8,128)S(1)}, f32[2,64,512]{2,1,0:T(8,128)S(1)}, u32[]{:S(2)}, u32[]{:S(2)}) collective-permute-start(f32[2,64,512]{2,1,0:T(8,128)S(1)} %pad_maximum_fusion), channel_id=1, source_target_pairs={{12,4},{13,5},{14,6},{15,7},{0,8},{1,9},{2,10},{3,11},{28,20},{29,... | collective-permute-start | bytes 786440 | tf_op jit(solution)/shard_map/ppermute | solution.py:635
  21.4 1.3 %shard_map.119 = (f32[2,128,256]{2,1,0:T(8,128)S(1)}, f32[2,128,512]{2,1,0:T(8,128)S(1)}) custom-call(s32[11]{0:T(128)S(1)} %pad_add_fusion.1.info, f32[1,2,128,2048]{3,2,1,0:T(8,128)S(1)} %copy-done, f32[1,2,128,2048]{3,2,1,0:T(8,128)S(1)} %copy-done, f32[2,64,512]{2,1,0:T(8,128)S(1)} %collective-permute-done.3.above, ...), custom_call_target="tpu_custom_call" | custom-call | tf_op jit(solution)/shard_map/pallas_call | solution.py:712
  25.1 5.1 %collective-permute-start.10 = (f32[2,128,256]{2,1,0:T(8,128)S(1)}, f32[2,128,256]{2,1,0:T(8,128)S(1)}, u32[]{:S(2)}, u32[]{:S(2)}) collective-permute-start(f32[2,128,256]{2,1,0:T(8,128)S(1)} %get-tuple-element.62), channel_id=1, source_target_pairs={{4,4},{5,5},{12,6},{13,7},{8,8},{9,9},{0,10},{1,11},{20,20},{21,21... | collective-permute-start | bytes 786440 | tf_op jit(solution)/shard_map/ppermute | solution.py:635
  30.2 1.3 %shard_map.120 = (f32[2,128,256]{2,1,0:T(8,128)S(1)}, f32[2,128,512]{2,1,0:T(8,128)S(1)}) custom-call(s32[11]{0:T(128)S(1)} %pad_add_fusion.1.info, f32[1,2,128,2048]{3,2,1,0:T(8,128)S(1)} %copy-done, f32[1,2,128,2048]{3,2,1,0:T(8,128)S(1)} %copy-done, f32[2,64,512]{2,1,0:T(8,128)S(1)} %collective-permute-done.3.above, ...), custom_call_target="tpu_custom_call" | custom-call | tf_op jit(solution)/shard_map/pallas_call | solution.py:712
  31.5 1.4 %collective-permute-start.11 = (f32[2,128,256]{2,1,0:T(8,128)S(1)}, f32[2,128,256]{2,1,0:T(8,128)S(1)}, u32[]{:S(2)}, u32[]{:S(2)}) collective-permute-start(f32[2,128,256]{2,1,0:T(8,128)S(1)} %get-tuple-element.64), channel_id=1, source_target_pairs={{8,4},{9,5},{0,6},{1,7},{12,8},{13,9},{4,10},{5,11},{24,20},{25,21... | collective-permute-start | bytes 786440 | tf_op jit(solution)/shard_map/ppermute | solution.py:635
  33.0 1.3 %shard_map.121 = (f32[2,128,256]{2,1,0:T(8,128)S(1)}, f32[2,128,512]{2,1,0:T(8,128)S(1)}) custom-call(s32[11]{0:T(128)S(1)} %pad_add_fusion.1.info, f32[1,2,128,2048]{3,2,1,0:T(8,128)S(1)} %copy-done, f32[1,2,128,2048]{3,2,1,0:T(8,128)S(1)} %copy-done, f32[2,64,512]{2,1,0:T(8,128)S(1)} %collective-permute-done.3.above, ...), custom_call_target="tpu_custom_call" | custom-call | tf_op jit(solution)/shard_map/pallas_call | solution.py:712
  34.4 1.3 %shard_map.122 = (f32[2,128,256]{2,1,0:T(8,128)S(1)}, f32[2,128,512]{2,1,0:T(8,128)S(1)}) custom-call(s32[11]{0:T(128)S(1)} %pad_add_fusion.1.info, f32[1,2,128,2048]{3,2,1,0:T(8,128)S(1)} %copy-done, f32[1,2,128,2048]{3,2,1,0:T(8,128)S(1)} %copy-done, f32[2,64,512]{2,1,0:T(8,128)S(1)} %collective-permute-done.3.above, ...), custom_call_target="tpu_custom_call" | custom-call | tf_op jit(solution)/shard_map/pallas_call | solution.py:712
  37.2 4.1 %collective-permute-done.11.refs_1_ = f32[2,128,256]{2,1,0:T(8,128)S(1)} collective-permute-done((f32[2,128,256]{2,1,0:T(8,128)S(1)}, f32[2,128,256]{2,1,0:T(8,128)S(1)}, u32[]{:S(2)}, u32[]{:S(2)}) %collective-permute-start.11) | collective-permute-done | bytes 262176 | tf_op jit(solution)/shard_map/ppermute | solution.py:635
  41.3 4.9 %collective-permute-start.13 = (f32[2,128,256]{2,1,0:T(8,128)S(1)}, f32[2,128,256]{2,1,0:T(8,128)S(1)}, u32[]{:S(2)}, u32[]{:S(2)}) collective-permute-start(f32[2,128,256]{2,1,0:T(8,128)S(1)} %get-tuple-element.79), channel_id=1, source_target_pairs={{0,4},{1,5},{8,6},{9,7},{4,8},{5,9},{12,10},{13,11},{16,20},{17,21... | collective-permute-start | bytes 786440 | tf_op jit(solution)/shard_map/ppermute | solution.py:635
  46.2 5.1 %collective-permute-start.12 = (f32[2,128,256]{2,1,0:T(8,128)S(1)}, f32[2,128,256]{2,1,0:T(8,128)S(1)}, u32[]{:S(2)}, u32[]{:S(2)}) collective-permute-start(f32[2,128,256]{2,1,0:T(8,128)S(1)} %get-tuple-element.78), channel_id=1, source_target_pairs={{12,4},{13,5},{4,6},{5,7},{0,8},{1,9},{8,10},{9,11},{28,20},{29,21... | collective-permute-start | bytes 786440 | tf_op jit(solution)/shard_map/ppermute | solution.py:635
  51.3 2.1 %shard_map.123.field = f32[2,512,256]{2,1,0:T(8,128)S(1)} custom-call(s32[3]{0:T(128)S(1)} %pad_add_fusion.info, f32[64,512]{1,0:T(8,128)S(1)} %get-tuple-element.69.refs_0_, f32[64,512]{1,0:T(8,128)S(1)} %get-tuple-element.113.refs_1_, f32[64,512]{1,0:T(8,128)S(1)} %bitcast.13, f32[64,512]{1,0:T(8,128)S(1)} %get-tuple-element.61.refs_3_), custom_call_target="tpu_custom_call" | custom-call | tf_op jit(solution)/shard_map/pallas_call | solution.py:774
  53.4 2.8 %collective-permute-done.12.refs_2_ = f32[2,128,256]{2,1,0:T(8,128)S(1)} collective-permute-done((f32[2,128,256]{2,1,0:T(8,128)S(1)}, f32[2,128,256]{2,1,0:T(8,128)S(1)}, u32[]{:S(2)}, u32[]{:S(2)}) %collective-permute-start.12) | collective-permute-done | bytes 262176 | tf_op jit(solution)/shard_map/ppermute | solution.py:635
  56.3 2.3 %shard_map.129 = (f32[2,256,256]{2,1,0:T(8,128)S(1)}, f32[2,256,256]{2,1,0:T(8,128)S(1)}) custom-call(s32[3]{0:T(128)S(1)} %pad_add_fusion.info, bf16[256,768]{1,0:T(8,128)(2,1)S(1)} %copy-done.6, bf16[256,768]{1,0:T(8,128)(2,1)S(1)} %copy-done.5, f32[4,2,128,128]{3,2,1,0:T(8,128)S(1)} %copy-done.3, f32[2,512,256]{2,1,0:T(8,128)S(1)} %shard_map.123.field, ...), custom_call_target="tpu_custom_call" | custom-call | tf_op jit(solution)/shard_map/pallas_call | solution.py:774
  58.7 1.9 %collective-permute-done.14.other = f32[2,256,256]{2,1,0:T(8,128)S(1)} collective-permute-done((f32[2,256,256]{2,1,0:T(8,128)S(1)}, f32[2,256,256]{2,1,0:T(8,128)S(1)}, u32[]{:S(2)}, u32[]{:S(2)}) %collective-permute-start.14) | collective-permute-done | bytes 524320 | tf_op jit(solution)/shard_map/ppermute | solution.py:638
  60.6 2.2 %shard_map.130 = (f32[2,256,512]{2,1,0:T(8,128)S(1)}, f32[2,256,256]{2,1,0:T(8,128)S(1)}, f32[2,256,256]{2,1,0:T(8,128)S(1)}) custom-call(s32[3]{0:T(128)S(1)} %pad_add_fusion.info, bf16[768,256]{1,0:T(8,128)(2,1)S(1)} %copy-done.1, bf16[768,256]{1,0:T(8,128)(2,1)S(1)} %copy-done.4, f32[8,128]{1,0:T(8,128)S(1)} %copy-done.8, ...), custom_call_target="tpu_custom_call" | custom-call | tf_op jit(solution)/shard_map/pallas_call | solution.py:774
  62.9 1.6 %shard_map.128.target = f32[512,256]{1,0:T(8,128)S(1)} custom-call(s32[3]{0:T(128)S(1)} %pad_add_fusion.info, f32[3,64,512]{2,1,0:T(8,128)S(1)} %collective-permute-done.6.refs_0_, f32[3,64,512]{2,1,0:T(8,128)S(1)} %collective-permute-done.7.refs_1_, f32[3,64,512]{2,1,0:T(8,128)S(1)} %collective-permute-done.8.refs_2_, ...), custom_call_target="tpu_custom_call" | custom-call | tf_op jit(solution)/shard_map/pallas_call | solution.py:774
  64.7 2.3 %shard_map.131 = (f32[2,256,256]{2,1,0:T(8,128)S(1)}, f32[2,256,256]{2,1,0:T(8,128)S(1)}) custom-call(s32[3]{0:T(128)S(1)} %pad_add_fusion.info, bf16[256,768]{1,0:T(8,128)(2,1)S(1)} %copy-done.6, bf16[256,768]{1,0:T(8,128)(2,1)S(1)} %copy-done.5, f32[4,2,128,128]{3,2,1,0:T(8,128)S(1)} %copy-done.3, f32[512,256]{1,0:T(8,128)S(1)} %shard_map.128.target, ...), custom_call_target="tpu_custom_call" | custom-call | tf_op jit(solution)/shard_map/pallas_call | solution.py:774
  67.3 1.7 %collective-permute-done.16.other = f32[2,256,256]{2,1,0:T(8,128)S(1)} collective-permute-done((f32[2,256,256]{2,1,0:T(8,128)S(1)}, f32[2,256,256]{2,1,0:T(8,128)S(1)}, u32[]{:S(2)}, u32[]{:S(2)}) %collective-permute-start.16) | collective-permute-done | bytes 524320 | tf_op jit(solution)/shard_map/ppermute | solution.py:638
  69.0 1.5 %shard_map.132 = (f32[2,64,512]{2,1,0:T(8,128)S(1)}, f32[2,64,512]{2,1,0:T(8,128)S(1)}, f32[2,64,512]{2,1,0:T(8,128)S(1)}, f32[2,64,512]{2,1,0:T(8,128)S(1)}, f32[2,256,512]{2,1,0:T(8,128)S(1)}) custom-call(s32[3]{0:T(128)S(1)} %pad_add_fusion.info, bf16[768,256]{1,0:T(8,128)(2,1)S(1)} %copy-done.4, f32[8,128]{1,0:T(8,128)S(1)} %copy-done.8, ...), custom_call_target="tpu_custom_call" | custom-call | tf_op jit(solution)/shard_map/pallas_call | solution.py:774
  70.5 1.2 %shard_map.133 = (f32[2,256,256]{2,1,0:T(8,128)S(1)}, f32[2,256,256]{2,1,0:T(8,128)S(1)}) custom-call(s32[3]{0:T(128)S(1)} %pad_add_fusion.info, bf16[768,256]{1,0:T(8,128)(2,1)S(1)} %copy-done.1, f32[8,128]{1,0:T(8,128)S(1)} %copy-done.8, f32[2,256,512]{2,1,0:T(8,128)S(1)} %get-tuple-element.91.leaving), custom_call_target="tpu_custom_call" | custom-call | tf_op jit(solution)/shard_map/pallas_call | solution.py:774
  75.8 2.3 %shard_map.134 = (f32[2,128,256]{2,1,0:T(8,128)S(1)}, f32[2,128,256]{2,1,0:T(8,128)S(1)}, f32[2,128,256]{2,1,0:T(8,128)S(1)}, f32[2,128,256]{2,1,0:T(8,128)S(1)}) custom-call(s32[3]{0:T(128)S(1)} %pad_add_fusion.info, bf16[256,768]{1,0:T(8,128)(2,1)S(1)} %copy-done.6, bf16[256,768]{1,0:T(8,128)(2,1)S(1)} %copy-done.5, f32[4,2,128,128]{3,2,1,0:T(8,128)S(1)} %copy-done.3, ...), custom_call_target="tpu_custom_call" | custom-call | tf_op jit(solution)/shard_map/pallas_call | solution.py:774
  78.3 1.3 %collective-permute-start.19 = (f32[2,128,256]{2,1,0:T(8,128)S(1)}, f32[2,128,256]{2,1,0:T(8,128)S(1)}, u32[]{:S(2)}, u32[]{:S(2)}) collective-permute-start(f32[2,128,256]{2,1,0:T(8,128)S(1)} %get-tuple-element.95), channel_id=1, source_target_pairs={{4,12},{5,13},{6,4},{7,5},{8,0},{9,1},{10,8},{11,9},{20,28},{21,29... | collective-permute-start | bytes 786440 | tf_op jit(solution)/shard_map/ppermute | solution.py:635
  79.6 1.3 %collective-permute-start.18 = (f32[2,128,256]{2,1,0:T(8,128)S(1)}, f32[2,128,256]{2,1,0:T(8,128)S(1)}, u32[]{:S(2)}, u32[]{:S(2)}) collective-permute-start(f32[2,128,256]{2,1,0:T(8,128)S(1)} %get-tuple-element.94), channel_id=1, source_target_pairs={{4,4},{5,5},{6,12},{7,13},{8,8},{9,9},{10,0},{11,1},{20,20},{21,21... | collective-permute-start | bytes 786440 | tf_op jit(solution)/shard_map/ppermute | solution.py:635
  81.0 1.3 %collective-permute-start.20 = (f32[2,128,256]{2,1,0:T(8,128)S(1)}, f32[2,128,256]{2,1,0:T(8,128)S(1)}, u32[]{:S(2)}, u32[]{:S(2)}) collective-permute-start(f32[2,128,256]{2,1,0:T(8,128)S(1)} %get-tuple-element.96), channel_id=1, source_target_pairs={{4,0},{5,1},{6,8},{7,9},{8,4},{9,5},{10,12},{11,13},{20,16},{21,17... | collective-permute-start | bytes 786440 | tf_op jit(solution)/shard_map/ppermute | solution.py:635
  82.3 1.3 %collective-permute-start.21 = (f32[2,128,256]{2,1,0:T(8,128)S(1)}, f32[2,128,256]{2,1,0:T(8,128)S(1)}, u32[]{:S(2)}, u32[]{:S(2)}) collective-permute-start(f32[2,128,256]{2,1,0:T(8,128)S(1)} %get-tuple-element.97), channel_id=1, source_target_pairs={{4,8},{5,9},{6,0},{7,1},{8,12},{9,13},{10,4},{11,5},{20,24},{21,25... | collective-permute-start | bytes 786440 | tf_op jit(solution)/shard_map/ppermute | solution.py:635
  83.9 15.0 %collective-permute-done.19.refs_1_ = f32[2,128,256]{2,1,0:T(8,128)S(1)} collective-permute-done((f32[2,128,256]{2,1,0:T(8,128)S(1)}, f32[2,128,256]{2,1,0:T(8,128)S(1)}, u32[]{:S(2)}, u32[]{:S(2)}) %collective-permute-start.19) | collective-permute-done | bytes 262176 | tf_op jit(solution)/shard_map/ppermute | solution.py:635
  98.9 5.0 %collective-permute-done.20.refs_2_ = f32[2,128,256]{2,1,0:T(8,128)S(1)} collective-permute-done((f32[2,128,256]{2,1,0:T(8,128)S(1)}, f32[2,128,256]{2,1,0:T(8,128)S(1)}, u32[]{:S(2)}, u32[]{:S(2)}) %collective-permute-start.20) | collective-permute-done | bytes 262176 | tf_op jit(solution)/shard_map/ppermute | solution.py:635
  106.9 4.4 %shard_map.135 = f32[1,2,128,2048]{3,2,1,0:T(8,128)} custom-call(s32[11]{0:T(128)S(1)} %pad_add_fusion.1.info, bf16[768,256]{1,0:T(8,128)(2,1)S(1)} %copy-done.4, f32[8,128]{1,0:T(8,128)S(1)} %copy-done.8, f32[2,128,256]{2,1,0:T(8,128)S(1)} %collective-permute-done.18.refs_0_, f32[2,128,256]{2,1,0:T(8,128)S(1)} %collective-permute-done.19.refs_1_, ...), custom_call_target="tpu_custom_call" | custom-call | tf_op jit(solution)/shard_map/pallas_call | solution.py:849
  (80 shorter events, 19.9 us)
Async XLA Ops:
  2.0 12.2 %collective-permute-start.3 = (f32[2,64,512]{2,1,0:T(8,128)S(1)}, f32[2,64,512]{2,1,0:T(8,128)S(1)}, u32[]{:S(2)}, u32[]{:S(2)}) collective-permute-start(f32[2,64,512]{2,1,0:T(8,128)S(1)} %slice_select_fusion), channel_id=1, source_target_pairs={{0,4},{4,8},{8,12},{12,0},{1,5},{5,9},{9,13},{13,1},{2,6},{6,10},{... | collective-permute-start | bytes 786440 | tf_op jit(solution)/shard_map/ppermute | solution.py:655
  7.9 8.3 %collective-permute-start.1 = (f32[1,64,512]{2,1,0:T(8,128)S(1)}, f32[1,64,512]{2,1,0:T(8,128)S(1)}, u32[]{:S(2)}, u32[]{:S(2)}) collective-permute-start(f32[1,64,512]{2,1,0:T(8,128)S(1)} %bitcast.11), channel_id=1, source_target_pairs={{0,4},{4,8},{8,12},{12,0},{1,5},{5,9},{9,13},{13,1},{2,6},{6,10},{... | collective-permute-start | bytes 393224 | tf_op jit(solution)/shard_map/ppermute | solution.py:689
  9.5 9.4 %collective-permute-start.5 = (f32[2,64,512]{2,1,0:T(8,128)S(1)}, f32[2,64,512]{2,1,0:T(8,128)S(1)}, u32[]{:S(2)}, u32[]{:S(2)}) collective-permute-start(f32[2,64,512]{2,1,0:T(8,128)S(1)} %get-tuple-element.71), channel_id=1, source_target_pairs={{0,1},{1,0},{2,3},{3,2},{4,5},{5,4},{6,7},{7,6},{8,9},{9,8},{10,11... | collective-permute-start | bytes 786440 | tf_op jit(solution)/shard_map/ppermute | solution.py:638
  14.2 7.1 %collective-permute-start.4 = (f32[2,64,512]{2,1,0:T(8,128)S(1)}, f32[2,64,512]{2,1,0:T(8,128)S(1)}, u32[]{:S(2)}, u32[]{:S(2)}) collective-permute-start(f32[2,64,512]{2,1,0:T(8,128)S(1)} %collective-permute-done.3.above), channel_id=1, source_target_pairs={{0,1},{1,0},{2,3},{3,2},{4,5},{5,4},{6,7},{7,6},{8,9},{9,8},{10,11... | collective-permute-start | bytes 786440 | tf_op jit(solution)/shard_map/ppermute | solution.py:638
  14.2 4.7 %collective-permute-start = (s32[4]{0:T(128)S(1)}, s32[4]{0:T(128)S(1)}, u32[]{:S(2)}, u32[]{:S(2)}) collective-permute-start(s32[4]{0:T(128)S(1)} %pad_add_fusion.2), channel_id=1, source_target_pairs={{0,1},{1,0},{2,3},{3,2},{4,5},{5,4},{6,7},{7,6},{8,9},{9,8},{10,11... | collective-permute-start | bytes 56 | tf_op jit(solution)/shard_map/ppermute | solution.py:638
  16.2 16.8 %collective-permute-start.2 = (f32[2,64,512]{2,1,0:T(8,128)S(1)}, f32[2,64,512]{2,1,0:T(8,128)S(1)}, u32[]{:S(2)}, u32[]{:S(2)}) collective-permute-start(f32[2,64,512]{2,1,0:T(8,128)S(1)} %pad_maximum_fusion), channel_id=1, source_target_pairs={{12,4},{13,5},{14,6},{15,7},{0,8},{1,9},{2,10},{3,11},{28,20},{29,... | collective-permute-start | bytes 786440 | tf_op jit(solution)/shard_map/ppermute | solution.py:635
  20.6 15.1 %collective-permute-start.7 = (f32[3,64,512]{2,1,0:T(8,128)S(1)}, f32[3,64,512]{2,1,0:T(8,128)S(1)}, u32[]{:S(2)}, u32[]{:S(2)}) collective-permute-start(f32[3,64,512]{2,1,0:T(8,128)S(1)} %shard_map.125), channel_id=1, source_target_pairs={{10,4},{11,5},{2,6},{3,7},{14,8},{15,9},{6,10},{7,11},{26,20},{27,... | collective-permute-start | bytes 1179656 | tf_op jit(solution)/shard_map/ppermute | solution.py:635
  22.7 13.7 %collective-permute-start.6 = (f32[3,64,512]{2,1,0:T(8,128)S(1)}, f32[3,64,512]{2,1,0:T(8,128)S(1)}, u32[]{:S(2)}, u32[]{:S(2)}) collective-permute-start(f32[3,64,512]{2,1,0:T(8,128)S(1)} %shard_map.124), channel_id=1, source_target_pairs={{6,4},{7,5},{14,6},{15,7},{10,8},{11,9},{2,10},{3,11},{22,20},{23,... | collective-permute-start | bytes 1179656 | tf_op jit(solution)/shard_map/ppermute | solution.py:635
  25.1 12.1 %collective-permute-start.10 = (f32[2,128,256]{2,1,0:T(8,128)S(1)}, f32[2,128,256]{2,1,0:T(8,128)S(1)}, u32[]{:S(2)}, u32[]{:S(2)}) collective-permute-start(f32[2,128,256]{2,1,0:T(8,128)S(1)} %get-tuple-element.62), channel_id=1, source_target_pairs={{4,4},{5,5},{12,6},{13,7},{8,8},{9,9},{0,10},{1,11},{20,20},{21,21... | collective-permute-start | bytes 786440 | tf_op jit(solution)/shard_map/ppermute | solution.py:635
  31.5 9.7 %collective-permute-start.11 = (f32[2,128,256]{2,1,0:T(8,128)S(1)}, f32[2,128,256]{2,1,0:T(8,128)S(1)}, u32[]{:S(2)}, u32[]{:S(2)}) collective-permute-start(f32[2,128,256]{2,1,0:T(8,128)S(1)} %get-tuple-element.64), channel_id=1, source_target_pairs={{8,4},{9,5},{0,6},{1,7},{12,8},{13,9},{4,10},{5,11},{24,20},{25,21... | collective-permute-start | bytes 786440 | tf_op jit(solution)/shard_map/ppermute | solution.py:635
  35.8 20.5 %collective-permute-start.9 = (f32[3,64,512]{2,1,0:T(8,128)S(1)}, f32[3,64,512]{2,1,0:T(8,128)S(1)}, u32[]{:S(2)}, u32[]{:S(2)}) collective-permute-start(f32[3,64,512]{2,1,0:T(8,128)S(1)} %shard_map.127), channel_id=1, source_target_pairs={{2,4},{3,5},{10,6},{11,7},{6,8},{7,9},{14,10},{15,11},{18,20},{19,... | collective-permute-start | bytes 1179656 | tf_op jit(solution)/shard_map/ppermute | solution.py:635
  36.5 19.8 %collective-permute-start.8 = (f32[3,64,512]{2,1,0:T(8,128)S(1)}, f32[3,64,512]{2,1,0:T(8,128)S(1)}, u32[]{:S(2)}, u32[]{:S(2)}) collective-permute-start(f32[3,64,512]{2,1,0:T(8,128)S(1)} %shard_map.126), channel_id=1, source_target_pairs={{14,4},{15,5},{6,6},{7,7},{2,8},{3,9},{10,10},{11,11},{30,20},{31,... | collective-permute-start | bytes 1179656 | tf_op jit(solution)/shard_map/ppermute | solution.py:635
  41.3 12.2 %collective-permute-start.13 = (f32[2,128,256]{2,1,0:T(8,128)S(1)}, f32[2,128,256]{2,1,0:T(8,128)S(1)}, u32[]{:S(2)}, u32[]{:S(2)}) collective-permute-start(f32[2,128,256]{2,1,0:T(8,128)S(1)} %get-tuple-element.79), channel_id=1, source_target_pairs={{0,4},{1,5},{8,6},{9,7},{4,8},{5,9},{12,10},{13,11},{16,20},{17,21... | collective-permute-start | bytes 786440 | tf_op jit(solution)/shard_map/ppermute | solution.py:635
  46.2 10.0 %collective-permute-start.12 = (f32[2,128,256]{2,1,0:T(8,128)S(1)}, f32[2,128,256]{2,1,0:T(8,128)S(1)}, u32[]{:S(2)}, u32[]{:S(2)}) collective-permute-start(f32[2,128,256]{2,1,0:T(8,128)S(1)} %get-tuple-element.78), channel_id=1, source_target_pairs={{12,4},{13,5},{4,6},{5,7},{0,8},{1,9},{8,10},{9,11},{28,20},{29,21... | collective-permute-start | bytes 786440 | tf_op jit(solution)/shard_map/ppermute | solution.py:635
  58.6 2.0 %collective-permute-start.14 = (f32[2,256,256]{2,1,0:T(8,128)S(1)}, f32[2,256,256]{2,1,0:T(8,128)S(1)}, u32[]{:S(2)}, u32[]{:S(2)}) collective-permute-start(f32[2,256,256]{2,1,0:T(8,128)S(1)} %get-tuple-element.85), channel_id=1, source_target_pairs={{0,1},{1,0},{2,3},{3,2},{4,5},{5,4},{6,7},{7,6},{8,9},{9,8},{10,11... | collective-permute-start | bytes 1572872 | tf_op jit(solution)/shard_map/ppermute | solution.py:638
  62.7 2.0 %collective-permute-start.15 = (f32[2,256,256]{2,1,0:T(8,128)S(1)}, f32[2,256,256]{2,1,0:T(8,128)S(1)}, u32[]{:S(2)}, u32[]{:S(2)}) collective-permute-start(f32[2,256,256]{2,1,0:T(8,128)S(1)} %get-tuple-element.87), channel_id=1, source_target_pairs={{0,1},{1,0},{2,3},{3,2},{4,5},{5,4},{6,7},{7,6},{8,9},{9,8},{10,11... | collective-permute-start | bytes 1572872 | tf_op jit(solution)/shard_map/ppermute | solution.py:638
  67.0 2.0 %collective-permute-start.16 = (f32[2,256,256]{2,1,0:T(8,128)S(1)}, f32[2,256,256]{2,1,0:T(8,128)S(1)}, u32[]{:S(2)}, u32[]{:S(2)}) collective-permute-start(f32[2,256,256]{2,1,0:T(8,128)S(1)} %get-tuple-element.89), channel_id=1, source_target_pairs={{0,1},{1,0},{2,3},{3,2},{4,5},{5,4},{6,7},{7,6},{8,9},{9,8},{10,11... | collective-permute-start | bytes 1572872 | tf_op jit(solution)/shard_map/ppermute | solution.py:638
  71.7 2.0 %collective-permute-start.17 = (f32[2,256,256]{2,1,0:T(8,128)S(1)}, f32[2,256,256]{2,1,0:T(8,128)S(1)}, u32[]{:S(2)}, u32[]{:S(2)}) collective-permute-start(f32[2,256,256]{2,1,0:T(8,128)S(1)} %get-tuple-element.93), channel_id=1, source_target_pairs={{0,1},{1,0},{2,3},{3,2},{4,5},{5,4},{6,7},{7,6},{8,9},{9,8},{10,11... | collective-permute-start | bytes 1572872 | tf_op jit(solution)/shard_map/ppermute | solution.py:638
  72.0 6.0 %collective-permute-start.26 = (f32[2,64,512]{2,1,0:T(8,128)S(1)}, f32[2,64,512]{2,1,0:T(8,128)S(1)}, u32[]{:S(2)}, u32[]{:S(2)}) collective-permute-start(f32[2,64,512]{2,1,0:T(8,128)S(1)} %get-tuple-element.98), channel_id=1, source_target_pairs={{4,6},{5,7},{6,14},{7,15},{8,10},{9,11},{10,2},{11,3},{20,22},{21,... | collective-permute-start | bytes 786440 | tf_op jit(solution)/shard_map/ppermute | solution.py:635
  73.7 5.9 %collective-permute-start.27 = (f32[2,64,512]{2,1,0:T(8,128)S(1)}, f32[2,64,512]{2,1,0:T(8,128)S(1)}, u32[]{:S(2)}, u32[]{:S(2)}) collective-permute-start(f32[2,64,512]{2,1,0:T(8,128)S(1)} %get-tuple-element.100), channel_id=1, source_target_pairs={{4,14},{5,15},{6,6},{7,7},{8,2},{9,3},{10,10},{11,11},{20,30},{21,... | collective-permute-start | bytes 786440 | tf_op jit(solution)/shard_map/ppermute | solution.py:635
  74.4 6.6 %collective-permute-start.28 = (f32[2,64,512]{2,1,0:T(8,128)S(1)}, f32[2,64,512]{2,1,0:T(8,128)S(1)}, u32[]{:S(2)}, u32[]{:S(2)}) collective-permute-start(f32[2,64,512]{2,1,0:T(8,128)S(1)} %get-tuple-element.102), channel_id=1, source_target_pairs={{4,2},{5,3},{6,10},{7,11},{8,6},{9,7},{10,14},{11,15},{20,18},{21,... | collective-permute-start | bytes 786440 | tf_op jit(solution)/shard_map/ppermute | solution.py:635
  75.1 7.2 %collective-permute-start.29 = (f32[2,64,512]{2,1,0:T(8,128)S(1)}, f32[2,64,512]{2,1,0:T(8,128)S(1)}, u32[]{:S(2)}, u32[]{:S(2)}) collective-permute-start(f32[2,64,512]{2,1,0:T(8,128)S(1)} %get-tuple-element.104), channel_id=1, source_target_pairs={{4,10},{5,11},{6,2},{7,3},{8,14},{9,15},{10,6},{11,7},{20,26},{21,... | collective-permute-start | bytes 786440 | tf_op jit(solution)/shard_map/ppermute | solution.py:635
  78.1 5.5 %collective-permute-start.30 = (f32[2,64,512]{2,1,0:T(8,128)S(1)}, f32[2,64,512]{2,1,0:T(8,128)S(1)}, u32[]{:S(2)}, u32[]{:S(2)}) collective-permute-start(f32[2,64,512]{2,1,0:T(8,128)S(1)} %collective-permute-done.26.refs_8_), channel_id=1, source_target_pairs={{0,1},{1,0},{2,3},{3,2},{4,5},{5,4},{6,7},{7,6},{8,9},{9,8},{10,11... | collective-permute-start | bytes 786440 | tf_op jit(solution)/shard_map/ppermute | solution.py:638
  78.3 20.6 %collective-permute-start.19 = (f32[2,128,256]{2,1,0:T(8,128)S(1)}, f32[2,128,256]{2,1,0:T(8,128)S(1)}, u32[]{:S(2)}, u32[]{:S(2)}) collective-permute-start(f32[2,128,256]{2,1,0:T(8,128)S(1)} %get-tuple-element.95), channel_id=1, source_target_pairs={{4,12},{5,13},{6,4},{7,5},{8,0},{9,1},{10,8},{11,9},{20,28},{21,29... | collective-permute-start | bytes 786440 | tf_op jit(solution)/shard_map/ppermute | solution.py:635
  79.6 24.8 %collective-permute-start.18 = (f32[2,128,256]{2,1,0:T(8,128)S(1)}, f32[2,128,256]{2,1,0:T(8,128)S(1)}, u32[]{:S(2)}, u32[]{:S(2)}) collective-permute-start(f32[2,128,256]{2,1,0:T(8,128)S(1)} %get-tuple-element.94), channel_id=1, source_target_pairs={{4,4},{5,5},{6,12},{7,13},{8,8},{9,9},{10,0},{11,1},{20,20},{21,21... | collective-permute-start | bytes 786440 | tf_op jit(solution)/shard_map/ppermute | solution.py:635
  81.0 22.9 %collective-permute-start.20 = (f32[2,128,256]{2,1,0:T(8,128)S(1)}, f32[2,128,256]{2,1,0:T(8,128)S(1)}, u32[]{:S(2)}, u32[]{:S(2)}) collective-permute-start(f32[2,128,256]{2,1,0:T(8,128)S(1)} %get-tuple-element.96), channel_id=1, source_target_pairs={{4,0},{5,1},{6,8},{7,9},{8,4},{9,5},{10,12},{11,13},{20,16},{21,17... | collective-permute-start | bytes 786440 | tf_op jit(solution)/shard_map/ppermute | solution.py:635
  82.3 21.7 %collective-permute-start.21 = (f32[2,128,256]{2,1,0:T(8,128)S(1)}, f32[2,128,256]{2,1,0:T(8,128)S(1)}, u32[]{:S(2)}, u32[]{:S(2)}) collective-permute-start(f32[2,128,256]{2,1,0:T(8,128)S(1)} %get-tuple-element.97), channel_id=1, source_target_pairs={{4,8},{5,9},{6,0},{7,1},{8,12},{9,13},{10,4},{11,5},{20,24},{21,25... | collective-permute-start | bytes 786440 | tf_op jit(solution)/shard_map/ppermute | solution.py:635
  83.6 20.9 %collective-permute-start.31 = (f32[2,64,512]{2,1,0:T(8,128)S(1)}, f32[2,64,512]{2,1,0:T(8,128)S(1)}, u32[]{:S(2)}, u32[]{:S(2)}) collective-permute-start(f32[2,64,512]{2,1,0:T(8,128)S(1)} %collective-permute-done.27.refs_9_), channel_id=1, source_target_pairs={{0,1},{1,0},{2,3},{3,2},{4,5},{5,4},{6,7},{7,6},{8,9},{9,8},{10,11... | collective-permute-start | bytes 786440 | tf_op jit(solution)/shard_map/ppermute | solution.py:638
  98.9 6.0 %collective-permute-start.32 = (f32[2,64,512]{2,1,0:T(8,128)S(1)}, f32[2,64,512]{2,1,0:T(8,128)S(1)}, u32[]{:S(2)}, u32[]{:S(2)}) collective-permute-start(f32[2,64,512]{2,1,0:T(8,128)S(1)} %collective-permute-done.28.refs_10_), channel_id=1, source_target_pairs={{0,1},{1,0},{2,3},{3,2},{4,5},{5,4},{6,7},{7,6},{8,9},{9,8},{10,11... | collective-permute-start | bytes 786440 | tf_op jit(solution)/shard_map/ppermute | solution.py:638
  103.9 1.9 %collective-permute-start.23 = (f32[2,128,256]{2,1,0:T(8,128)S(1)}, f32[2,128,256]{2,1,0:T(8,128)S(1)}, u32[]{:S(2)}, u32[]{:S(2)}) collective-permute-start(f32[2,128,256]{2,1,0:T(8,128)S(1)} %collective-permute-done.19.refs_1_), channel_id=1, source_target_pairs={{0,1},{1,0},{2,3},{3,2},{4,5},{5,4},{6,7},{7,6},{8,9},{9,8},{10,11... | collective-permute-start | bytes 786440 | tf_op jit(solution)/shard_map/ppermute | solution.py:638
  104.5 2.1 %collective-permute-start.25 = (f32[2,128,256]{2,1,0:T(8,128)S(1)}, f32[2,128,256]{2,1,0:T(8,128)S(1)}, u32[]{:S(2)}, u32[]{:S(2)}) collective-permute-start(f32[2,128,256]{2,1,0:T(8,128)S(1)} %collective-permute-done.21.refs_3_), channel_id=1, source_target_pairs={{0,1},{1,0},{2,3},{3,2},{4,5},{5,4},{6,7},{7,6},{8,9},{9,8},{10,11... | collective-permute-start | bytes 786440 | tf_op jit(solution)/shard_map/ppermute | solution.py:638
  104.9 2.0 %collective-permute-start.22 = (f32[2,128,256]{2,1,0:T(8,128)S(1)}, f32[2,128,256]{2,1,0:T(8,128)S(1)}, u32[]{:S(2)}, u32[]{:S(2)}) collective-permute-start(f32[2,128,256]{2,1,0:T(8,128)S(1)} %collective-permute-done.18.refs_0_), channel_id=1, source_target_pairs={{0,1},{1,0},{2,3},{3,2},{4,5},{5,4},{6,7},{7,6},{8,9},{9,8},{10,11... | collective-permute-start | bytes 786440 | tf_op jit(solution)/shard_map/ppermute | solution.py:638
  (12 other events, 101.7 us)
